TPU v7x, 256 devices: a whole 4x4x8 slice. The times are simulated.
256 devices in a mesh: space: 8 (over x, core), work: 32 (over y, z).
Axes of the slice: x: 4, y: 4, z: 8, core: 2. Of those that a mesh axis runs over, the one named last changes fastest.
Arguments:
- adjoint: float32 [3, 19, 16, 32, 128], P(None, None, 'space', 'work'), may hold values from -6 to 6
- velocity: bfloat16 [3, 16, 32, 128], P(None, 'space', 'work'), may hold values from -0.29882812 to 0.29882812
- relaxation: float32 [3], replicated, may hold values from 0.6 to 1.8
- uptake: float32 [3], replicated, may hold values from 0.5 to 2
- fluid_mask: int32 [16, 32, 128], P('space', 'work'), may hold values 0 or 1
- block_cells: int32 [8, 32, 32, 4, 128], P('space', 'work'), may hold values from 0 to 255
- owner_load: int32 [8, 32, 32], P('space', 'work'), may hold values from 0 to 4, as said below
- response: bfloat16 [8, 32, 32, 4, 128, 128], P('space', 'work'), may hold values from -1 to 1
Outputs:
- rewound: float32 [3, 19, 16, 32, 128], P(None, None, 'space', 'work')
Inputs may be any that keep to these rules, and one draw needn't show every extreme that they name: `owner_load`: in every space group one owner receives 4 live slots from every brick.
All inputs are finite; a program needn't handle non-finite values. No bound on the sum of `fluid_mask` on one device may be relied on, other than what follows from the above.
Results may differ from a plain program's by a relative error of at most 0.0038.
Values may be sent and summed in bfloat16 or wider, within the bound.
No kernel may reach another device: no remote copies, remote signals or barrier semaphores. Data moves between devices by JAX's collectives and lax.ppermute only.
A program may use at most 64 MiB of HBM per device.

v0:
```python
import jax
import jax.numpy as jnp
from jax import lax
from jax.sharding import PartitionSpec as P

STEPS = 2


DIRECTIONS = (
    (0, 0, 0),
    (1, 0, 0),
    (-1, 0, 0),
    (0, 1, 0),
    (0, -1, 0),
    (0, 0, 1),
    (0, 0, -1),
    (1, 1, 0),
    (-1, -1, 0),
    (1, -1, 0),
    (-1, 1, 0),
    (1, 0, 1),
    (-1, 0, -1),
    (1, 0, -1),
    (-1, 0, 1),
    (0, 1, 1),
    (0, -1, -1),
    (0, 1, -1),
    (0, -1, 1),
)
WEIGHTS = (1.0 / 3.0,) + (1.0 / 18.0,) * 6 + (1.0 / 36.0,) * 12


def extended(shard, sides, width):
    for axis, dim in sides:
        count, length = (lax.axis_size(axis), shard.shape[dim])
        up = [(i, (i + 1) % count) for i in range(count - 1)]
        down = [(j, i) for i, j in up]
        last = lax.slice_in_dim(shard, length - width, length, axis=dim)
        first = lax.slice_in_dim(shard, 0, width, axis=dim)
        before = lax.ppermute(last, axis, up)
        after = lax.ppermute(first, axis, down)
        shard = jnp.concatenate([before, shard, after], axis=dim)
    return shard


def select_moves(padded, width_x, width_y):
    pieces = []
    for number, offset in enumerate(DIRECTIONS):
        sliced = padded[
            :,
            number,
            1 + offset[0] : 1 + offset[0] + width_x,
            1 + offset[1] : 1 + offset[1] + width_y,
            :,
        ]
        pieces.append(jnp.roll(sliced, -offset[2], axis=-1))
    return jnp.stack(pieces, axis=1)


def pull_whole(field):
    padded = extended(field, (("space", 2), ("work", 3)), 1)
    return select_moves(padded, field.shape[2], field.shape[3])


def collide(pulled, velocity, relaxation, fluid_mask):
    speeds = velocity.astype(jnp.float32)
    density = jnp.zeros(pulled.shape[:1] + pulled.shape[2:], jnp.float32)
    for number, offset in enumerate(DIRECTIONS):
        factor = 1.0 + 3.0 * (offset[0] * speeds[0] + offset[1] * speeds[1] + offset[2] * speeds[2])
        density = density + WEIGHTS[number] * factor * pulled[:, number]
    rate_column = relaxation[:, None, None, None, None]
    keeper = fluid_mask.astype(jnp.float32)
    collided = ((1.0 - rate_column) * pulled + rate_column * density[:, None]) * keeper
    return (collided, density)


def one_hot_table(places, cell_count):
    cell_numbers = lax.broadcasted_iota(jnp.int32, (places.shape[0], cell_count), 1)
    return (places[:, None] == cell_numbers).astype(jnp.float32)


def couple(collided, density, block_cells, owner_load, response, uptake):
    voxel_cells = block_cells[0, 0]
    owner_count, capacity, length = voxel_cells.shape
    species = density.shape[0]
    group_size = min(4, owner_count)
    while owner_count % group_size != 0:
        group_size = group_size - 1
    group_count = owner_count // group_size
    grouped_cells = voxel_cells.reshape(group_count, group_size * capacity * length)
    flat_density = density.reshape(species, -1)
    cell_count = flat_density.shape[1]

    def pick_group(places):
        table = one_hot_table(places, cell_count)
        return jnp.dot(
            flat_density,
            table.T,
            precision=lax.Precision.HIGHEST,
            preferred_element_type=jnp.float32,
        )

    picked = lax.map(pick_group, grouped_cells)
    picked = jnp.transpose(picked, (1, 0, 2)).reshape(species, owner_count, capacity, length)
    slot_numbers = jnp.arange(capacity, dtype=jnp.int32)
    occupied = (slot_numbers[None, :] < owner_load[0, 0][:, None]).astype(jnp.float32)
    outgoing = (picked * occupied[None, :, :, None]).astype(jnp.bfloat16)
    incoming = lax.all_to_all(outgoing, "work", split_axis=1, concat_axis=1, tiled=True)
    answer = jnp.einsum(
        "bkij,sbkj->sbki", response[0, 0], incoming, preferred_element_type=jnp.float32
    )
    answer = answer * uptake[:, None, None, None]
    returned = lax.all_to_all(answer, "work", split_axis=1, concat_axis=1, tiled=True)
    grouped_values = jnp.transpose(returned.reshape(species, group_count, -1), (1, 0, 2))

    def spread_group(total, pair):
        places, values = pair
        table = one_hot_table(places, cell_count)
        added = jnp.dot(
            values, table, precision=lax.Precision.HIGHEST, preferred_element_type=jnp.float32
        )
        return (total + added, None)

    source, unused = lax.scan(
        spread_group, jnp.zeros((species, cell_count), jnp.float32), (grouped_cells, grouped_values)
    )
    weights = jnp.array(WEIGHTS, jnp.float32)
    return collided + weights[None, :, None, None, None] * source.reshape(density.shape)[:, None]


def body(adjoint, velocity, relaxation, uptake, fluid_mask, block_cells, owner_load, response):
    field = adjoint
    for step_number in range(STEPS):
        pulled = pull_whole(field)
        collided, density = collide(pulled, velocity, relaxation, fluid_mask)
        field = couple(collided, density, block_cells, owner_load, response, uptake)
    return field


def solution(mesh):
    placed = (
        P(None, None, "space", "work", None),
        P(None, "space", "work", None),
        P(),
        P(),
        P("space", "work", None),
        P("space", "work", None, None, None),
        P("space", "work", None),
        P("space", "work", None, None, None, None),
    )
    return jax.shard_map(
        body,
        mesh=mesh,
        in_specs=placed,
        out_specs=P(None, None, "space", "work", None),
        check_vma=False,
    )
```

profile of v0, /device:TPU:32, one launch (start us, length us, event | category | flops | bytes accessed | tf_op | source)
XLA Modules:
  0.0 155.4 jit_solution(11895795556785591456)
XLA Ops:
  0.0 0.8 fusion.146
  0.8 1.3 collective-permute-start
  2.1 3.0 %collective-permute-start.1 = (f32[3,19,1,1,128]{4,2,0,3,1:T(1,128)S(1)}, f32[3,19,1,1,128]{4,2,0,3,1:T(1,128)S(1)}, u32[]{:S(2)}, u32[]{:S(2)}) collective-permute-start(f32[3,19,1,1,128]{4,2,0,3,1:T(1,128)S(1)} %copy.132), channel_id=1, source_target_pairs={{0,32},{32,64},{64,96},{96,128},{128,160},{160,192},{192,224},{1,3... | collective-permute-start | bytes 87560 | tf_op jit(solution)/shard_map/ppermute | solution.py:40
  5.9 0.7 fusion.28
  7.3 0.8 copy.129
  8.9 0.9 reshape_squeeze.4
  9.8 3.8 %collective-permute-start.3 = (f32[3,19,4,1,128]{4,2,0,3,1:T(4,128)S(1)}, f32[3,19,4,1,128]{4,2,0,3,1:T(4,128)S(1)}, u32[]{:S(2)}, u32[]{:S(2)}) collective-permute-start(f32[3,19,4,1,128]{4,2,0,3,1:T(4,128)S(1)} %pad_maximum_fusion), channel_id=1, source_target_pairs={{0,1},{1,2},{2,3},{3,4},{4,5},{5,6},{6,7},{7,8},{8,9},{9,10},{10,1... | collective-permute-start | bytes 350216 | tf_op jit(solution)/shard_map/ppermute | solution.py:40
  13.7 2.0 %collective-permute-start.2 = (f32[3,19,4,1,128]{4,2,0,3,1:T(4,128)S(1)}, f32[3,19,4,1,128]{4,2,0,3,1:T(4,128)S(1)}, u32[]{:S(2)}, u32[]{:S(2)}) collective-permute-start(f32[3,19,4,1,128]{4,2,0,3,1:T(4,128)S(1)} %pad_maximum_fusion), channel_id=1, source_target_pairs={{1,0},{2,1},{3,2},{4,3},{5,4},{6,5},{7,6},{8,7},{9,8},{10,9},{11,1... | collective-permute-start | bytes 350216 | tf_op jit(solution)/shard_map/ppermute | solution.py:41
  18.2 3.4 %collective-permute-done.2 = f32[3,19,4,1,128]{4,2,0,3,1:T(4,128)S(1)} collective-permute-done((f32[3,19,4,1,128]{4,2,0,3,1:T(4,128)S(1)}, f32[3,19,4,1,128]{4,2,0,3,1:T(4,128)S(1)}, u32[]{:S(2)}, u32[]{:S(2)}) %collective-permute-start.2) | collective-permute-done | bytes 116768 | tf_op jit(solution)/shard_map/ppermute | solution.py:41
  22.4 0.8 multiply_bitcast_fusion.1
  24.1 8.8 %while.42 = (s32[]{:T(128)}, f32[8,3,2048]{2,1,0:T(4,128)S(1)}, s32[8,2048]{1,0:T(8,128)S(1)}, f32[3,256]{1,0:T(4,128)S(1)}, s32[]{:T(128)}) while((s32[]{:T(128)}, f32[8,3,2048]{2,1,0:T(4,128)S(1)}, s32[8,2048]{1,0:T(8,128)S(1)}, f32[3,256]{1,0:T(4,128)S(1)}, s32[]{:T(128)}) %tuple.190), condition=%wide.region_1.2_spmd, body=%wide.region_0.1_spmd.sunk | while | flops 19398656 | bytes 61517 | solution.py:103
  24.1 1.1 fusion.178
  25.2 1.1 fusion.178
  26.3 1.1 fusion.178
  27.4 1.1 fusion.178
  28.5 1.1 fusion.178
  29.6 1.1 fusion.178
  30.7 1.1 fusion.178
  31.8 1.1 fusion.178
  33.9 11.1 %all-to-all-start = ((bf16[3,32,4,128]{3,2,0,1:T(4,128)(2,1)}), bf16[3,32,4,128]{3,2,0,1:T(4,128)(2,1)S(1)}, u32[]{:S(2)}, u32[]{:S(2)}) async-start(bf16[3,32,4,128]{3,2,0,1:T(4,128)(2,1)} %copy.158), calls=%async_computation | async-start | bytes 196608 | tf_op jit(solution)/shard_map/all_to_all | solution.py:108
  45.2 9.3 %all-to-all-done = bf16[3,32,4,128]{3,2,0,1:T(4,128)(2,1)S(1)} async-done(((bf16[3,32,4,128]{3,2,0,1:T(4,128)(2,1)}), bf16[3,32,4,128]{3,2,0,1:T(4,128)(2,1)S(1)}, u32[]{:S(2)}, u32[]{:S(2)}) %all-to-all-start) | async-done | bytes 98336 | tf_op jit(solution)/shard_map/all_to_all | solution.py:108
  54.5 4.4 %fusion.17 = f32[3,32,4,128]{3,0,2,1:T(4,128)S(1)} fusion(bf16[1,1,32,4,128,128]{5,4,3,2,1,0:T(8,128)(2,1)} %param.25, bf16[3,32,4,128]{3,2,0,1:T(4,128)(2,1)S(1)} %all-to-all-done, f32[3]{0:T(128)S(1)} %copy-done.1), kind=kOutput, calls=%fused_computation.29 | convolution fusion | flops 12632064 | bytes 4489228 | tf_op jit(solution)/shard_map/bkij,sbkj->sbki/dot_general | solution.py:109
  58.9 0.8 copy.160
  59.7 4.5 %all-to-all-start.1 = ((f32[3,32,4,128]{3,2,0,1:T(4,128)}), f32[3,32,4,128]{3,2,0,1:T(4,128)S(1)}, u32[]{:S(2)}, u32[]{:S(2)}) async-start(f32[3,32,4,128]{3,2,0,1:T(4,128)} %copy.160), calls=%async_computation.1 | async-start | bytes 393216 | tf_op jit(solution)/shard_map/all_to_all | solution.py:113
  64.5 10.1 %all-to-all-done.1 = f32[3,32,4,128]{3,2,0,1:T(4,128)S(1)} async-done(((f32[3,32,4,128]{3,2,0,1:T(4,128)}), f32[3,32,4,128]{3,2,0,1:T(4,128)S(1)}, u32[]{:S(2)}, u32[]{:S(2)}) %all-to-all-start.1) | async-done | bytes 196640 | tf_op jit(solution)/shard_map/all_to_all | solution.py:113
  74.8 6.9 %while.44 = (s32[]{:T(128)}, f32[3,256]{1,0:T(4,128)S(1)}, f32[8,3,2048]{2,0,1:T(8,128)S(1)}, s32[8,2048]{1,0:T(8,128)S(1)}, s32[]{:T(128)}, /*index=5*/s32[]{:T(128)}) while((s32[]{:T(128)}, f32[3,256]{1,0:T(4,128)S(1)}, f32[8,3,2048]{2,0,1:T(8,128)S(1)}, s32[8,2048]{1,0:T(8,128)S(1)}, s32[]{:T(128)}, /*index=5*/s32[]{:T(128)}) %tuple.206), condition=%wide.region_3.4_spmd.clone, body=%wide.region_2.3_spmd.clone.sunk | while | flops 19400196 | bytes 104543 | solution.py:124
  74.8 0.8 fusion.181
  75.7 0.8 fusion.181
  76.5 0.8 fusion.181
  77.4 0.8 fusion.181
  78.3 0.8 fusion.181
  79.1 0.8 fusion.181
  80.0 0.8 fusion.181
  80.8 0.8 fusion.181
  82.0 1.3 collective-permute-start.4
  83.3 3.0 %collective-permute-start.5 = (f32[3,19,1,1,128]{4,2,0,3,1:T(1,128)S(1)}, f32[3,19,1,1,128]{4,2,0,3,1:T(1,128)S(1)}, u32[]{:S(2)}, u32[]{:S(2)}) collective-permute-start(f32[3,19,1,1,128]{4,2,0,3,1:T(1,128)S(1)} %get-tuple-element.218), channel_id=1, source_target_pairs={{0,32},{32,64},{64,96},{96,128},{128,160},{160,192},{192,224},{1,3... | collective-permute-start | bytes 87560 | tf_op jit(solution)/shard_map/ppermute | solution.py:40
  87.2 2.7 %collective-permute-start.7 = (f32[3,19,4,1,128]{4,2,0,3,1:T(4,128)S(1)}, f32[3,19,4,1,128]{4,2,0,3,1:T(4,128)S(1)}, u32[]{:S(2)}, u32[]{:S(2)}) collective-permute-start(f32[3,19,4,1,128]{4,2,0,3,1:T(4,128)S(1)} %pad_maximum_fusion.1), channel_id=1, source_target_pairs={{0,1},{1,2},{2,3},{3,4},{4,5},{5,6},{6,7},{7,8},{8,9},{9,10},{10,1... | collective-permute-start | bytes 350216 | tf_op jit(solution)/shard_map/ppermute | solution.py:40
  90.0 3.1 %collective-permute-start.6 = (f32[3,19,4,1,128]{4,2,0,3,1:T(4,128)S(1)}, f32[3,19,4,1,128]{4,2,0,3,1:T(4,128)S(1)}, u32[]{:S(2)}, u32[]{:S(2)}) collective-permute-start(f32[3,19,4,1,128]{4,2,0,3,1:T(4,128)S(1)} %pad_maximum_fusion.1), channel_id=1, source_target_pairs={{1,0},{2,1},{3,2},{4,3},{5,4},{6,5},{7,6},{8,7},{9,8},{10,9},{11,1... | collective-permute-start | bytes 350216 | tf_op jit(solution)/shard_map/ppermute | solution.py:41
  94.9 3.1 %collective-permute-done.6 = f32[3,19,4,1,128]{4,2,0,3,1:T(4,128)S(1)} collective-permute-done((f32[3,19,4,1,128]{4,2,0,3,1:T(4,128)S(1)}, f32[3,19,4,1,128]{4,2,0,3,1:T(4,128)S(1)}, u32[]{:S(2)}, u32[]{:S(2)}) %collective-permute-start.6) | collective-permute-done | bytes 116768 | tf_op jit(solution)/shard_map/ppermute | solution.py:41
  100.2 8.8 %while.43 = (s32[]{:T(128)}, f32[8,3,2048]{2,1,0:T(4,128)S(1)}, s32[8,2048]{1,0:T(8,128)S(1)}, f32[3,256]{1,0:T(4,128)S(1)}, s32[]{:T(128)}) while((s32[]{:T(128)}, f32[8,3,2048]{2,1,0:T(4,128)S(1)}, s32[8,2048]{1,0:T(8,128)S(1)}, f32[3,256]{1,0:T(4,128)S(1)}, s32[]{:T(128)}) %tuple.203), condition=%wide.region_5.6_spmd, body=%wide.region_4.5_spmd.sunk | while | flops 19398656 | bytes 61517 | solution.py:103
  100.2 1.1 fusion.180
  101.3 1.1 fusion.180
  102.4 1.1 fusion.180
  103.5 1.1 fusion.180
  104.6 1.1 fusion.180
  105.7 1.1 fusion.180
  106.8 1.1 fusion.180
  107.9 1.1 fusion.180
  110.0 8.0 %all-to-all-start.2 = ((bf16[3,32,4,128]{3,2,0,1:T(4,128)(2,1)}), bf16[3,32,4,128]{3,2,0,1:T(4,128)(2,1)S(1)}, u32[]{:S(2)}, u32[]{:S(2)}) async-start(bf16[3,32,4,128]{3,2,0,1:T(4,128)(2,1)} %copy.192), calls=%async_computation.2 | async-start | bytes 196608 | tf_op jit(solution)/shard_map/all_to_all | solution.py:108
  118.2 9.3 %all-to-all-done.2 = bf16[3,32,4,128]{3,2,0,1:T(4,128)(2,1)S(1)} async-done(((bf16[3,32,4,128]{3,2,0,1:T(4,128)(2,1)}), bf16[3,32,4,128]{3,2,0,1:T(4,128)(2,1)S(1)}, u32[]{:S(2)}, u32[]{:S(2)}) %all-to-all-start.2) | async-done | bytes 98336 | tf_op jit(solution)/shard_map/all_to_all | solution.py:108
  127.5 4.4 %fusion.23 = f32[3,32,4,128]{3,0,2,1:T(4,128)S(1)} fusion(bf16[1,1,32,4,128,128]{5,4,3,2,1,0:T(8,128)(2,1)} %param.25, bf16[3,32,4,128]{3,2,0,1:T(4,128)(2,1)S(1)} %all-to-all-done.2, f32[3]{0:T(128)S(1)} %copy-done.1), kind=kOutput, calls=%fused_computation.31 | convolution fusion | flops 12632064 | bytes 4489228 | tf_op jit(solution)/shard_map/bkij,sbkj->sbki/dot_general | solution.py:109
  132.0 0.8 copy.194
  132.7 4.4 %all-to-all-start.3 = ((f32[3,32,4,128]{3,2,0,1:T(4,128)}), f32[3,32,4,128]{3,2,0,1:T(4,128)S(1)}, u32[]{:S(2)}, u32[]{:S(2)}) async-start(f32[3,32,4,128]{3,2,0,1:T(4,128)} %copy.194), calls=%async_computation.3 | async-start | bytes 393216 | tf_op jit(solution)/shard_map/all_to_all | solution.py:113
  137.4 10.1 %all-to-all-done.3 = f32[3,32,4,128]{3,2,0,1:T(4,128)S(1)} async-done(((f32[3,32,4,128]{3,2,0,1:T(4,128)}), f32[3,32,4,128]{3,2,0,1:T(4,128)S(1)}, u32[]{:S(2)}, u32[]{:S(2)}) %all-to-all-start.3) | async-done | bytes 196640 | tf_op jit(solution)/shard_map/all_to_all | solution.py:113
  147.7 6.9 %while.45 = (s32[]{:T(128)}, f32[3,256]{1,0:T(4,128)S(1)}, f32[8,3,2048]{2,0,1:T(8,128)S(1)}, s32[8,2048]{1,0:T(8,128)S(1)}, s32[]{:T(128)}, /*index=5*/s32[]{:T(128)}) while((s32[]{:T(128)}, f32[3,256]{1,0:T(4,128)S(1)}, f32[8,3,2048]{2,0,1:T(8,128)S(1)}, s32[8,2048]{1,0:T(8,128)S(1)}, s32[]{:T(128)}, /*index=5*/s32[]{:T(128)}) %tuple.205), condition=%wide.region_7.8_spmd.clone, body=%wide.region_6.7_spmd.clone.sunk | while | flops 19400196 | bytes 104543 | solution.py:124
  147.8 0.8 fusion.182
  148.6 0.8 fusion.182
  149.5 0.8 fusion.182
  150.3 0.8 fusion.182
  151.2 0.8 fusion.182
  152.1 0.8 fusion.182
  152.9 0.8 fusion.182
  153.8 0.8 fusion.182
  154.6 0.8 copy_add_fusion
  (226 shorter events, 15.7 us)
Async XLA Ops:
  0.8 8.9 %collective-permute-start = (f32[3,19,1,1,128]{4,2,0,3,1:T(1,128)S(1)}, f32[3,19,1,1,128]{4,2,0,3,1:T(1,128)S(1)}, u32[]{:S(2)}, u32[]{:S(2)}) collective-permute-start(f32[3,19,1,1,128]{4,2,0,3,1:T(1,128)S(1)} %copy.130), channel_id=1, source_target_pairs={{32,0},{64,32},{96,64},{128,96},{160,128},{192,160},{224,192},{33,... | collective-permute-start | bytes 87560 | tf_op jit(solution)/shard_map/ppermute | solution.py:41
  2.1 7.6 %collective-permute-start.1 = (f32[3,19,1,1,128]{4,2,0,3,1:T(1,128)S(1)}, f32[3,19,1,1,128]{4,2,0,3,1:T(1,128)S(1)}, u32[]{:S(2)}, u32[]{:S(2)}) collective-permute-start(f32[3,19,1,1,128]{4,2,0,3,1:T(1,128)S(1)} %copy.132), channel_id=1, source_target_pairs={{0,32},{32,64},{64,96},{96,128},{128,160},{160,192},{192,224},{1,3... | collective-permute-start | bytes 87560 | tf_op jit(solution)/shard_map/ppermute | solution.py:40
  9.8 8.0 %collective-permute-start.3 = (f32[3,19,4,1,128]{4,2,0,3,1:T(4,128)S(1)}, f32[3,19,4,1,128]{4,2,0,3,1:T(4,128)S(1)}, u32[]{:S(2)}, u32[]{:S(2)}) collective-permute-start(f32[3,19,4,1,128]{4,2,0,3,1:T(4,128)S(1)} %pad_maximum_fusion), channel_id=1, source_target_pairs={{0,1},{1,2},{2,3},{3,4},{4,5},{5,6},{6,7},{7,8},{8,9},{9,10},{10,1... | collective-permute-start | bytes 350216 | tf_op jit(solution)/shard_map/ppermute | solution.py:40
  13.7 7.9 %collective-permute-start.2 = (f32[3,19,4,1,128]{4,2,0,3,1:T(4,128)S(1)}, f32[3,19,4,1,128]{4,2,0,3,1:T(4,128)S(1)}, u32[]{:S(2)}, u32[]{:S(2)}) collective-permute-start(f32[3,19,4,1,128]{4,2,0,3,1:T(4,128)S(1)} %pad_maximum_fusion), channel_id=1, source_target_pairs={{1,0},{2,1},{3,2},{4,3},{5,4},{6,5},{7,6},{8,7},{9,8},{10,9},{11,1... | collective-permute-start | bytes 350216 | tf_op jit(solution)/shard_map/ppermute | solution.py:41
  24.1 30.4 %copy-start.1 = (f32[3]{0:T(128)S(1)}, f32[3]{0:T(128)}, u32[]{:S(2)}) copy-start(f32[3]{0:T(128)} %param.21) | copy-start | bytes 40
  33.9 20.5 %all-to-all-start = ((bf16[3,32,4,128]{3,2,0,1:T(4,128)(2,1)}), bf16[3,32,4,128]{3,2,0,1:T(4,128)(2,1)S(1)}, u32[]{:S(2)}, u32[]{:S(2)}) async-start(bf16[3,32,4,128]{3,2,0,1:T(4,128)(2,1)} %copy.158), calls=%async_computation | async-start | bytes 196608 | tf_op jit(solution)/shard_map/all_to_all | solution.py:108
  59.7 14.9 %all-to-all-start.1 = ((f32[3,32,4,128]{3,2,0,1:T(4,128)}), f32[3,32,4,128]{3,2,0,1:T(4,128)S(1)}, u32[]{:S(2)}, u32[]{:S(2)}) async-start(f32[3,32,4,128]{3,2,0,1:T(4,128)} %copy.160), calls=%async_computation.1 | async-start | bytes 393216 | tf_op jit(solution)/shard_map/all_to_all | solution.py:113
  64.5 17.2 %copy-start.2 = (f32[19]{0:T(128)S(1)}, f32[19]{0:T(128)}, u32[]{:S(2)}) copy-start(f32[19]{0:T(128)} %constant.52.clone) | copy-start | bytes 232
  74.7 24.4 %copy-start = (f32[3]{0:T(128)S(1)}, f32[3]{0:T(128)}, u32[]{:S(2)}) copy-start(f32[3]{0:T(128)} %param.20) | copy-start | bytes 40
  82.0 4.6 %collective-permute-start.4 = (f32[3,19,1,1,128]{4,2,0,3,1:T(1,128)S(1)}, f32[3,19,1,1,128]{4,2,0,3,1:T(1,128)S(1)}, u32[]{:S(2)}, u32[]{:S(2)}) collective-permute-start(f32[3,19,1,1,128]{4,2,0,3,1:T(1,128)S(1)} %get-tuple-element.219), channel_id=1, source_target_pairs={{32,0},{64,32},{96,64},{128,96},{160,128},{192,160},{224,192},{33,... | collective-permute-start | bytes 87560 | tf_op jit(solution)/shard_map/ppermute | solution.py:41
  83.3 3.9 %collective-permute-start.5 = (f32[3,19,1,1,128]{4,2,0,3,1:T(1,128)S(1)}, f32[3,19,1,1,128]{4,2,0,3,1:T(1,128)S(1)}, u32[]{:S(2)}, u32[]{:S(2)}) collective-permute-start(f32[3,19,1,1,128]{4,2,0,3,1:T(1,128)S(1)} %get-tuple-element.218), channel_id=1, source_target_pairs={{0,32},{32,64},{64,96},{96,128},{128,160},{160,192},{192,224},{1,3... | collective-permute-start | bytes 87560 | tf_op jit(solution)/shard_map/ppermute | solution.py:40
  87.2 10.8 %collective-permute-start.7 = (f32[3,19,4,1,128]{4,2,0,3,1:T(4,128)S(1)}, f32[3,19,4,1,128]{4,2,0,3,1:T(4,128)S(1)}, u32[]{:S(2)}, u32[]{:S(2)}) collective-permute-start(f32[3,19,4,1,128]{4,2,0,3,1:T(4,128)S(1)} %pad_maximum_fusion.1), channel_id=1, source_target_pairs={{0,1},{1,2},{2,3},{3,4},{4,5},{5,6},{6,7},{7,8},{8,9},{9,10},{10,1... | collective-permute-start | bytes 350216 | tf_op jit(solution)/shard_map/ppermute | solution.py:40
  90.0 8.0 %collective-permute-start.6 = (f32[3,19,4,1,128]{4,2,0,3,1:T(4,128)S(1)}, f32[3,19,4,1,128]{4,2,0,3,1:T(4,128)S(1)}, u32[]{:S(2)}, u32[]{:S(2)}) collective-permute-start(f32[3,19,4,1,128]{4,2,0,3,1:T(4,128)S(1)} %pad_maximum_fusion.1), channel_id=1, source_target_pairs={{1,0},{2,1},{3,2},{4,3},{5,4},{6,5},{7,6},{8,7},{9,8},{10,9},{11,1... | collective-permute-start | bytes 350216 | tf_op jit(solution)/shard_map/ppermute | solution.py:41
  110.0 17.5 %all-to-all-start.2 = ((bf16[3,32,4,128]{3,2,0,1:T(4,128)(2,1)}), bf16[3,32,4,128]{3,2,0,1:T(4,128)(2,1)S(1)}, u32[]{:S(2)}, u32[]{:S(2)}) async-start(bf16[3,32,4,128]{3,2,0,1:T(4,128)(2,1)} %copy.192), calls=%async_computation.2 | async-start | bytes 196608 | tf_op jit(solution)/shard_map/all_to_all | solution.py:108
  132.7 14.8 %all-to-all-start.3 = ((f32[3,32,4,128]{3,2,0,1:T(4,128)}), f32[3,32,4,128]{3,2,0,1:T(4,128)S(1)}, u32[]{:S(2)}, u32[]{:S(2)}) async-start(f32[3,32,4,128]{3,2,0,1:T(4,128)} %copy.194), calls=%async_computation.3 | async-start | bytes 393216 | tf_op jit(solution)/shard_map/all_to_all | solution.py:113
where the time goes:
time: 157 us; the launch traced here: 155 us
  starting transfers between devices  48.4 us (31%)
  waiting for transfers between devices  45.9 us (29%)
  matrix products  38.7 us (25%)
  local copies, waits for them, and re-layouts  13 us (8%)
  other arithmetic  8.38 us (5%)
    all_to_all x2, waiting for transfers between devices, couple(): lax.all_to_all(answer, 'work', split_axis=1, concat_axis=1, tiled=True)  20.3 us
    all_to_all x2, starting transfers between devices, couple(): lax.all_to_all(outgoing, 'work', split_axis=1, concat_axis=1, tiled=True)  19.1 us
    all_to_all x2, waiting for transfers between devices, couple(): lax.all_to_all(outgoing, 'work', split_axis=1, concat_axis=1, tiled=True)  18.6 us
    dot_general x16, matrix products, pick_group(): jnp.dot(flat_density, table.T, precision=lax.Precision.HIGHEST, preferred...  17 us
    dot_general x16, matrix products, spread_group(): jnp.dot(values, table, precision=lax.Precision.HIGHEST, preferred_element...  12.9 us
    ppermute x4, starting transfers between devices, extended(): before = lax.ppermute(last, axis, up)  12.6 us
    all_to_all x2, starting transfers between devices, couple(): lax.all_to_all(answer, 'work', split_axis=1, concat_axis=1, tiled=True)  8.89 us
    dot_general x2, matrix products, couple(): jnp.einsum('bkij,sbkj->sbki', response[0, 0], incoming, preferred_element...  8.86 us
  transfers between devices with their start and end apart: 12, of which 7 were waited for; matrix products, arithmetic and copies ran while one was open for 6% of the time, Pallas kernels for 0%

commit v1 on v0

v1 whole, which is shorter than its diff:
```python
import jax
import jax.numpy as jnp
from jax import lax
from jax.experimental import pallas as pl
from jax.experimental.pallas import tpu as pltpu
from jax.sharding import PartitionSpec as P

DIRECTIONS = (
    (0, 0, 0),
    (1, 0, 0),
    (-1, 0, 0),
    (0, 1, 0),
    (0, -1, 0),
    (0, 0, 1),
    (0, 0, -1),
    (1, 1, 0),
    (-1, -1, 0),
    (1, -1, 0),
    (-1, 1, 0),
    (1, 0, 1),
    (-1, 0, -1),
    (1, 0, -1),
    (-1, 0, 1),
    (0, 1, 1),
    (0, -1, -1),
    (0, 1, -1),
    (0, -1, 1),
)
WEIGHTS = (1.0 / 3.0,) + (1.0 / 18.0,) * 6 + (1.0 / 36.0,) * 12
INDEX = {c: i for i, c in enumerate(DIRECTIONS)}

MIDDLE = ((0, 0, 0), (0, 0, 1), (0, 0, -1), (0, 1, 0), (0, 1, 1), (0, 1, -1), (0, -1, 0), (0, -1, 1), (0, -1, -1))
PLUS = ((1, 0, 0), (1, 0, 1), (1, 0, -1), (1, 1, 0), (1, -1, 0))
MINUS = ((-1, 0, 0), (-1, 0, 1), (-1, 0, -1), (-1, 1, 0), (-1, -1, 0))
PLACE = {c: n for n, c in enumerate(MIDDLE)}
PLACE.update({c: n for n, c in enumerate(PLUS)})
PLACE.update({c: n for n, c in enumerate(MINUS)})
SPECIES = 3
LANES = 128
F32 = jnp.float32
BF16 = jnp.bfloat16
CHUNKS = 4

VM = pl.BlockSpec(memory_space=pltpu.VMEM)
SM = pl.BlockSpec(memory_space=pltpu.SMEM)
HBM = pl.BlockSpec(memory_space=pl.ANY)


def tile(count, dtype=F32, rows=8):
    return jax.ShapeDtypeStruct((count, rows, LANES), dtype)


def rows_of(shape=(8, LANES)):
    return lax.broadcasted_iota(jnp.int32, shape, 0)


def half(value):
    return pltpu.roll(value, 4, 0)


def along(value, step):
    return pltpu.roll(value, (-step) % LANES, 1) if step else value


def per_species(ref):
    species = rows_of() % 4
    out = jnp.zeros((8, LANES), F32)
    for s in range(SPECIES):
        out = jnp.where(species == s, ref[s], out)
    return out


def mask_tile(mask_ref):
    keep = mask_ref[:].astype(F32)
    return jnp.where(rows_of() < 4, keep[0:1], keep[1:2])


def speed_tiles(velocity_ref):
    speeds = velocity_ref[:].astype(F32)
    low = rows_of() < 4
    return [jnp.where(low, speeds[2 * c : 2 * c + 1], speeds[2 * c + 1 : 2 * c + 2]) for c in range(3)]


def moment(pulled, speeds):
    density = None
    for c, value in pulled.items():
        factor = 1.0
        drift = None
        for axis in range(3):
            if c[axis]:
                part = speeds[axis] if c[axis] > 0 else -speeds[axis]
                drift = part if drift is None else drift + part
        weight = WEIGHTS[INDEX[c]]
        term = value * weight if drift is None else value * (weight + (3.0 * weight) * drift)
        density = term if density is None else density + term
    return density


def edges():
    a = lax.axis_index("space")
    b = lax.axis_index("work")
    return (a < lax.axis_size("space") - 1, a > 0, b < lax.axis_size("work") - 1, b > 0)


def arrange_kernel(field_ref, mask_ref, middle_ref, plus_ref, minus_ref):
    keep = mask_ref[:].astype(F32)
    for group, ref in ((MIDDLE, middle_ref), (PLUS, plus_ref), (MINUS, minus_ref)):
        for n, c in enumerate(group):
            for x in range(2):
                ref[n, 4 * x : 4 * x + 3, :] = field_ref[pl.ds(INDEX[c] * 2 + x, SPECIES, stride=38), :]
                ref[n, 4 * x + 3 : 4 * x + 4, :] = keep[x : x + 1]


def across_kernel(middle_ref, plus_ref, minus_ref, right_ref, left_ref, up_ref, down_ref):
    has_right, has_left, _, _ = edges()
    for sign, ref in ((1, up_ref), (-1, down_ref)):
        for n, cz in enumerate((0, 1, -1)):
            ref[n] = middle_ref[PLACE[(0, sign, cz)]]
        p = PLACE[(1, sign, 0)]
        ref[3] = plus_ref[p]
        ref[4] = jnp.where(has_right, right_ref[p], 0.0)
        p = PLACE[(-1, sign, 0)]
        ref[5] = minus_ref[p]
        ref[6] = jnp.where(has_left, left_ref[p], 0.0)


def write_payload(payload_ref, density, cells_ref, load_ref):
    high = density.astype(BF16).astype(F32)
    low = density - high
    rows = rows_of()
    for q in range(payload_ref.shape[0]):
        load = load_ref[q]
        cells = cells_ref[4 * q : 4 * q + 4, :].astype(F32)
        live = [jnp.where(k < load, cells[k : k + 1], -1.0) for k in range(4)]
        top = jnp.where(rows == 3, live[0], jnp.where(rows == 7, live[1], high))
        bottom = jnp.where(rows == 3, live[2], jnp.where(rows == 7, live[3], low))
        payload_ref[q] = jnp.concatenate([top, bottom], axis=0).astype(BF16)


def first_kernel(
    middle_ref, plus_ref, minus_ref, right_ref, left_ref, above_ref, below_ref,
    velocity_ref, mask_ref, cells_ref, relaxation_ref, load_ref,
    stay_ref, up_ref, down_ref, gain_ref, payload_ref,
):
    has_right, has_left, has_above, has_below = edges()
    first_half = rows_of() < 4
    rate = per_species(relaxation_ref)
    keep = mask_tile(mask_ref)
    right = [jnp.where(has_right, right_ref[n], 0.0) for n in range(5)]
    left = [jnp.where(has_left, left_ref[n], 0.0) for n in range(5)]
    above = [jnp.where(has_above, above_ref[n], 0.0) for n in range(7)]
    below = [jnp.where(has_below, below_ref[n], 0.0) for n in range(7)]
    pulled = {}
    for cz in (0, 1, -1):
        pulled[(0, 0, cz)] = along(middle_ref[PLACE[(0, 0, cz)]], cz)
        p = PLACE[(1, 0, cz)]
        pulled[(1, 0, cz)] = along(jnp.where(first_half, half(plus_ref[p]), half(right[p])), cz)
        p = PLACE[(-1, 0, cz)]
        pulled[(-1, 0, cz)] = along(jnp.where(first_half, half(left[p]), half(minus_ref[p])), cz)
    for sign, side in ((1, above), (-1, below)):
        for n, cz in enumerate((0, 1, -1)):
            pulled[(0, sign, cz)] = along(side[n], cz)
        pulled[(1, sign, 0)] = jnp.where(first_half, half(side[3]), half(side[4]))
        pulled[(-1, sign, 0)] = jnp.where(first_half, half(side[6]), half(side[5]))
    pulled = {c: pulled[c] for c in DIRECTIONS if c in pulled}
    density = moment(pulled, speed_tiles(velocity_ref))
    write_payload(payload_ref, density, cells_ref, load_ref)

    kept = 1.0 - rate
    right_mask = jnp.where(first_half, keep[4:5], right[0][3:4])
    left_mask = jnp.where(first_half, left[0][7:8], keep[0:1])
    here, to_right, to_left = (keep * kept, right_mask * kept, left_mask * kept)
    for n, cz in enumerate((0, 1, -1)):
        stay_ref[n] = here * pulled[(0, 0, cz)]
        stay_ref[3 + n] = to_right * along(right[PLACE[(1, 0, cz)]], cz)
        stay_ref[6 + n] = to_left * along(left[PLACE[(-1, 0, cz)]], cz)
    for sign, side, ref in ((1, above, up_ref), (-1, below, down_ref)):
        for n, cz in enumerate((0, 1, -1)):
            ref[n] = here * pulled[(0, sign, cz)]
        ref[3] = to_right * side[4]
        ref[4] = to_left * side[6]
    for n, side in enumerate((below, None, above)):
        if side is None:
            gain_ref[n] = keep * rate
        else:
            gain_ref[n] = jnp.where(first_half, side[0][3:4], side[0][7:8]) * rate
    gain_ref[3] = density


def owner_kernel(incoming_ref, response_ref, out_ref, matrices_ref, sums_ref, done, *, fold):
    count = incoming_ref.shape[0]
    each = count // CHUNKS
    copies = [
        pltpu.make_async_copy(
            response_ref.at[pl.ds(n * each, each)], matrices_ref.at[pl.ds(n * each, each)], done.at[n]
        )
        for n in range(CHUNKS)
    ]
    for copy in copies:
        copy.start()
    if fold:
        out_ref[0, 16:24, :] = jnp.zeros((8, LANES), BF16)
        out_ref[count - 1, 24:32, :] = jnp.zeros((8, LANES), BF16)
    first_half = rows_of() < 4
    cell_rows = lax.broadcasted_iota(jnp.int32, (LANES, LANES), 0)
    contract = (((1,), (1,)), ((), ()))

    def one(b):
        tiles = incoming_ref[b].astype(F32)
        top = tiles[0:8]
        lefts = []
        rights = []
        for k, row in enumerate((3, 7, 11, 15)):
            cell = tiles[row : row + 1].astype(jnp.int32)
            lane = cell & (LANES - 1)
            second = jnp.broadcast_to(cell >> 7, (8, LANES))
            mine = second == jnp.where(first_half, 0, 1)
            found = jnp.take_along_axis(
                top, jnp.broadcast_to(lane, (8, LANES)), axis=1, mode="promise_in_bounds"
            )
            picked = jnp.where(mine, found, half(found)).astype(BF16)
            reply = lax.dot_general(picked, matrices_ref[b, k], contract, preferred_element_type=F32)
            reply = jnp.where(mine, reply, 0.0)
            high = reply.astype(BF16).astype(F32)
            lefts.append(jnp.concatenate([high, reply - high], axis=0).astype(BF16))
            rights.append(jnp.where(cell_rows == lane, 1.0, 0.0).astype(BF16))
        both = lax.dot_general(
            jnp.concatenate(lefts, axis=1), jnp.concatenate(rights, axis=1), contract, preferred_element_type=F32
        )
        total = both[0:8] + both[8:16]
        high = total.astype(BF16).astype(F32)
        out_ref[b, 0:16, :] = jnp.concatenate([high, total - high], axis=0).astype(BF16)
        sums_ref[b] = total

    for n in range(CHUNKS):
        copies[n].wait()

        def group(g, carry):
            for u in range(4):
                one(n * each + g * 4 + u)
            return carry

        lax.fori_loop(0, each // 4, group, 0)
    if fold:
        zero = jnp.zeros((8, LANES), F32)
        for b in range(count):
            before = sums_ref[b - 1] if b > 0 else zero
            after = sums_ref[b + 1] if b < count - 1 else zero
            out_ref[b, 16:32, :] = jnp.concatenate([before, after], axis=0).astype(BF16)


def total_of(returned_ref, rows):
    total = returned_ref[0, 0:rows, :].astype(F32)
    for q in range(1, returned_ref.shape[0]):
        total = total + returned_ref[q, 0:rows, :].astype(F32)
    return total


def gather_kernel(returned_ref, incoming_ref, gain_ref, uptake_ref, parts_ref, right_ref, left_ref):
    first_half = rows_of() < 4
    factor = per_species(uptake_ref)
    total = total_of(returned_ref, 32)
    sources = (total[16:24], total[0:8] + total[8:16], total[24:32])
    b = lax.axis_index("work")
    last = lax.axis_size("work") - 1
    for n, source in enumerate(sources):
        source = factor * source
        if n == 1:
            density = gain_ref[3]
        else:
            tiles = incoming_ref[jnp.clip(b + n - 1, 0, last)].astype(F32)
            density = tiles[0:8] + tiles[8:16]
        equilibrium = gain_ref[n] * density
        parts_ref[n] = equilibrium
        parts_ref[3 + n] = source
        right_ref[n] = jnp.where(first_half, equilibrium, half(source))
        left_ref[n] = jnp.where(first_half, half(equilibrium), source)


def second_kernel(
    stay_ref, above_ref, below_ref, parts_ref, right_ref, left_ref,
    velocity_ref, cells_ref, load_ref,
    pulled_ref, density_ref, payload_ref,
):
    has_right, has_left, has_above, has_below = edges()
    first_half = rows_of() < 4
    pulled = {}
    for n, cy in enumerate((-1, 0, 1)):
        equilibrium, source = (parts_ref[n], parts_ref[3 + n])
        right = jnp.where(has_right, right_ref[n], 0.0)
        left = jnp.where(has_left, left_ref[n], 0.0)
        moved = {
            0: (equilibrium, source),
            1: (jnp.where(first_half, half(equilibrium), half(right)), jnp.where(first_half, half(source), right)),
            -1: (jnp.where(first_half, left, half(equilibrium)), jnp.where(first_half, half(left), half(source))),
        }
        for c in DIRECTIONS:
            if c[1] != cy:
                continue
            shifted, added = moved[c[0]]
            if cy == 0:
                base = stay_ref[(0, 3, 6)[c[0]] + (0, 1, 2)[c[2]]]
            else:
                inside, ref = (has_above, above_ref) if cy > 0 else (has_below, below_ref)
                base = ref[(0, 1, 2)[c[2]] if c[0] == 0 else (3 if c[0] > 0 else 4)]
                base = jnp.where(inside, base, 0.0)
            pulled[c] = along(base + shifted + WEIGHTS[INDEX[c]] * added, c[2])
    pulled = {c: pulled[c] for c in DIRECTIONS}
    density = moment(pulled, speed_tiles(velocity_ref))
    write_payload(payload_ref, density, cells_ref, load_ref)
    for i, c in enumerate(DIRECTIONS):
        pulled_ref[i] = pulled[c]
    density_ref[0] = density


def last_kernel(returned_ref, pulled_ref, density_ref, mask_ref, relaxation_ref, uptake_ref, out_ref):
    total = total_of(returned_ref, 16)
    source = per_species(uptake_ref) * (total[0:8] + total[8:16])
    rate = per_species(relaxation_ref)
    keep = mask_tile(mask_ref)
    shared = keep * rate * density_ref[0]
    here = keep * (1.0 - rate)
    for i in range(len(DIRECTIONS)):
        value = here * pulled_ref[i] + shared + WEIGHTS[i] * source
        for x in range(2):
            out_ref[pl.ds(i * 2 + x, SPECIES, stride=38), :] = value[4 * x : 4 * x + 3]


def call(kernel, out_shape, in_specs, name, **rest):
    single = not isinstance(out_shape, (tuple, list))
    return pl.pallas_call(
        kernel,
        out_shape=out_shape,
        in_specs=in_specs,
        out_specs=VM if single else tuple(VM for _ in out_shape),
        name=name,
        compiler_params=pltpu.CompilerParams(vmem_limit_bytes=32 * 1024 * 1024),
        **rest,
    )


def body(adjoint, velocity, relaxation, uptake, fluid_mask, block_cells, owner_load, response):
    columns = lax.axis_size("space")
    owners = lax.axis_size("work")
    field = adjoint.reshape(-1, LANES)
    speeds = velocity.reshape(-1, LANES)
    mask = fluid_mask.reshape(-1, LANES)
    cells = block_cells.reshape(-1, LANES)
    load = owner_load.reshape(-1)
    matrices = response.reshape(response.shape[2:])

    def to_lower(value, axis, count):
        return lax.ppermute(value, axis, [((i + 1) % count, i) for i in range(count)])

    def to_upper(value, axis, count):
        return lax.ppermute(value, axis, [(i, (i + 1) % count) for i in range(count)])

    def owner(incoming, fold):
        return call(
            lambda *refs: owner_kernel(*refs, fold=fold),
            jax.ShapeDtypeStruct((owners, 32 if fold else 16, LANES), BF16),
            [VM, HBM],
            "owner_fold" if fold else "owner",
            scratch_shapes=[
                pltpu.VMEM(matrices.shape, BF16),
                pltpu.VMEM((owners, 8, LANES), F32),
                pltpu.SemaphoreType.DMA((CHUNKS,)),
            ],
        )(incoming, matrices)

    def exchange(value):
        return lax.all_to_all(value, "work", split_axis=0, concat_axis=0, tiled=True)

    payload_shape = jax.ShapeDtypeStruct((owners, 16, LANES), BF16)
    middle, plus, minus = call(arrange_kernel, (tile(9), tile(5), tile(5)), [VM] * 2, "arrange")(field, mask)
    right = to_lower(plus, "space", columns)
    left = to_upper(minus, "space", columns)
    up, down = call(across_kernel, (tile(7), tile(7)), [VM] * 5, "across")(middle, plus, minus, right, left)
    above = to_lower(up, "work", owners)
    below = to_upper(down, "work", owners)
    stay, up, down, gain, payload = call(
        first_kernel, (tile(9), tile(5), tile(5), tile(4), payload_shape), [VM] * 10 + [SM] * 2, "first"
    )(middle, plus, minus, right, left, above, below, speeds, mask, cells, relaxation, load)
    incoming = exchange(payload)
    above = to_lower(up, "work", owners)
    below = to_upper(down, "work", owners)
    returned = exchange(owner(incoming, True))
    parts, right, left = call(gather_kernel, (tile(6), tile(3), tile(3)), [VM] * 3 + [SM], "gather")(
        returned, incoming, gain, uptake
    )
    right = to_lower(right, "space", columns)
    left = to_upper(left, "space", columns)
    pulled, density, payload = call(
        second_kernel, (tile(19), tile(1), payload_shape), [VM] * 8 + [SM], "second"
    )(stay, above, below, parts, right, left, speeds, cells, load)
    returned = exchange(owner(exchange(payload), False))
    out = call(last_kernel, jax.ShapeDtypeStruct(field.shape, F32), [VM] * 4 + [SM] * 2, "last")(
        returned, pulled, density, mask, relaxation, uptake
    )
    return out.reshape(adjoint.shape)


def solution(mesh):
    placed = (
        P(None, None, "space", "work", None),
        P(None, "space", "work", None),
        P(),
        P(),
        P("space", "work", None),
        P("space", "work", None, None, None),
        P("space", "work", None),
        P("space", "work", None, None, None, None),
    )
    return jax.shard_map(
        body,
        mesh=mesh,
        in_specs=placed,
        out_specs=P(None, None, "space", "work", None),
        check_vma=False,
    )
```

time: 157 us -> 110 us (0.70)
  blocking collectives: 0 us -> 45.6 us
  matrix products: 38.7 us -> 0 us
  starting transfers between devices: 48.4 us -> 11.2 us
  waiting for transfers between devices: 45.9 us -> 24.8 us
  Pallas kernels: 0 us -> 17.4 us
  other arithmetic: 8.38 us -> 0 us
  local copies, waits for them, and re-layouts: 13 us -> 10.2 us
    all_to_all x0 -> x3, blocking collectives: none -> 45.6 us  [exchange(): lax.all_to_all(value, 'work', split_axis=0, concat_axis=0, tiled=True)]
    dot_general x34 -> x0, matrix products: 38.7 us -> none  [the longest x16 17 us: pick_group(): jnp.dot(flat_density, table.T, precision=lax.Precision.HIGHEST, preferred...]
    all_to_all x4 -> x1, waiting for transfers between devices: 38.9 us -> 8.96 us  [exchange(): lax.all_to_all(value, 'work', split_axis=0, concat_axis=0, tiled=True)]
    all_to_all x4 -> x1, starting transfers between devices: 28 us -> 4.4 us  [exchange(): lax.all_to_all(value, 'work', split_axis=0, concat_axis=0, tiled=True)]
    pallas_call x0 -> x8, Pallas kernels: none -> 17.4 us  [the longest x2 14.8 us: owner(): call(lambda *refs: owner_kernel(*refs, fold=fold), jax.ShapeDtypeStruct((...]
    ppermute x8, starting transfers between devices: 20.3 us -> 6.85 us  [the longest x4 4.1 us: to_upper(): lax.ppermute(value, axis, [(i, (i + 1) % count) for i in range(count)])]
    ppermute x8, waiting for transfers between devices: 7.03 us -> 15.8 us  [the longest x4 12.3 us: to_upper(): lax.ppermute(value, axis, [(i, (i + 1) % count) for i in range(count)])]
    unnamed x27 -> x26, local copies, waits for them, and re-layouts: 1.06 us -> 8.82 us
  transfers between devices with their start and end apart: 12 -> 9, of which waited for: 7 -> 7; matrix products, arithmetic and copies ran while one was open for 6% -> 1% of each run, Pallas kernels for 0% -> 1%
where the time goes in v1:
time: 110 us; the launch traced here: 109 us
  blocking collectives  45.6 us (41%)
  waiting for transfers between devices  24.8 us (23%)
  Pallas kernels  17.4 us (16%)
  starting transfers between devices  11.2 us (10%)
  local copies, waits for them, and re-layouts  10.2 us (9%)
    all_to_all x3, blocking collectives, exchange(): lax.all_to_all(value, 'work', split_axis=0, concat_axis=0, tiled=True)  45.6 us
    pallas_call x2, Pallas kernels, owner(): call(lambda *refs: owner_kernel(*refs, fold=fold), jax.ShapeDtypeStruct((...  14.8 us
    ppermute x4, waiting for transfers between devices, to_upper(): lax.ppermute(value, axis, [(i, (i + 1) % count) for i in range(count)])  12.3 us
    all_to_all x1, waiting for transfers between devices, exchange(): lax.all_to_all(value, 'work', split_axis=0, concat_axis=0, tiled=True)  8.96 us
    unnamed x26, local copies, waits for them, and re-layouts  8.82 us
    all_to_all x1, starting transfers between devices, exchange(): lax.all_to_all(value, 'work', split_axis=0, concat_axis=0, tiled=True)  4.4 us
    ppermute x4, starting transfers between devices, to_upper(): lax.ppermute(value, axis, [(i, (i + 1) % count) for i in range(count)])  4.1 us
    ppermute x4, waiting for transfers between devices, to_lower(): lax.ppermute(value, axis, [((i + 1) % count, i) for i in range(count)])  3.52 us
  transfers between devices with their start and end apart: 9, of which 7 were waited for; matrix products, arithmetic and copies ran while one was open for 1% of the time, Pallas kernels for 1%

profile of v1, /device:TPU:32, one launch (start us, length us, event | category | flops | bytes accessed | tf_op | source)
XLA Modules:
  0.0 109.3 jit_solution(9353088218236072626)
XLA Ops:
  0.0 0.0 copy-start.8
  0.0 0.0 copy-start.3
  0.0 0.0 copy-start.11
  0.0 0.9 pad
  0.9 0.0 copy-start.4
  0.9 0.7 copy-done.4
  1.7 2.2 %collective-permute-start = (f32[5,8,128]{2,1,0:T(8,128)S(1)}, f32[5,8,128]{2,1,0:T(8,128)S(1)}, u32[]{:S(2)}, u32[]{:S(2)}) collective-permute-start(f32[5,8,128]{2,1,0:T(8,128)S(1)} %get-tuple-element.22.plus_ref), channel_id=1, source_target_pairs={{32,0},{64,32},{96,64},{128,96},{160,128},{192,160},{224,192},{0,2... | collective-permute-start | bytes 61448 | tf_op jit(solution)/shard_map/ppermute | solution.py:353
  3.9 0.0 collective-permute-start.1
  3.9 1.5 %collective-permute-done.right_ref = f32[5,8,128]{2,1,0:T(8,128)S(1)} collective-permute-done((f32[5,8,128]{2,1,0:T(8,128)S(1)}, f32[5,8,128]{2,1,0:T(8,128)S(1)}, u32[]{:S(2)}, u32[]{:S(2)}) %collective-permute-start) | collective-permute-done | bytes 20512 | tf_op jit(solution)/shard_map/ppermute | solution.py:353
  5.3 2.9 %collective-permute-done.1.left_ref = f32[5,8,128]{2,1,0:T(8,128)S(1)} collective-permute-done((f32[5,8,128]{2,1,0:T(8,128)S(1)}, f32[5,8,128]{2,1,0:T(8,128)S(1)}, u32[]{:S(2)}, u32[]{:S(2)}) %collective-permute-start.1) | collective-permute-done | bytes 20512 | tf_op jit(solution)/shard_map/ppermute | solution.py:356
  8.3 0.1 collective-permute-start.2
  8.4 1.9 %collective-permute-start.3 = (f32[7,8,128]{2,1,0:T(8,128)S(1)}, f32[7,8,128]{2,1,0:T(8,128)S(1)}, u32[]{:S(2)}, u32[]{:S(2)}) collective-permute-start(f32[7,8,128]{2,1,0:T(8,128)S(1)} %get-tuple-element.25), channel_id=1, source_target_pairs={{0,1},{1,2},{2,3},{3,4},{4,5},{5,6},{6,7},{7,8},{8,9},{9,10},{10,1... | collective-permute-start | bytes 86024 | tf_op jit(solution)/shard_map/ppermute | solution.py:356
  10.3 0.7 reshape.23.velocity_ref
  11.0 1.1 %collective-permute-done.2.above_ref = f32[7,8,128]{2,1,0:T(8,128)S(1)} collective-permute-done((f32[7,8,128]{2,1,0:T(8,128)S(1)}, f32[7,8,128]{2,1,0:T(8,128)S(1)}, u32[]{:S(2)}, u32[]{:S(2)}) %collective-permute-start.2) | collective-permute-done | bytes 28704 | tf_op jit(solution)/shard_map/ppermute | solution.py:353
  12.2 6.4 %collective-permute-done.3.below_ref = f32[7,8,128]{2,1,0:T(8,128)S(1)} collective-permute-done((f32[7,8,128]{2,1,0:T(8,128)S(1)}, f32[7,8,128]{2,1,0:T(8,128)S(1)}, u32[]{:S(2)}, u32[]{:S(2)}) %collective-permute-start.3) | collective-permute-done | bytes 28704 | tf_op jit(solution)/shard_map/ppermute | solution.py:356
  18.5 0.0 copy-start.2
  18.6 0.8 copy-done.2
  19.4 0.0 copy-start.5
  19.4 0.7 copy-done.5
  20.1 0.0 copy-start.7
  20.1 0.7 copy-done.7
  20.7 0.0 copy-start.9
  20.7 0.7 copy-done.9
  21.4 0.7 first.1
  22.1 17.7 %all_to_all.20.refs_0_.incoming_ref = bf16[32,16,128]{2,1,0:T(8,128)(2,1)S(1)} all-to-all(bf16[32,16,128]{2,1,0:T(8,128)(2,1)S(1)} %get-tuple-element.29), channel_id=1, replica_groups=mesh['space'=8,'work'=32] {'work'}, dimensions={0} | all-to-all | bytes 262144 | tf_op jit(solution)/shard_map/all_to_all | solution.py:372
  39.8 0.0 copy-start
  39.8 2.2 %copy-done = bf16[1,1,32,4,128,128]{5,4,3,2,1,0:T(8,128)(2,1)S(1)} copy-done((bf16[1,1,32,4,128,128]{5,4,3,2,1,0:T(8,128)(2,1)S(1)}, bf16[1,1,32,4,128,128]{5,4,3,2,1,0:T(8,128)(2,1)}, u32[]{:S(2)}) %copy-start) | copy-done | bytes 4194328
  42.0 7.8 %owner_fold.1 = bf16[32,32,128]{2,1,0:T(8,128)(2,1)} custom-call(bf16[32,16,128]{2,1,0:T(8,128)(2,1)S(1)} %all_to_all.20.refs_0_.incoming_ref, bf16[32,4,128,128]{3,2,1,0:T(8,128)(2,1)S(1)} %bitcast.12), custom_call_target="tpu_custom_call" | custom-call | tf_op jit(solution)/shard_map/owner_fold/pallas_call | solution.py:359
  49.8 0.0 copy-start.6
  49.8 0.0 copy-start.10
  49.8 4.4 %all-to-all-start.1 = ((bf16[32,32,128]{2,1,0:T(8,128)(2,1)}), bf16[32,32,128]{2,1,0:T(8,128)(2,1)S(1)}, u32[]{:S(2)}, u32[]{:S(2)}) async-start(bf16[32,32,128]{2,1,0:T(8,128)(2,1)} %owner_fold.1), calls=%async_computation.1 | async-start | bytes 524288 | tf_op jit(solution)/shard_map/all_to_all | solution.py:372
  54.2 0.4 collective-permute-start.4
  54.6 1.7 %collective-permute-start.5 = (f32[5,8,128]{2,1,0:T(8,128)S(1)}, f32[5,8,128]{2,1,0:T(8,128)S(1)}, u32[]{:S(2)}, u32[]{:S(2)}) collective-permute-start(f32[5,8,128]{2,1,0:T(8,128)S(1)} %get-tuple-element.28), channel_id=1, source_target_pairs={{0,1},{1,2},{2,3},{3,4},{4,5},{5,6},{6,7},{7,8},{8,9},{9,10},{10,1... | collective-permute-start | bytes 61448 | tf_op jit(solution)/shard_map/ppermute | solution.py:356
  56.3 9.0 %all-to-all-done.1.returned_ref = bf16[32,32,128]{2,1,0:T(8,128)(2,1)S(1)} async-done(((bf16[32,32,128]{2,1,0:T(8,128)(2,1)}), bf16[32,32,128]{2,1,0:T(8,128)(2,1)S(1)}, u32[]{:S(2)}, u32[]{:S(2)}) %all-to-all-start.1) | async-done | bytes 262176 | tf_op jit(solution)/shard_map/all_to_all | solution.py:372
  65.3 0.0 copy-done.11
  65.3 0.6 gather.1
  65.9 0.0 collective-permute-start.6
  65.9 0.5 collective-permute-start.7
  66.4 0.0 collective-permute-done.4.above_ref
  66.4 0.0 collective-permute-done.5.below_ref
  66.4 0.9 collective-permute-done.6.right_ref
  67.3 2.9 %collective-permute-done.7.left_ref = f32[3,8,128]{2,1,0:T(8,128)S(1)} collective-permute-done((f32[3,8,128]{2,1,0:T(8,128)S(1)}, f32[3,8,128]{2,1,0:T(8,128)S(1)}, u32[]{:S(2)}, u32[]{:S(2)}) %collective-permute-start.7) | collective-permute-done | bytes 12320 | tf_op jit(solution)/shard_map/ppermute | solution.py:356
  70.3 0.0 copy-done.8
  70.3 0.0 copy-done.3
  70.3 0.7 second.1
  71.0 14.0 %all_to_all.21.refs_0_ = bf16[32,16,128]{2,1,0:T(8,128)(2,1)S(1)} all-to-all(bf16[32,16,128]{2,1,0:T(8,128)(2,1)S(1)} %get-tuple-element.34), channel_id=1, replica_groups=mesh['space'=8,'work'=32] {'work'}, dimensions={0} | all-to-all | bytes 262144 | tf_op jit(solution)/shard_map/all_to_all | solution.py:372
  85.0 0.0 copy-start.1
  85.0 2.2 %copy-done.1 = bf16[1,1,32,4,128,128]{5,4,3,2,1,0:T(8,128)(2,1)S(1)} copy-done((bf16[1,1,32,4,128,128]{5,4,3,2,1,0:T(8,128)(2,1)S(1)}, bf16[1,1,32,4,128,128]{5,4,3,2,1,0:T(8,128)(2,1)}, u32[]{:S(2)}) %copy-start.1) | copy-done | bytes 4194328
  87.1 7.1 %owner.1 = bf16[32,16,128]{2,1,0:T(8,128)(2,1)S(1)} custom-call(bf16[32,16,128]{2,1,0:T(8,128)(2,1)S(1)} %all_to_all.21.refs_0_, bf16[32,4,128,128]{3,2,1,0:T(8,128)(2,1)S(1)} %bitcast.13), custom_call_target="tpu_custom_call" | custom-call | tf_op jit(solution)/shard_map/owner/pallas_call | solution.py:359
  94.2 13.9 %all_to_all.22.returned_ref = bf16[32,16,128]{2,1,0:T(8,128)(2,1)S(1)} all-to-all(bf16[32,16,128]{2,1,0:T(8,128)(2,1)S(1)} %owner.1), channel_id=1, replica_groups=mesh['space'=8,'work'=32] {'work'}, dimensions={0} | all-to-all | bytes 262144 | tf_op jit(solution)/shard_map/all_to_all | solution.py:372
  108.1 0.0 copy-done.6
  108.1 0.0 copy-done.10
  108.1 0.6 last.1
  108.7 0.7 reshape.27
  (3 shorter events, 0.0 us)
Async XLA Ops:
  0.0 70.3 %copy-start.8 = (s32[1,1,32]{2,1,0:T(1,128)S(1)}, s32[1,1,32]{2,1,0:T(1,128)}, u32[]{:S(2)}) copy-start(s32[1,1,32]{2,1,0:T(1,128)} %param.14) | copy-start | bytes 388
  0.0 70.3 %copy-start.3 = (s32[1,1,32,4,128]{4,3,2,1,0:T(4,128)S(1)}, s32[1,1,32,4,128]{4,3,2,1,0:T(4,128)}, u32[]{:S(2)}) copy-start(s32[1,1,32,4,128]{4,3,2,1,0:T(4,128)} %param.13) | copy-start | bytes 196612
  0.0 65.3 %copy-start.11 = (f32[3]{0:T(128)S(1)}, f32[3]{0:T(128)}, u32[]{:S(2)}) copy-start(f32[3]{0:T(128)} %uptake_ref.3) | copy-start | bytes 40
  0.9 0.7 copy-start.4
  1.7 3.7 %collective-permute-start = (f32[5,8,128]{2,1,0:T(8,128)S(1)}, f32[5,8,128]{2,1,0:T(8,128)S(1)}, u32[]{:S(2)}, u32[]{:S(2)}) collective-permute-start(f32[5,8,128]{2,1,0:T(8,128)S(1)} %get-tuple-element.22.plus_ref), channel_id=1, source_target_pairs={{32,0},{64,32},{96,64},{128,96},{160,128},{192,160},{224,192},{0,2... | collective-permute-start | bytes 61448 | tf_op jit(solution)/shard_map/ppermute | solution.py:353
  3.9 4.4 %collective-permute-start.1 = (f32[5,8,128]{2,1,0:T(8,128)S(1)}, f32[5,8,128]{2,1,0:T(8,128)S(1)}, u32[]{:S(2)}, u32[]{:S(2)}) collective-permute-start(f32[5,8,128]{2,1,0:T(8,128)S(1)} %get-tuple-element.23.minus_ref), channel_id=1, source_target_pairs={{0,32},{32,64},{64,96},{96,128},{128,160},{160,192},{192,224},{224... | collective-permute-start | bytes 61448 | tf_op jit(solution)/shard_map/ppermute | solution.py:356
  8.3 3.9 %collective-permute-start.2 = (f32[7,8,128]{2,1,0:T(8,128)S(1)}, f32[7,8,128]{2,1,0:T(8,128)S(1)}, u32[]{:S(2)}, u32[]{:S(2)}) collective-permute-start(f32[7,8,128]{2,1,0:T(8,128)S(1)} %get-tuple-element.24), channel_id=1, source_target_pairs={{1,0},{2,1},{3,2},{4,3},{5,4},{6,5},{7,6},{8,7},{9,8},{10,9},{11,1... | collective-permute-start | bytes 86024 | tf_op jit(solution)/shard_map/ppermute | solution.py:353
  8.4 10.2 %collective-permute-start.3 = (f32[7,8,128]{2,1,0:T(8,128)S(1)}, f32[7,8,128]{2,1,0:T(8,128)S(1)}, u32[]{:S(2)}, u32[]{:S(2)}) collective-permute-start(f32[7,8,128]{2,1,0:T(8,128)S(1)} %get-tuple-element.25), channel_id=1, source_target_pairs={{0,1},{1,2},{2,3},{3,4},{4,5},{5,6},{6,7},{7,8},{8,9},{9,10},{10,1... | collective-permute-start | bytes 86024 | tf_op jit(solution)/shard_map/ppermute | solution.py:356
  18.5 0.8 copy-start.2
  19.4 0.7 copy-start.5
  20.1 0.7 copy-start.7
  20.7 0.7 copy-start.9
  39.8 2.2 %copy-start = (bf16[1,1,32,4,128,128]{5,4,3,2,1,0:T(8,128)(2,1)S(1)}, bf16[1,1,32,4,128,128]{5,4,3,2,1,0:T(8,128)(2,1)}, u32[]{:S(2)}) copy-start(bf16[1,1,32,4,128,128]{5,4,3,2,1,0:T(8,128)(2,1)} %param.15) | copy-start | bytes 12582916
  49.8 58.3 %copy-start.6 = (s32[2,1,128]{2,1,0:T(1,128)S(1)}, s32[2,1,128]{2,1,0:T(1,128)}, u32[]{:S(2)}) copy-start(s32[2,1,128]{2,1,0:T(1,128)} %param.12) | copy-start | bytes 3076
  49.8 58.3 %copy-start.10 = (f32[3]{0:T(128)S(1)}, f32[3]{0:T(128)}, u32[]{:S(2)}) copy-start(f32[3]{0:T(128)} %relaxation_ref.3) | copy-start | bytes 40
  49.8 15.5 %all-to-all-start.1 = ((bf16[32,32,128]{2,1,0:T(8,128)(2,1)}), bf16[32,32,128]{2,1,0:T(8,128)(2,1)S(1)}, u32[]{:S(2)}, u32[]{:S(2)}) async-start(bf16[32,32,128]{2,1,0:T(8,128)(2,1)} %owner_fold.1), calls=%async_computation.1 | async-start | bytes 524288 | tf_op jit(solution)/shard_map/all_to_all | solution.py:372
  54.2 12.2 %collective-permute-start.4 = (f32[5,8,128]{2,1,0:T(8,128)S(1)}, f32[5,8,128]{2,1,0:T(8,128)S(1)}, u32[]{:S(2)}, u32[]{:S(2)}) collective-permute-start(f32[5,8,128]{2,1,0:T(8,128)S(1)} %get-tuple-element.27), channel_id=1, source_target_pairs={{1,0},{2,1},{3,2},{4,3},{5,4},{6,5},{7,6},{8,7},{9,8},{10,9},{11,1... | collective-permute-start | bytes 61448 | tf_op jit(solution)/shard_map/ppermute | solution.py:353
  54.6 11.8 %collective-permute-start.5 = (f32[5,8,128]{2,1,0:T(8,128)S(1)}, f32[5,8,128]{2,1,0:T(8,128)S(1)}, u32[]{:S(2)}, u32[]{:S(2)}) collective-permute-start(f32[5,8,128]{2,1,0:T(8,128)S(1)} %get-tuple-element.28), channel_id=1, source_target_pairs={{0,1},{1,2},{2,3},{3,4},{4,5},{5,6},{6,7},{7,8},{8,9},{9,10},{10,1... | collective-permute-start | bytes 61448 | tf_op jit(solution)/shard_map/ppermute | solution.py:356
  65.9 1.4 %collective-permute-start.6 = (f32[3,8,128]{2,1,0:T(8,128)S(1)}, f32[3,8,128]{2,1,0:T(8,128)S(1)}, u32[]{:S(2)}, u32[]{:S(2)}) collective-permute-start(f32[3,8,128]{2,1,0:T(8,128)S(1)} %get-tuple-element.32), channel_id=1, source_target_pairs={{32,0},{64,32},{96,64},{128,96},{160,128},{192,160},{224,192},{0,2... | collective-permute-start | bytes 36872 | tf_op jit(solution)/shard_map/ppermute | solution.py:353
  65.9 4.3 %collective-permute-start.7 = (f32[3,8,128]{2,1,0:T(8,128)S(1)}, f32[3,8,128]{2,1,0:T(8,128)S(1)}, u32[]{:S(2)}, u32[]{:S(2)}) collective-permute-start(f32[3,8,128]{2,1,0:T(8,128)S(1)} %get-tuple-element.33), channel_id=1, source_target_pairs={{0,32},{32,64},{64,96},{96,128},{128,160},{160,192},{192,224},{224... | collective-permute-start | bytes 36872 | tf_op jit(solution)/shard_map/ppermute | solution.py:356
  85.0 2.2 %copy-start.1 = (bf16[1,1,32,4,128,128]{5,4,3,2,1,0:T(8,128)(2,1)S(1)}, bf16[1,1,32,4,128,128]{5,4,3,2,1,0:T(8,128)(2,1)}, u32[]{:S(2)}) copy-start(bf16[1,1,32,4,128,128]{5,4,3,2,1,0:T(8,128)(2,1)} %param.15) | copy-start | bytes 12582916

commit v2 on v1

v2 whole, which is shorter than its diff:
```python
import jax
import jax.numpy as jnp
from jax import lax
from jax.experimental import pallas as pl
from jax.experimental.pallas import tpu as pltpu
from jax.sharding import PartitionSpec as P

DIRECTIONS = (
    (0, 0, 0),
    (1, 0, 0),
    (-1, 0, 0),
    (0, 1, 0),
    (0, -1, 0),
    (0, 0, 1),
    (0, 0, -1),
    (1, 1, 0),
    (-1, -1, 0),
    (1, -1, 0),
    (-1, 1, 0),
    (1, 0, 1),
    (-1, 0, -1),
    (1, 0, -1),
    (-1, 0, 1),
    (0, 1, 1),
    (0, -1, -1),
    (0, 1, -1),
    (0, -1, 1),
)
WEIGHTS = (1.0 / 3.0,) + (1.0 / 18.0,) * 6 + (1.0 / 36.0,) * 12
INDEX = {c: i for i, c in enumerate(DIRECTIONS)}

MIDDLE = ((0, 0, 0), (0, 0, 1), (0, 0, -1), (0, 1, 0), (0, 1, 1), (0, 1, -1), (0, -1, 0), (0, -1, 1), (0, -1, -1))
PLUS = ((1, 0, 0), (1, 0, 1), (1, 0, -1), (1, 1, 0), (1, -1, 0))
MINUS = ((-1, 0, 0), (-1, 0, 1), (-1, 0, -1), (-1, 1, 0), (-1, -1, 0))
PLACE = {c: n for n, c in enumerate(MIDDLE)}
PLACE.update({c: n for n, c in enumerate(PLUS)})
PLACE.update({c: n for n, c in enumerate(MINUS)})
SPECIES = 3
LANES = 128
F32 = jnp.float32
BF16 = jnp.bfloat16
CHUNKS = 4

VM = pl.BlockSpec(memory_space=pltpu.VMEM)
SM = pl.BlockSpec(memory_space=pltpu.SMEM)
HBM = pl.BlockSpec(memory_space=pltpu.HBM)


def tile(count, dtype=F32, rows=8):
    return jax.ShapeDtypeStruct((count, rows, LANES), dtype)


def rows_of(shape=(8, LANES)):
    return lax.broadcasted_iota(jnp.int32, shape, 0)


def half(value):
    return pltpu.roll(value, 4, 0)


def along(value, step):
    return pltpu.roll(value, (-step) % LANES, 1) if step else value


def per_species(ref):
    species = rows_of() % 4
    out = jnp.zeros((8, LANES), F32)
    for s in range(SPECIES):
        out = jnp.where(species == s, ref[s], out)
    return out


def moment(pulled, speeds):
    density = None
    for c, value in pulled.items():
        factor = 1.0
        drift = None
        for axis in range(3):
            if c[axis]:
                part = speeds[axis] if c[axis] > 0 else -speeds[axis]
                drift = part if drift is None else drift + part
        weight = WEIGHTS[INDEX[c]]
        term = value * weight if drift is None else value * (weight + (3.0 * weight) * drift)
        density = term if density is None else density + term
    return density


def edges():
    a = lax.axis_index("space")
    b = lax.axis_index("work")
    return (a < lax.axis_size("space") - 1, a > 0, b < lax.axis_size("work") - 1, b > 0)


def is_even(axis):
    return lax.axis_index(axis) % 2 == 0


def arrange_kernel(
    field_hbm, velocity_hbm, mask_hbm, relaxation_ref, uptake_ref,
    middle_ref, near_ref, far_ref, fixed_ref,
    field_ref, velocity_ref, mask_ref, plus_ref, minus_ref, done,
):
    pairs = ((field_hbm, field_ref), (velocity_hbm, velocity_ref), (mask_hbm, mask_ref))
    copies = [pltpu.make_async_copy(source, target, done.at[n]) for n, (source, target) in enumerate(pairs)]
    for copy in copies:
        copy.start()
    for copy in copies:
        copy.wait()
    first_half = rows_of() < 4
    keep = [mask_ref[x].astype(F32) for x in range(2)]
    for group, ref in ((MIDDLE, middle_ref), (PLUS, plus_ref), (MINUS, minus_ref)):
        for n, c in enumerate(group):
            for x in range(2):
                for s in range(SPECIES):
                    row = 4 * x + s
                    ref[n, row : row + 1, :] = field_ref[s, INDEX[c], x]
                ref[n, 4 * x + 3 : 4 * x + 4, :] = keep[x]
    even = is_even("space")
    for n in range(5):
        plus, minus = (plus_ref[n], minus_ref[n])
        near_ref[n] = jnp.where(even, minus, plus)
        far_ref[n] = jnp.where(even, plus, minus)
    fixed_ref[0] = per_species(relaxation_ref)
    fixed_ref[1] = per_species(uptake_ref)
    fixed_ref[2] = jnp.where(first_half, keep[0], keep[1])
    for c in range(3):
        speeds = velocity_ref[c, 0].astype(F32)
        fixed_ref[3 + c] = jnp.where(first_half, speeds[0:1], speeds[1:2])


def slots_kernel(cells_hbm, load_hbm, slots_ref, cells_ref, load_ref, done):
    pairs = ((cells_hbm, cells_ref), (load_hbm, load_ref))
    copies = [pltpu.make_async_copy(source, target, done.at[n]) for n, (source, target) in enumerate(pairs)]
    for copy in copies:
        copy.start()
    for copy in copies:
        copy.wait()
    rows = rows_of()
    for q in range(slots_ref.shape[0]):
        load = load_ref[0, 0, q]
        cells = cells_ref[0, 0, q].astype(F32)
        live = [jnp.where(k < load, cells[k : k + 1], -1.0) for k in range(4)]
        for n in range(2):
            slots_ref[q, 8 * n : 8 * n + 8, :] = jnp.where(
                rows == 3, live[2 * n], jnp.where(rows == 7, live[2 * n + 1], 0.0)
            )


def across_kernel(middle_ref, near_ref, far_ref, first_ref, second_ref, one_ref, two_ref):
    has_right, has_left, _, _ = edges()
    even = is_even("space")
    even_row = is_even("work")
    pieces = {}
    for sign in (1, -1):
        p, m = (PLACE[(1, sign, 0)], PLACE[(-1, sign, 0)])
        pieces[sign] = [middle_ref[PLACE[(0, sign, cz)]] for cz in (0, 1, -1)] + [
            jnp.where(even, far_ref[p], near_ref[p]),
            jnp.where(has_right, jnp.where(even, first_ref[p], second_ref[p]), 0.0),
            jnp.where(even, near_ref[m], far_ref[m]),
            jnp.where(has_left, jnp.where(even, second_ref[m], first_ref[m]), 0.0),
        ]
    for n in range(7):
        one_ref[n] = jnp.where(even_row, pieces[-1][n], pieces[1][n])
        two_ref[n] = jnp.where(even_row, pieces[1][n], pieces[-1][n])


def write_payload(payload_ref, density, slots_ref):
    live = rows_of() % 4 < SPECIES
    high = density.astype(BF16).astype(F32)
    both = jnp.concatenate([jnp.where(live, high, 0.0), jnp.where(live, density - high, 0.0)], axis=0)
    for q in range(payload_ref.shape[0]):
        payload_ref[q] = (both + slots_ref[q]).astype(BF16)


def first_kernel(
    middle_ref, near_ref, far_ref, first_ref, second_ref, one_ref, two_ref, fixed_ref, slots_ref,
    stay_ref, third_ref, fourth_ref, gain_ref, payload_ref,
):
    has_right, has_left, has_above, has_below = edges()
    even = is_even("space")
    even_row = is_even("work")
    first_half = rows_of() < 4
    rate = fixed_ref[0]
    keep = fixed_ref[2]
    plus = [jnp.where(even, far_ref[n], near_ref[n]) for n in range(3)]
    minus = [jnp.where(even, near_ref[n], far_ref[n]) for n in range(3)]
    right = [jnp.where(has_right, jnp.where(even, first_ref[n], second_ref[n]), 0.0) for n in range(3)]
    left = [jnp.where(has_left, jnp.where(even, second_ref[n], first_ref[n]), 0.0) for n in range(3)]
    above = [jnp.where(has_above, jnp.where(even_row, one_ref[n], two_ref[n]), 0.0) for n in range(7)]
    below = [jnp.where(has_below, jnp.where(even_row, two_ref[n], one_ref[n]), 0.0) for n in range(7)]
    pulled = {}
    for n, cz in enumerate((0, 1, -1)):
        pulled[(0, 0, cz)] = along(middle_ref[PLACE[(0, 0, cz)]], cz)
        pulled[(1, 0, cz)] = along(jnp.where(first_half, half(plus[n]), half(right[n])), cz)
        pulled[(-1, 0, cz)] = along(jnp.where(first_half, half(left[n]), half(minus[n])), cz)
    for sign, side in ((1, above), (-1, below)):
        for n, cz in enumerate((0, 1, -1)):
            pulled[(0, sign, cz)] = along(side[n], cz)
        pulled[(1, sign, 0)] = jnp.where(first_half, half(side[3]), half(side[4]))
        pulled[(-1, sign, 0)] = jnp.where(first_half, half(side[6]), half(side[5]))
    pulled = {c: pulled[c] for c in DIRECTIONS}
    density = moment(pulled, [fixed_ref[3 + c] for c in range(3)])
    write_payload(payload_ref, density, slots_ref)

    kept = 1.0 - rate
    right_mask = jnp.where(first_half, keep[4:5], right[0][3:4])
    left_mask = jnp.where(first_half, left[0][7:8], keep[0:1])
    here, to_right, to_left = (keep * kept, right_mask * kept, left_mask * kept)
    for n, cz in enumerate((0, 1, -1)):
        stay_ref[n] = here * pulled[(0, 0, cz)]
        stay_ref[3 + n] = to_right * along(right[n], cz)
        stay_ref[6 + n] = to_left * along(left[n], cz)
    sends = {}
    for sign, side in ((1, above), (-1, below)):
        sends[sign] = [here * pulled[(0, sign, cz)] for cz in (0, 1, -1)] + [to_right * side[4], to_left * side[6]]
    for n in range(5):
        third_ref[n] = jnp.where(even_row, sends[-1][n], sends[1][n])
        fourth_ref[n] = jnp.where(even_row, sends[1][n], sends[-1][n])
    gain_ref[0] = jnp.where(first_half, below[0][3:4], below[0][7:8]) * rate
    gain_ref[1] = keep * rate
    gain_ref[2] = jnp.where(first_half, above[0][3:4], above[0][7:8]) * rate
    gain_ref[3] = density


def owner_kernel(incoming_ref, response_ref, out_ref, matrices_ref, picked_ref, reply_ref, sums_ref, done, *, fold):
    count = incoming_ref.shape[0]
    each = count // CHUNKS
    copies = [
        pltpu.make_async_copy(
            response_ref.at[pl.ds(n * each, each)], matrices_ref.at[pl.ds(n * each, each)], done.at[n]
        )
        for n in range(CHUNKS)
    ]
    for copy in copies:
        copy.start()
    column = jnp.where(rows_of() < 4, 0, 1)
    cell_rows = lax.broadcasted_iota(jnp.int32, (LANES, LANES), 0)
    contract = (((1,), (1,)), ((), ()))
    zero = jnp.zeros((8, LANES), F32)
    slot_rows = (3, 7, 11, 15)
    for b in range(count):
        tiles = incoming_ref[b].astype(F32)
        top = tiles[0:8]
        picked = []
        for row in slot_rows:
            cell = jnp.broadcast_to(tiles[row : row + 1].astype(jnp.int32), (8, LANES))
            found = jnp.take_along_axis(top, cell & (LANES - 1), axis=1, mode="promise_in_bounds")
            picked.append(jnp.where((cell >> 7) == column, found, half(found)))
        upper = jnp.concatenate([picked[0], zero, picked[2], zero], axis=0)
        lower = jnp.concatenate([zero, picked[1], zero, picked[3]], axis=0)
        picked_ref[b] = jnp.concatenate([upper, lower], axis=1).astype(BF16)
    for n in range(CHUNKS):
        copies[n].wait()
        for b in range(n * each, (n + 1) * each):
            top = jnp.concatenate([matrices_ref[b, 0], matrices_ref[b, 1]], axis=1)
            bottom = jnp.concatenate([matrices_ref[b, 2], matrices_ref[b, 3]], axis=1)
            grid = jnp.concatenate([top, bottom], axis=0)
            reply = lax.dot_general(picked_ref[b], grid, contract, preferred_element_type=F32)
            reply_ref[b] = jnp.concatenate([reply[0:16, 0:LANES], reply[16:32, LANES:]], axis=0)
    for b in range(count):
        tiles = incoming_ref[b].astype(F32)
        lefts = []
        rights = []
        for k, row in enumerate(slot_rows):
            cell = tiles[row : row + 1].astype(jnp.int32)
            mine = jnp.broadcast_to(cell >> 7, (8, LANES)) == column
            reply = jnp.where(mine, reply_ref[b, 8 * k : 8 * k + 8, :], 0.0)
            high = reply.astype(BF16).astype(F32)
            lefts.append(jnp.concatenate([high, reply - high], axis=0).astype(BF16))
            rights.append(jnp.where(cell_rows == (cell & (LANES - 1)), 1.0, 0.0).astype(BF16))
        both = lax.dot_general(
            jnp.concatenate(lefts, axis=1), jnp.concatenate(rights, axis=1), contract, preferred_element_type=F32
        )
        total = both[0:8] + both[8:16]
        high = total.astype(BF16).astype(F32)
        out_ref[b, 0:16, :] = jnp.concatenate([high, total - high], axis=0).astype(BF16)
        if fold:
            sums_ref[b] = total
    if fold:
        for b in range(count):
            before = sums_ref[b - 1] if b > 0 else zero
            after = sums_ref[b + 1] if b < count - 1 else zero
            out_ref[b, 16:32, :] = jnp.concatenate([before, after], axis=0).astype(BF16)


def total_of(returned_ref, rows):
    total = returned_ref[0, 0:rows, :].astype(F32)
    for q in range(1, returned_ref.shape[0]):
        total = total + returned_ref[q, 0:rows, :].astype(F32)
    return total


def gather_kernel(returned_ref, incoming_ref, gain_ref, fixed_ref, parts_ref, near_ref, far_ref):
    first_half = rows_of() < 4
    factor = fixed_ref[1]
    total = total_of(returned_ref, 32)
    sources = (total[16:24], total[0:8] + total[8:16], total[24:32])
    b = lax.axis_index("work")
    last = lax.axis_size("work") - 1
    even = is_even("space")
    for n, source in enumerate(sources):
        source = factor * source
        if n == 1:
            density = gain_ref[3]
        else:
            tiles = incoming_ref[jnp.clip(b + n - 1, 0, last)].astype(F32)
            density = tiles[0:8] + tiles[8:16]
        equilibrium = gain_ref[n] * density
        parts_ref[n] = equilibrium
        parts_ref[3 + n] = source
        to_lower = jnp.where(first_half, equilibrium, half(source))
        to_upper = jnp.where(first_half, half(equilibrium), source)
        near_ref[n] = jnp.where(even, to_upper, to_lower)
        far_ref[n] = jnp.where(even, to_lower, to_upper)


def second_kernel(
    stay_ref, third_ref, fourth_ref, parts_ref, first_ref, second_ref, fixed_ref, slots_ref,
    pulled_ref, density_ref, payload_ref,
):
    has_right, has_left, has_above, has_below = edges()
    even = is_even("space")
    even_row = is_even("work")
    first_half = rows_of() < 4
    above = [jnp.where(has_above, jnp.where(even_row, third_ref[n], fourth_ref[n]), 0.0) for n in range(5)]
    below = [jnp.where(has_below, jnp.where(even_row, fourth_ref[n], third_ref[n]), 0.0) for n in range(5)]
    pulled = {}
    for n, cy in enumerate((-1, 0, 1)):
        equilibrium, source = (parts_ref[n], parts_ref[3 + n])
        right = jnp.where(has_right, jnp.where(even, first_ref[n], second_ref[n]), 0.0)
        left = jnp.where(has_left, jnp.where(even, second_ref[n], first_ref[n]), 0.0)
        moved = {
            0: (equilibrium, source),
            1: (jnp.where(first_half, half(equilibrium), half(right)), jnp.where(first_half, half(source), right)),
            -1: (jnp.where(first_half, left, half(equilibrium)), jnp.where(first_half, half(left), half(source))),
        }
        for c in DIRECTIONS:
            if c[1] != cy:
                continue
            shifted, added = moved[c[0]]
            if cy == 0:
                base = stay_ref[{0: 0, 1: 3, -1: 6}[c[0]] + {0: 0, 1: 1, -1: 2}[c[2]]]
            else:
                side = above if cy > 0 else below
                base = side[{0: {0: 0, 1: 1, -1: 2}[c[2]], 1: 3, -1: 4}[c[0]]]
            pulled[c] = along(base + shifted + WEIGHTS[INDEX[c]] * added, c[2])
    pulled = {c: pulled[c] for c in DIRECTIONS}
    density = moment(pulled, [fixed_ref[3 + c] for c in range(3)])
    write_payload(payload_ref, density, slots_ref)
    for i, c in enumerate(DIRECTIONS):
        pulled_ref[i] = pulled[c]
    density_ref[0] = density


def last_kernel(returned_ref, pulled_ref, density_ref, fixed_ref, out_ref):
    total = total_of(returned_ref, 16)
    rate = fixed_ref[0]
    keep = fixed_ref[2]
    source = fixed_ref[1] * (total[0:8] + total[8:16])
    shared = keep * rate * density_ref[0]
    here = keep * (1.0 - rate)
    for i in range(len(DIRECTIONS)):
        value = here * pulled_ref[i] + shared + WEIGHTS[i] * source
        for x in range(2):
            for s in range(SPECIES):
                row = 4 * x + s
                out_ref[s, i, x] = value[row : row + 1]


def call(kernel, out_shape, in_specs, name, **rest):
    single = not isinstance(out_shape, (tuple, list))
    return pl.pallas_call(
        kernel,
        out_shape=out_shape,
        in_specs=in_specs,
        out_specs=VM if single else tuple(VM for _ in out_shape),
        name=name,
        compiler_params=pltpu.CompilerParams(vmem_limit_bytes=32 * 1024 * 1024),
        **rest,
    )


def swapped(value, axis, odd):
    count = lax.axis_size(axis)
    step = [(1 if (i % 2 == 0) != odd else -1) for i in range(count)]
    return lax.ppermute(value, axis, [(i, (i + step[i]) % count) for i in range(count)])


def body(adjoint, velocity, relaxation, uptake, fluid_mask, block_cells, owner_load, response):
    owners = lax.axis_size("work")
    matrices = response.reshape(response.shape[2:])
    speeds = velocity.transpose(0, 2, 1, 3)

    def both_ways(near, far, axis):
        return swapped(near, axis, False), swapped(far, axis, True)

    def owner(incoming, fold):
        return call(
            lambda *refs: owner_kernel(*refs, fold=fold),
            jax.ShapeDtypeStruct((owners, 32 if fold else 16, LANES), BF16),
            [VM, HBM],
            "owner_fold" if fold else "owner",
            scratch_shapes=[
                pltpu.VMEM(matrices.shape, BF16),
                pltpu.VMEM((owners, 32, 2 * LANES), BF16),
                pltpu.VMEM((owners, 32, LANES), F32),
                pltpu.VMEM((owners, 8, LANES), F32),
                pltpu.SemaphoreType.DMA((CHUNKS,)),
            ],
        )(incoming, matrices)

    def exchange(value):
        return lax.all_to_all(value, "work", split_axis=0, concat_axis=0, tiled=True)

    payload_shape = jax.ShapeDtypeStruct((owners, 16, LANES), BF16)
    middle, near, far, fixed = call(
        arrange_kernel,
        (tile(9), tile(5), tile(5), tile(6)),
        [HBM] * 3 + [SM] * 2,
        "arrange",
        scratch_shapes=[
            pltpu.VMEM(adjoint.shape, F32),
            pltpu.VMEM(speeds.shape, BF16),
            pltpu.VMEM(fluid_mask.shape, jnp.int32),
            pltpu.VMEM((5, 8, LANES), F32),
            pltpu.VMEM((5, 8, LANES), F32),
            pltpu.SemaphoreType.DMA((3,)),
        ],
    )(adjoint, speeds, fluid_mask, relaxation, uptake)
    first, second = both_ways(near, far, "space")
    slots = call(
        slots_kernel,
        tile(owners, rows=16),
        [HBM] * 2,
        "slots",
        scratch_shapes=[
            pltpu.VMEM(block_cells.shape, jnp.int32),
            pltpu.SMEM(owner_load.shape, jnp.int32),
            pltpu.SemaphoreType.DMA((2,)),
        ],
    )(block_cells, owner_load)
    one, two = call(across_kernel, (tile(7), tile(7)), [VM] * 5, "across")(middle, near, far, first, second)
    one, two = both_ways(one, two, "work")
    stay, third, fourth, gain, payload = call(
        first_kernel, (tile(9), tile(5), tile(5), tile(4), payload_shape), [VM] * 9, "first"
    )(middle, near, far, first, second, one, two, fixed, slots)
    incoming = exchange(payload)
    third, fourth = both_ways(third, fourth, "work")
    returned = exchange(owner(incoming, True))
    parts, near, far = call(gather_kernel, (tile(6), tile(3), tile(3)), [VM] * 4, "gather")(
        returned, incoming, gain, fixed
    )
    first, second = both_ways(near, far, "space")
    pulled, density, payload = call(
        second_kernel, (tile(19), tile(1), payload_shape), [VM] * 8, "second"
    )(stay, third, fourth, parts, first, second, fixed, slots)
    returned = exchange(owner(exchange(payload), False))
    return call(last_kernel, jax.ShapeDtypeStruct(adjoint.shape, F32), [VM] * 4, "last")(
        returned, pulled, density, fixed
    )


def solution(mesh):
    placed = (
        P(None, None, "space", "work", None),
        P(None, "space", "work", None),
        P(),
        P(),
        P("space", "work", None),
        P("space", "work", None, None, None),
        P("space", "work", None),
        P("space", "work", None, None, None, None),
    )
    return jax.shard_map(
        body,
        mesh=mesh,
        in_specs=placed,
        out_specs=P(None, None, "space", "work", None),
        check_vma=False,
    )
```

time: 110 us -> 99.1 us (0.901)
  waiting for transfers between devices: 24.8 us -> 11.2 us
  Pallas kernels: 17.4 us -> 10.2 us
  starting transfers between devices: 11.2 us -> 17.3 us
  blocking collectives: 45.6 us -> 49.2 us
    ppermute x8, waiting for transfers between devices: 15.8 us -> 3.2 us  [swapped(): lax.ppermute(value, axis, [(i, (i + step[i]) % count) for i in range(coun...]
    pallas_call x2, Pallas kernels: 14.8 us -> 7.73 us  [owner(): call(lambda *refs: owner_kernel(*refs, fold=fold), jax.ShapeDtypeStruct((...]
    ppermute x8, starting transfers between devices: 6.85 us -> 12.9 us  [swapped(): lax.ppermute(value, axis, [(i, (i + step[i]) % count) for i in range(coun...]
    all_to_all x3, blocking collectives: 45.6 us -> 49.2 us  [exchange(): lax.all_to_all(value, 'work', split_axis=0, concat_axis=0, tiled=True)]
    reshape x2 -> x0, local copies, waits for them, and re-layouts: 1.35 us -> none  [the longest x1 0.7 us: body(): speeds = velocity.reshape(-1, LANES)]
    unnamed x26 -> x18, local copies, waits for them, and re-layouts: 8.82 us -> 9.36 us
    pallas_call x4 -> x5, Pallas kernels: 1.92 us -> 2.29 us  [the longest x1 0.73 us: body(): call(slots_kernel, tile(owners, rows=16), [HBM] * 2, 'slots', scratch_sha...]
  transfers between devices with their start and end apart: 9 -> 9, of which waited for: 7 -> 3; matrix products, arithmetic and copies ran while one was open for 1% -> 0% of each run, Pallas kernels for 1% -> 1%
where the time goes in v2:
time: 99.1 us; the launch traced here: 97.4 us
  blocking collectives  49.2 us (50%)
  starting transfers between devices  17.3 us (17%)
  waiting for transfers between devices  11.2 us (11%)
  Pallas kernels  10.2 us (10%)
  local copies, waits for them, and re-layouts  9.36 us (9%)
    all_to_all x3, blocking collectives, exchange(): lax.all_to_all(value, 'work', split_axis=0, concat_axis=0, tiled=True)  49.2 us
    ppermute x8, starting transfers between devices, swapped(): lax.ppermute(value, axis, [(i, (i + step[i]) % count) for i in range(coun...  12.9 us
    unnamed x18, local copies, waits for them, and re-layouts  9.36 us
    all_to_all x1, waiting for transfers between devices, exchange(): lax.all_to_all(value, 'work', split_axis=0, concat_axis=0, tiled=True)  8.05 us
    pallas_call x2, Pallas kernels, owner(): call(lambda *refs: owner_kernel(*refs, fold=fold), jax.ShapeDtypeStruct((...  7.73 us
    all_to_all x1, starting transfers between devices, exchange(): lax.all_to_all(value, 'work', split_axis=0, concat_axis=0, tiled=True)  4.46 us
    ppermute x8, waiting for transfers between devices, swapped(): lax.ppermute(value, axis, [(i, (i + step[i]) % count) for i in range(coun...  3.2 us
  transfers between devices with their start and end apart: 9, of which 3 were waited for; matrix products, arithmetic and copies ran while one was open for 0% of the time, Pallas kernels for 1%

profile of v2, /device:TPU:32, one launch (start us, length us, event | category | flops | bytes accessed | tf_op | source)
XLA Modules:
  0.0 97.4 jit_solution(17361614657261382209)
XLA Ops:
  0.0 0.0 copy-start.3
  0.0 0.8 copy-done.3
  0.8 0.0 copy-start.4
  0.8 0.7 copy-done.4
  1.5 0.0 copy-start.5
  1.5 0.7 copy-done.5
  2.2 0.0 copy-start.6
  2.2 0.7 copy-done.6
  2.8 0.0 copy-start.7
  2.8 0.7 copy-done.7
  3.5 0.7 arrange.1
  4.2 0.1 collective-permute-start
  4.3 2.9 %collective-permute-start.1 = (f32[5,8,128]{2,1,0:T(8,128)S(1)}, f32[5,8,128]{2,1,0:T(8,128)S(1)}, u32[]{:S(2)}, u32[]{:S(2)}) collective-permute-start(f32[5,8,128]{2,1,0:T(8,128)S(1)} %get-tuple-element.24.far_ref), channel_id=1, source_target_pairs={{0,224},{32,64},{64,32},{96,128},{128,96},{160,192},{192,160},{224... | collective-permute-start | bytes 61448 | tf_op jit(solution)/shard_map/ppermute | solution.py:386
  7.2 0.0 collective-permute-done.first_ref
  7.2 1.6 %collective-permute-done.1.second_ref = f32[5,8,128]{2,1,0:T(8,128)S(1)} collective-permute-done((f32[5,8,128]{2,1,0:T(8,128)S(1)}, f32[5,8,128]{2,1,0:T(8,128)S(1)}, u32[]{:S(2)}, u32[]{:S(2)}) %collective-permute-start.1) | collective-permute-done | bytes 20512 | tf_op jit(solution)/shard_map/ppermute | solution.py:386
  8.8 1.9 %collective-permute-start.2 = (f32[7,8,128]{2,1,0:T(8,128)S(1)}, f32[7,8,128]{2,1,0:T(8,128)S(1)}, u32[]{:S(2)}, u32[]{:S(2)}) collective-permute-start(f32[7,8,128]{2,1,0:T(8,128)S(1)} %get-tuple-element.25), channel_id=1, source_target_pairs={{0,1},{1,0},{2,3},{3,2},{4,5},{5,4},{6,7},{7,6},{8,9},{9,8},{10,11... | collective-permute-start | bytes 86024 | tf_op jit(solution)/shard_map/ppermute | solution.py:386
  10.8 2.0 %collective-permute-start.3 = (f32[7,8,128]{2,1,0:T(8,128)S(1)}, f32[7,8,128]{2,1,0:T(8,128)S(1)}, u32[]{:S(2)}, u32[]{:S(2)}) collective-permute-start(f32[7,8,128]{2,1,0:T(8,128)S(1)} %get-tuple-element.26), channel_id=1, source_target_pairs={{0,31},{1,2},{2,1},{3,4},{4,3},{5,6},{6,5},{7,8},{8,7},{9,10},{10,... | collective-permute-start | bytes 86024 | tf_op jit(solution)/shard_map/ppermute | solution.py:386
  12.8 0.0 copy-start.2
  12.8 0.8 copy-done.2
  13.6 0.0 copy-start.8
  13.6 0.7 copy-done.8
  14.3 0.7 slots.1.slots_ref
  15.0 0.0 collective-permute-done.2.one_ref
  15.0 0.0 collective-permute-done.3.two_ref
  15.0 0.1 first.1
  15.1 21.4 %all_to_all.20.refs_0_.incoming_ref = bf16[32,16,128]{2,1,0:T(8,128)(2,1)S(1)} all-to-all(bf16[32,16,128]{2,1,0:T(8,128)(2,1)S(1)} %get-tuple-element.31), channel_id=1, replica_groups=mesh['space'=8,'work'=32] {'work'}, dimensions={0} | all-to-all | bytes 262144 | tf_op jit(solution)/shard_map/all_to_all | solution.py:413
  36.5 0.0 copy-start
  36.6 2.2 %copy-done = bf16[1,1,32,4,128,128]{5,4,3,2,1,0:T(8,128)(2,1)S(1)} copy-done((bf16[1,1,32,4,128,128]{5,4,3,2,1,0:T(8,128)(2,1)S(1)}, bf16[1,1,32,4,128,128]{5,4,3,2,1,0:T(8,128)(2,1)}, u32[]{:S(2)}) %copy-start) | copy-done | bytes 4194328
  38.7 4.2 %owner_fold.1 = bf16[32,32,128]{2,1,0:T(8,128)(2,1)} custom-call(bf16[32,16,128]{2,1,0:T(8,128)(2,1)S(1)} %all_to_all.20.refs_0_.incoming_ref, bf16[32,4,128,128]{3,2,1,0:T(8,128)(2,1)S(1)} %bitcast.2), custom_call_target="tpu_custom_call" | custom-call | tf_op jit(solution)/shard_map/owner_fold/pallas_call | solution.py:398
  43.0 4.5 %all-to-all-start.1 = ((bf16[32,32,128]{2,1,0:T(8,128)(2,1)}), bf16[32,32,128]{2,1,0:T(8,128)(2,1)S(1)}, u32[]{:S(2)}, u32[]{:S(2)}) async-start(bf16[32,32,128]{2,1,0:T(8,128)(2,1)} %owner_fold.1), calls=%async_computation.1 | async-start | bytes 524288 | tf_op jit(solution)/shard_map/all_to_all | solution.py:413
  47.4 0.4 collective-permute-start.4
  47.9 2.6 %collective-permute-start.5 = (f32[5,8,128]{2,1,0:T(8,128)S(1)}, f32[5,8,128]{2,1,0:T(8,128)S(1)}, u32[]{:S(2)}, u32[]{:S(2)}) collective-permute-start(f32[5,8,128]{2,1,0:T(8,128)S(1)} %get-tuple-element.30), channel_id=1, source_target_pairs={{0,31},{1,2},{2,1},{3,4},{4,3},{5,6},{6,5},{7,8},{8,7},{9,10},{10,... | collective-permute-start | bytes 61448 | tf_op jit(solution)/shard_map/ppermute | solution.py:386
  50.5 8.0 %all-to-all-done.1.returned_ref = bf16[32,32,128]{2,1,0:T(8,128)(2,1)S(1)} async-done(((bf16[32,32,128]{2,1,0:T(8,128)(2,1)}), bf16[32,32,128]{2,1,0:T(8,128)(2,1)S(1)}, u32[]{:S(2)}, u32[]{:S(2)}) %all-to-all-start.1) | async-done | bytes 262176 | tf_op jit(solution)/shard_map/all_to_all | solution.py:413
  58.5 0.1 gather.1
  58.6 0.1 collective-permute-start.6
  58.7 2.9 %collective-permute-start.7 = (f32[3,8,128]{2,1,0:T(8,128)S(1)}, f32[3,8,128]{2,1,0:T(8,128)S(1)}, u32[]{:S(2)}, u32[]{:S(2)}) collective-permute-start(f32[3,8,128]{2,1,0:T(8,128)S(1)} %get-tuple-element.35), channel_id=1, source_target_pairs={{0,224},{32,64},{64,32},{96,128},{128,96},{160,192},{192,160},{224... | collective-permute-start | bytes 36872 | tf_op jit(solution)/shard_map/ppermute | solution.py:386
  61.5 0.0 collective-permute-done.4.third_ref
  61.5 0.0 collective-permute-done.5.fourth_ref
  61.5 0.0 collective-permute-done.6.first_ref
  61.5 1.5 %collective-permute-done.7.second_ref = f32[3,8,128]{2,1,0:T(8,128)S(1)} collective-permute-done((f32[3,8,128]{2,1,0:T(8,128)S(1)}, f32[3,8,128]{2,1,0:T(8,128)S(1)}, u32[]{:S(2)}, u32[]{:S(2)}) %collective-permute-start.7) | collective-permute-done | bytes 12320 | tf_op jit(solution)/shard_map/ppermute | solution.py:386
  63.1 0.1 second.1
  63.2 14.1 %all_to_all.21.refs_0_ = bf16[32,16,128]{2,1,0:T(8,128)(2,1)S(1)} all-to-all(bf16[32,16,128]{2,1,0:T(8,128)(2,1)S(1)} %get-tuple-element.36), channel_id=1, replica_groups=mesh['space'=8,'work'=32] {'work'}, dimensions={0} | all-to-all | bytes 262144 | tf_op jit(solution)/shard_map/all_to_all | solution.py:413
  77.3 0.0 copy-start.1
  77.3 2.2 %copy-done.1 = bf16[1,1,32,4,128,128]{5,4,3,2,1,0:T(8,128)(2,1)S(1)} copy-done((bf16[1,1,32,4,128,128]{5,4,3,2,1,0:T(8,128)(2,1)S(1)}, bf16[1,1,32,4,128,128]{5,4,3,2,1,0:T(8,128)(2,1)}, u32[]{:S(2)}) %copy-start.1) | copy-done | bytes 4194328
  79.4 3.5 %owner.1 = bf16[32,16,128]{2,1,0:T(8,128)(2,1)S(1)} custom-call(bf16[32,16,128]{2,1,0:T(8,128)(2,1)S(1)} %all_to_all.21.refs_0_, bf16[32,4,128,128]{3,2,1,0:T(8,128)(2,1)S(1)} %bitcast.3), custom_call_target="tpu_custom_call" | custom-call | tf_op jit(solution)/shard_map/owner/pallas_call | solution.py:398
  83.0 13.8 %all_to_all.22.returned_ref = bf16[32,16,128]{2,1,0:T(8,128)(2,1)S(1)} all-to-all(bf16[32,16,128]{2,1,0:T(8,128)(2,1)S(1)} %owner.1), channel_id=1, replica_groups=mesh['space'=8,'work'=32] {'work'}, dimensions={0} | all-to-all | bytes 262144 | tf_op jit(solution)/shard_map/all_to_all | solution.py:413
  96.7 0.7 last.1
  (1 shorter events, 0.0 us)
Async XLA Ops:
  0.0 0.8 copy-start.3
  0.8 0.7 copy-start.4
  1.5 0.7 copy-start.5
  2.2 0.7 copy-start.6
  2.8 0.7 copy-start.7
  4.2 3.0 %collective-permute-start = (f32[5,8,128]{2,1,0:T(8,128)S(1)}, f32[5,8,128]{2,1,0:T(8,128)S(1)}, u32[]{:S(2)}, u32[]{:S(2)}) collective-permute-start(f32[5,8,128]{2,1,0:T(8,128)S(1)} %get-tuple-element.23.near_ref), channel_id=1, source_target_pairs={{0,32},{32,0},{64,96},{96,64},{128,160},{160,128},{192,224},{224,1... | collective-permute-start | bytes 61448 | tf_op jit(solution)/shard_map/ppermute | solution.py:386
  4.3 4.5 %collective-permute-start.1 = (f32[5,8,128]{2,1,0:T(8,128)S(1)}, f32[5,8,128]{2,1,0:T(8,128)S(1)}, u32[]{:S(2)}, u32[]{:S(2)}) collective-permute-start(f32[5,8,128]{2,1,0:T(8,128)S(1)} %get-tuple-element.24.far_ref), channel_id=1, source_target_pairs={{0,224},{32,64},{64,32},{96,128},{128,96},{160,192},{192,160},{224... | collective-permute-start | bytes 61448 | tf_op jit(solution)/shard_map/ppermute | solution.py:386
  8.8 6.2 %collective-permute-start.2 = (f32[7,8,128]{2,1,0:T(8,128)S(1)}, f32[7,8,128]{2,1,0:T(8,128)S(1)}, u32[]{:S(2)}, u32[]{:S(2)}) collective-permute-start(f32[7,8,128]{2,1,0:T(8,128)S(1)} %get-tuple-element.25), channel_id=1, source_target_pairs={{0,1},{1,0},{2,3},{3,2},{4,5},{5,4},{6,7},{7,6},{8,9},{9,8},{10,11... | collective-permute-start | bytes 86024 | tf_op jit(solution)/shard_map/ppermute | solution.py:386
  10.8 4.2 %collective-permute-start.3 = (f32[7,8,128]{2,1,0:T(8,128)S(1)}, f32[7,8,128]{2,1,0:T(8,128)S(1)}, u32[]{:S(2)}, u32[]{:S(2)}) collective-permute-start(f32[7,8,128]{2,1,0:T(8,128)S(1)} %get-tuple-element.26), channel_id=1, source_target_pairs={{0,31},{1,2},{2,1},{3,4},{4,3},{5,6},{6,5},{7,8},{8,7},{9,10},{10,... | collective-permute-start | bytes 86024 | tf_op jit(solution)/shard_map/ppermute | solution.py:386
  12.8 0.8 copy-start.2
  13.6 0.7 copy-start.8
  36.5 2.2 %copy-start = (bf16[1,1,32,4,128,128]{5,4,3,2,1,0:T(8,128)(2,1)S(1)}, bf16[1,1,32,4,128,128]{5,4,3,2,1,0:T(8,128)(2,1)}, u32[]{:S(2)}) copy-start(bf16[1,1,32,4,128,128]{5,4,3,2,1,0:T(8,128)(2,1)} %param.15) | copy-start | bytes 12582916
  43.0 15.5 %all-to-all-start.1 = ((bf16[32,32,128]{2,1,0:T(8,128)(2,1)}), bf16[32,32,128]{2,1,0:T(8,128)(2,1)S(1)}, u32[]{:S(2)}, u32[]{:S(2)}) async-start(bf16[32,32,128]{2,1,0:T(8,128)(2,1)} %owner_fold.1), calls=%async_computation.1 | async-start | bytes 524288 | tf_op jit(solution)/shard_map/all_to_all | solution.py:413
  47.4 14.1 %collective-permute-start.4 = (f32[5,8,128]{2,1,0:T(8,128)S(1)}, f32[5,8,128]{2,1,0:T(8,128)S(1)}, u32[]{:S(2)}, u32[]{:S(2)}) collective-permute-start(f32[5,8,128]{2,1,0:T(8,128)S(1)} %get-tuple-element.29), channel_id=1, source_target_pairs={{0,1},{1,0},{2,3},{3,2},{4,5},{5,4},{6,7},{7,6},{8,9},{9,8},{10,11... | collective-permute-start | bytes 61448 | tf_op jit(solution)/shard_map/ppermute | solution.py:386
  47.9 13.7 %collective-permute-start.5 = (f32[5,8,128]{2,1,0:T(8,128)S(1)}, f32[5,8,128]{2,1,0:T(8,128)S(1)}, u32[]{:S(2)}, u32[]{:S(2)}) collective-permute-start(f32[5,8,128]{2,1,0:T(8,128)S(1)} %get-tuple-element.30), channel_id=1, source_target_pairs={{0,31},{1,2},{2,1},{3,4},{4,3},{5,6},{6,5},{7,8},{8,7},{9,10},{10,... | collective-permute-start | bytes 61448 | tf_op jit(solution)/shard_map/ppermute | solution.py:386
  58.6 3.0 %collective-permute-start.6 = (f32[3,8,128]{2,1,0:T(8,128)S(1)}, f32[3,8,128]{2,1,0:T(8,128)S(1)}, u32[]{:S(2)}, u32[]{:S(2)}) collective-permute-start(f32[3,8,128]{2,1,0:T(8,128)S(1)} %get-tuple-element.34), channel_id=1, source_target_pairs={{0,32},{32,0},{64,96},{96,64},{128,160},{160,128},{192,224},{224,1... | collective-permute-start | bytes 36872 | tf_op jit(solution)/shard_map/ppermute | solution.py:386
  58.7 4.4 %collective-permute-start.7 = (f32[3,8,128]{2,1,0:T(8,128)S(1)}, f32[3,8,128]{2,1,0:T(8,128)S(1)}, u32[]{:S(2)}, u32[]{:S(2)}) collective-permute-start(f32[3,8,128]{2,1,0:T(8,128)S(1)} %get-tuple-element.35), channel_id=1, source_target_pairs={{0,224},{32,64},{64,32},{96,128},{128,96},{160,192},{192,160},{224... | collective-permute-start | bytes 36872 | tf_op jit(solution)/shard_map/ppermute | solution.py:386
  77.3 2.2 %copy-start.1 = (bf16[1,1,32,4,128,128]{5,4,3,2,1,0:T(8,128)(2,1)S(1)}, bf16[1,1,32,4,128,128]{5,4,3,2,1,0:T(8,128)(2,1)}, u32[]{:S(2)}) copy-start(bf16[1,1,32,4,128,128]{5,4,3,2,1,0:T(8,128)(2,1)} %param.15) | copy-start | bytes 12582916

commit v3 on v2

--- a/solution.py
+++ b/solution.py
@@ -96,11 +96,17 @@
 
 
 def arrange_kernel(
-    field_hbm, velocity_hbm, mask_hbm, relaxation_ref, uptake_ref,
+    field_hbm, velocity_hbm, mask_hbm, relaxation_hbm, uptake_hbm,
     middle_ref, near_ref, far_ref, fixed_ref,
-    field_ref, velocity_ref, mask_ref, plus_ref, minus_ref, done,
+    field_ref, velocity_ref, mask_ref, relaxation_ref, uptake_ref, plus_ref, minus_ref, done,
 ):
-    pairs = ((field_hbm, field_ref), (velocity_hbm, velocity_ref), (mask_hbm, mask_ref))
+    pairs = (
+        (field_hbm, field_ref),
+        (velocity_hbm, velocity_ref),
+        (mask_hbm, mask_ref),
+        (relaxation_hbm, relaxation_ref),
+        (uptake_hbm, uptake_ref),
+    )
     copies = [pltpu.make_async_copy(source, target, done.at[n]) for n, (source, target) in enumerate(pairs)]
     for copy in copies:
         copy.start()
@@ -128,6 +134,39 @@
         fixed_ref[3 + c] = jnp.where(first_half, speeds[0:1], speeds[1:2])
 
 
+def start_fetch(response_hbm, response_ref, done):
+    parts = done.shape[0]
+    each = response_hbm.shape[0] // parts
+    copies = [
+        pltpu.make_async_copy(
+            response_hbm.at[pl.ds(n * each, each)], response_ref.at[pl.ds(n * each, each)], done.at[n]
+        )
+        for n in range(parts)
+    ]
+    for copy in copies:
+        copy.start()
+    return copies
+
+
+def fetch_kernel(response_hbm, middle_ref, response_ref, sides_ref, done):
+    copies = start_fetch(response_hbm, response_ref, done)
+    sides_ref[...] = middle_ref[3:9]
+    for copy in copies:
+        copy.wait()
+
+
+def fetch_again_kernel(response_hbm, third_ref, fourth_ref, response_ref, sides_ref, done):
+    copies = start_fetch(response_hbm, response_ref, done)
+    _, _, has_above, has_below = edges()
+    even_row = is_even("work")
+    for n in range(5):
+        third, fourth = (third_ref[n], fourth_ref[n])
+        sides_ref[n] = jnp.where(has_above, jnp.where(even_row, third, fourth), 0.0)
+        sides_ref[5 + n] = jnp.where(has_below, jnp.where(even_row, fourth, third), 0.0)
+    for copy in copies:
+        copy.wait()
+
+
 def slots_kernel(cells_hbm, load_hbm, slots_ref, cells_ref, load_ref, done):
     pairs = ((cells_hbm, cells_ref), (load_hbm, load_ref))
     copies = [pltpu.make_async_copy(source, target, done.at[n]) for n, (source, target) in enumerate(pairs)]
@@ -146,14 +185,14 @@
             )
 
 
-def across_kernel(middle_ref, near_ref, far_ref, first_ref, second_ref, one_ref, two_ref):
+def across_kernel(sides_ref, near_ref, far_ref, first_ref, second_ref, one_ref, two_ref):
     has_right, has_left, _, _ = edges()
     even = is_even("space")
     even_row = is_even("work")
     pieces = {}
     for sign in (1, -1):
         p, m = (PLACE[(1, sign, 0)], PLACE[(-1, sign, 0)])
-        pieces[sign] = [middle_ref[PLACE[(0, sign, cz)]] for cz in (0, 1, -1)] + [
+        pieces[sign] = [sides_ref[PLACE[(0, sign, cz)] - 3] for cz in (0, 1, -1)] + [
             jnp.where(even, far_ref[p], near_ref[p]),
             jnp.where(has_right, jnp.where(even, first_ref[p], second_ref[p]), 0.0),
             jnp.where(even, near_ref[m], far_ref[m]),
@@ -222,17 +261,8 @@
     gain_ref[3] = density
 
 
-def owner_kernel(incoming_ref, response_ref, out_ref, matrices_ref, picked_ref, reply_ref, sums_ref, done, *, fold):
+def owner_kernel(incoming_ref, matrices_ref, out_ref, picked_ref, reply_ref, sums_ref, *, fold):
     count = incoming_ref.shape[0]
-    each = count // CHUNKS
-    copies = [
-        pltpu.make_async_copy(
-            response_ref.at[pl.ds(n * each, each)], matrices_ref.at[pl.ds(n * each, each)], done.at[n]
-        )
-        for n in range(CHUNKS)
-    ]
-    for copy in copies:
-        copy.start()
     column = jnp.where(rows_of() < 4, 0, 1)
     cell_rows = lax.broadcasted_iota(jnp.int32, (LANES, LANES), 0)
     contract = (((1,), (1,)), ((), ()))
@@ -249,15 +279,15 @@
         upper = jnp.concatenate([picked[0], zero, picked[2], zero], axis=0)
         lower = jnp.concatenate([zero, picked[1], zero, picked[3]], axis=0)
         picked_ref[b] = jnp.concatenate([upper, lower], axis=1).astype(BF16)
-    for n in range(CHUNKS):
-        copies[n].wait()
-        for b in range(n * each, (n + 1) * each):
-            top = jnp.concatenate([matrices_ref[b, 0], matrices_ref[b, 1]], axis=1)
-            bottom = jnp.concatenate([matrices_ref[b, 2], matrices_ref[b, 3]], axis=1)
-            grid = jnp.concatenate([top, bottom], axis=0)
-            reply = lax.dot_general(picked_ref[b], grid, contract, preferred_element_type=F32)
-            reply_ref[b] = jnp.concatenate([reply[0:16, 0:LANES], reply[16:32, LANES:]], axis=0)
-    for b in range(count):
+
+    def respond(b):
+        top = jnp.concatenate([matrices_ref[b, 0], matrices_ref[b, 1]], axis=1)
+        bottom = jnp.concatenate([matrices_ref[b, 2], matrices_ref[b, 3]], axis=1)
+        grid = jnp.concatenate([top, bottom], axis=0)
+        reply = lax.dot_general(picked_ref[b], grid, contract, preferred_element_type=F32)
+        reply_ref[b] = jnp.concatenate([reply[0:16, 0:LANES], reply[16:32, LANES:]], axis=0)
+
+    def spread(b):
         tiles = incoming_ref[b].astype(F32)
         lefts = []
         rights = []
@@ -276,6 +306,11 @@
         out_ref[b, 0:16, :] = jnp.concatenate([high, total - high], axis=0).astype(BF16)
         if fold:
             sums_ref[b] = total
+
+    for b in range(count):
+        respond(b)
+    for b in range(count):
+        spread(b)
     if fold:
         for b in range(count):
             before = sums_ref[b - 1] if b > 0 else zero
@@ -315,15 +350,14 @@
 
 
 def second_kernel(
-    stay_ref, third_ref, fourth_ref, parts_ref, first_ref, second_ref, fixed_ref, slots_ref,
+    stay_ref, sides_ref, parts_ref, first_ref, second_ref, fixed_ref, slots_ref,
     pulled_ref, density_ref, payload_ref,
 ):
-    has_right, has_left, has_above, has_below = edges()
+    has_right, has_left, _, _ = edges()
     even = is_even("space")
-    even_row = is_even("work")
     first_half = rows_of() < 4
-    above = [jnp.where(has_above, jnp.where(even_row, third_ref[n], fourth_ref[n]), 0.0) for n in range(5)]
-    below = [jnp.where(has_below, jnp.where(even_row, fourth_ref[n], third_ref[n]), 0.0) for n in range(5)]
+    above = [sides_ref[n] for n in range(5)]
+    below = [sides_ref[5 + n] for n in range(5)]
     pulled = {}
     for n, cy in enumerate((-1, 0, 1)):
         equilibrium, source = (parts_ref[n], parts_ref[3 + n])
@@ -391,23 +425,24 @@
     matrices = response.reshape(response.shape[2:])
     speeds = velocity.transpose(0, 2, 1, 3)
 
+    def outside(value):
+        return pltpu.with_memory_space_constraint(value, pltpu.HBM)
+
     def both_ways(near, far, axis):
         return swapped(near, axis, False), swapped(far, axis, True)
 
-    def owner(incoming, fold):
+    def owner(incoming, fetched, fold):
         return call(
             lambda *refs: owner_kernel(*refs, fold=fold),
             jax.ShapeDtypeStruct((owners, 32 if fold else 16, LANES), BF16),
-            [VM, HBM],
+            [VM, VM],
             "owner_fold" if fold else "owner",
             scratch_shapes=[
-                pltpu.VMEM(matrices.shape, BF16),
                 pltpu.VMEM((owners, 32, 2 * LANES), BF16),
                 pltpu.VMEM((owners, 32, LANES), F32),
                 pltpu.VMEM((owners, 8, LANES), F32),
-                pltpu.SemaphoreType.DMA((CHUNKS,)),
             ],
-        )(incoming, matrices)
+        )(incoming, fetched)
 
     def exchange(value):
         return lax.all_to_all(value, "work", split_axis=0, concat_axis=0, tiled=True)
@@ -416,17 +451,19 @@
     middle, near, far, fixed = call(
         arrange_kernel,
         (tile(9), tile(5), tile(5), tile(6)),
-        [HBM] * 3 + [SM] * 2,
+        [HBM] * 5,
         "arrange",
         scratch_shapes=[
             pltpu.VMEM(adjoint.shape, F32),
             pltpu.VMEM(speeds.shape, BF16),
             pltpu.VMEM(fluid_mask.shape, jnp.int32),
+            pltpu.SMEM(relaxation.shape, F32),
+            pltpu.SMEM(uptake.shape, F32),
             pltpu.VMEM((5, 8, LANES), F32),
             pltpu.VMEM((5, 8, LANES), F32),
-            pltpu.SemaphoreType.DMA((3,)),
+            pltpu.SemaphoreType.DMA((5,)),
         ],
-    )(adjoint, speeds, fluid_mask, relaxation, uptake)
+    )(*map(outside, (adjoint, speeds, fluid_mask, relaxation, uptake)))
     first, second = both_ways(near, far, "space")
     slots = call(
         slots_kernel,
@@ -438,23 +475,37 @@
             pltpu.SMEM(owner_load.shape, jnp.int32),
             pltpu.SemaphoreType.DMA((2,)),
         ],
-    )(block_cells, owner_load)
-    one, two = call(across_kernel, (tile(7), tile(7)), [VM] * 5, "across")(middle, near, far, first, second)
+    )(*map(outside, (block_cells, owner_load)))
+    fetched, sides = call(
+        fetch_kernel,
+        (pltpu.VMEM(matrices.shape, BF16), tile(6)),
+        [HBM, VM],
+        "fetch",
+        scratch_shapes=[pltpu.SemaphoreType.DMA((CHUNKS,))],
+    )(outside(matrices), middle)
+    one, two = call(across_kernel, (tile(7), tile(7)), [VM] * 5, "across")(sides, near, far, first, second)
     one, two = both_ways(one, two, "work")
     stay, third, fourth, gain, payload = call(
         first_kernel, (tile(9), tile(5), tile(5), tile(4), payload_shape), [VM] * 9, "first"
     )(middle, near, far, first, second, one, two, fixed, slots)
     incoming = exchange(payload)
     third, fourth = both_ways(third, fourth, "work")
-    returned = exchange(owner(incoming, True))
+    returned = exchange(owner(incoming, fetched, True))
     parts, near, far = call(gather_kernel, (tile(6), tile(3), tile(3)), [VM] * 4, "gather")(
         returned, incoming, gain, fixed
     )
     first, second = both_ways(near, far, "space")
+    fetched, sides = call(
+        fetch_again_kernel,
+        (pltpu.VMEM(matrices.shape, BF16), tile(10)),
+        [HBM, VM, VM],
+        "fetch_again",
+        scratch_shapes=[pltpu.SemaphoreType.DMA((CHUNKS,))],
+    )(outside(matrices), third, fourth)
     pulled, density, payload = call(
-        second_kernel, (tile(19), tile(1), payload_shape), [VM] * 8, "second"
-    )(stay, third, fourth, parts, first, second, fixed, slots)
-    returned = exchange(owner(exchange(payload), False))
+        second_kernel, (tile(19), tile(1), payload_shape), [VM] * 7, "second"
+    )(stay, sides, parts, first, second, fixed, slots)
+    returned = exchange(owner(exchange(payload), fetched, False))
     return call(last_kernel, jax.ShapeDtypeStruct(adjoint.shape, F32), [VM] * 4, "last")(
         returned, pulled, density, fixed
     )

time: 99.1 us -> 89 us (0.90)
  local copies, waits for them, and re-layouts: 9.36 us -> 0 us
  Pallas kernels: 10.2 us -> 12.8 us
  waiting for transfers between devices: 11.2 us -> 8.99 us
    unnamed x18 -> x0, local copies, waits for them, and re-layouts: 9.36 us -> none
    pallas_call x2 -> x4, Pallas kernels: 0.83 us -> 5.49 us  [the longest x1 2.21 us: body(): call(fetch_again_kernel, (pltpu.VMEM(matrices.shape, BF16), tile(10)), [H...]
    ppermute x8, waiting for transfers between devices: 3.2 us -> 0.86 us  [swapped(): lax.ppermute(value, axis, [(i, (i + step[i]) % count) for i in range(coun...]
    pallas_call x2, Pallas kernels: 7.73 us -> 5.43 us  [owner(): call(lambda *refs: owner_kernel(*refs, fold=fold), jax.ShapeDtypeStruct((...]
  transfers between devices with their start and end apart: 9 -> 9, of which waited for: 3 -> 2; matrix products, arithmetic and copies ran while one was open for 0% -> 0% of each run, Pallas kernels for 1% -> 6%
where the time goes in v3:
time: 89 us; the launch traced here: 88.3 us
  blocking collectives  49.8 us (56%)
  starting transfers between devices  16.6 us (19%)
  Pallas kernels  12.8 us (14%)
  waiting for transfers between devices  8.99 us (10%)
    all_to_all x3, blocking collectives, exchange(): lax.all_to_all(value, 'work', split_axis=0, concat_axis=0, tiled=True)  49.8 us
    ppermute x8, starting transfers between devices, swapped(): lax.ppermute(value, axis, [(i, (i + step[i]) % count) for i in range(coun...  12.2 us
    all_to_all x1, waiting for transfers between devices, exchange(): lax.all_to_all(value, 'work', split_axis=0, concat_axis=0, tiled=True)  8.12 us
    pallas_call x2, Pallas kernels, owner(): call(lambda *refs: owner_kernel(*refs, fold=fold), jax.ShapeDtypeStruct((...  5.43 us
    all_to_all x1, starting transfers between devices, exchange(): lax.all_to_all(value, 'work', split_axis=0, concat_axis=0, tiled=True)  4.39 us
    pallas_call x1, Pallas kernels, body(): call(fetch_again_kernel, (pltpu.VMEM(matrices.shape, BF16), tile(10)), [H...  2.21 us
    pallas_call x1, Pallas kernels, body(): call(fetch_kernel, (pltpu.VMEM(matrices.shape, BF16), tile(6)), [HBM, VM]...  2.21 us
  transfers between devices with their start and end apart: 9, of which 2 were waited for; matrix products, arithmetic and copies ran while one was open for 0% of the time, Pallas kernels for 6%

profile of v3, /device:TPU:32, one launch (start us, length us, event | category | flops | bytes accessed | tf_op | source)
XLA Modules:
  0.0 88.3 jit_solution(14169503724062163232)
XLA Ops:
  0.0 1.0 %arrange.1 = (f32[9,8,128]{2,1,0:T(8,128)S(1)}, f32[5,8,128]{2,1,0:T(8,128)S(1)}, f32[5,8,128]{2,1,0:T(8,128)S(1)}, f32[6,8,128]{2,1,0:T(8,128)S(1)}) custom-call(f32[3,19,2,1,128]{4,3,2,1,0:T(1,128)} %field_hbm.1, bf16[3,1,2,128]{3,2,1,0:T(2,128)(2,1)} %bitcast.4, s32[2,1,128]{2,1,0:T(1,128)} %mask_hbm.1, f32[3]{0:T(128)} %relaxation_hbm.1, f32[3]{0:T(128)} %uptake_hbm.1), custom_call_target="tpu_custom_call" | custom-call | tf_op jit(solution)/shard_map/arrange/pallas_call | solution.py:451
  1.0 0.1 collective-permute-start
  1.1 2.9 %collective-permute-start.1 = (f32[5,8,128]{2,1,0:T(8,128)S(1)}, f32[5,8,128]{2,1,0:T(8,128)S(1)}, u32[]{:S(2)}, u32[]{:S(2)}) collective-permute-start(f32[5,8,128]{2,1,0:T(8,128)S(1)} %get-tuple-element.28.far_ref), channel_id=1, source_target_pairs={{0,224},{32,64},{64,32},{96,128},{128,96},{160,192},{192,160},{224... | collective-permute-start | bytes 61448 | tf_op jit(solution)/shard_map/ppermute | solution.py:420
  3.9 2.2 %fetch.1 = (bf16[32,4,128,128]{3,2,1,0:T(8,128)(2,1)S(1)}, f32[6,8,128]{2,1,0:T(8,128)S(1)}) custom-call(bf16[32,4,128,128]{3,2,1,0:T(8,128)(2,1)} %bitcast.2, f32[9,8,128]{2,1,0:T(8,128)S(1)} %get-tuple-element.26.middle_ref), custom_call_target="tpu_custom_call" | custom-call | tf_op jit(solution)/shard_map/fetch/pallas_call | solution.py:479
  6.1 0.0 collective-permute-done.first_ref
  6.1 0.0 collective-permute-done.1.second_ref
  6.2 1.3 %collective-permute-start.2 = (f32[7,8,128]{2,1,0:T(8,128)S(1)}, f32[7,8,128]{2,1,0:T(8,128)S(1)}, u32[]{:S(2)}, u32[]{:S(2)}) collective-permute-start(f32[7,8,128]{2,1,0:T(8,128)S(1)} %get-tuple-element.30), channel_id=1, source_target_pairs={{0,1},{1,0},{2,3},{3,2},{4,5},{5,4},{6,7},{7,6},{8,9},{9,8},{10,11... | collective-permute-start | bytes 86024 | tf_op jit(solution)/shard_map/ppermute | solution.py:420
  7.5 2.6 %collective-permute-start.3 = (f32[7,8,128]{2,1,0:T(8,128)S(1)}, f32[7,8,128]{2,1,0:T(8,128)S(1)}, u32[]{:S(2)}, u32[]{:S(2)}) collective-permute-start(f32[7,8,128]{2,1,0:T(8,128)S(1)} %get-tuple-element.31), channel_id=1, source_target_pairs={{0,31},{1,2},{2,1},{3,4},{4,3},{5,6},{6,5},{7,8},{8,7},{9,10},{10,... | collective-permute-start | bytes 86024 | tf_op jit(solution)/shard_map/ppermute | solution.py:420
  10.1 1.0 %slots.1.slots_ref = f32[32,16,128]{2,1,0:T(8,128)S(1)} custom-call(s32[1,1,32,4,128]{4,3,2,1,0:T(4,128)} %cells_hbm.1, s32[1,1,32]{2,1,0:T(1,128)} %load_hbm.1), custom_call_target="tpu_custom_call" | custom-call | tf_op jit(solution)/shard_map/slots/pallas_call | solution.py:468
  11.1 0.0 collective-permute-done.2.one_ref
  11.1 0.8 collective-permute-done.3.two_ref
  12.0 0.1 first.1
  12.1 21.8 %all_to_all.20.refs_0_.incoming_ref = bf16[32,16,128]{2,1,0:T(8,128)(2,1)S(1)} all-to-all(bf16[32,16,128]{2,1,0:T(8,128)(2,1)S(1)} %get-tuple-element.37), channel_id=1, replica_groups=mesh['space'=8,'work'=32] {'work'}, dimensions={0} | all-to-all | bytes 262144 | tf_op jit(solution)/shard_map/all_to_all | solution.py:448
  33.9 3.1 %owner_fold.1 = bf16[32,32,128]{2,1,0:T(8,128)(2,1)} custom-call(bf16[32,16,128]{2,1,0:T(8,128)(2,1)S(1)} %all_to_all.20.refs_0_.incoming_ref, bf16[32,4,128,128]{3,2,1,0:T(8,128)(2,1)S(1)} %get-tuple-element.38.refs_1_), custom_call_target="tpu_custom_call" | custom-call | tf_op jit(solution)/shard_map/owner_fold/pallas_call | solution.py:435
  37.0 4.4 %all-to-all-start.1 = ((bf16[32,32,128]{2,1,0:T(8,128)(2,1)}), bf16[32,32,128]{2,1,0:T(8,128)(2,1)S(1)}, u32[]{:S(2)}, u32[]{:S(2)}) async-start(bf16[32,32,128]{2,1,0:T(8,128)(2,1)} %owner_fold.1), calls=%async_computation.1 | async-start | bytes 524288 | tf_op jit(solution)/shard_map/all_to_all | solution.py:448
  41.4 0.4 collective-permute-start.4
  41.8 2.6 %collective-permute-start.5 = (f32[5,8,128]{2,1,0:T(8,128)S(1)}, f32[5,8,128]{2,1,0:T(8,128)S(1)}, u32[]{:S(2)}, u32[]{:S(2)}) collective-permute-start(f32[5,8,128]{2,1,0:T(8,128)S(1)} %get-tuple-element.35), channel_id=1, source_target_pairs={{0,31},{1,2},{2,1},{3,4},{4,3},{5,6},{6,5},{7,8},{8,7},{9,10},{10,... | collective-permute-start | bytes 61448 | tf_op jit(solution)/shard_map/ppermute | solution.py:420
  44.4 8.1 %all-to-all-done.1.returned_ref = bf16[32,32,128]{2,1,0:T(8,128)(2,1)S(1)} async-done(((bf16[32,32,128]{2,1,0:T(8,128)(2,1)}), bf16[32,32,128]{2,1,0:T(8,128)(2,1)S(1)}, u32[]{:S(2)}, u32[]{:S(2)}) %all-to-all-start.1) | async-done | bytes 262176 | tf_op jit(solution)/shard_map/all_to_all | solution.py:448
  52.5 0.1 gather.1
  52.6 0.1 collective-permute-start.6
  52.7 2.2 %collective-permute-start.7 = (f32[3,8,128]{2,1,0:T(8,128)S(1)}, f32[3,8,128]{2,1,0:T(8,128)S(1)}, u32[]{:S(2)}, u32[]{:S(2)}) collective-permute-start(f32[3,8,128]{2,1,0:T(8,128)S(1)} %get-tuple-element.42), channel_id=1, source_target_pairs={{0,224},{32,64},{64,32},{96,128},{128,96},{160,192},{192,160},{224... | collective-permute-start | bytes 36872 | tf_op jit(solution)/shard_map/ppermute | solution.py:420
  54.9 0.0 collective-permute-done.4.third_ref
  54.9 0.0 collective-permute-done.5.fourth_ref
  54.9 2.2 %fetch_again.1 = (bf16[32,4,128,128]{3,2,1,0:T(8,128)(2,1)S(1)}, f32[10,8,128]{2,1,0:T(8,128)S(1)}) custom-call(bf16[32,4,128,128]{3,2,1,0:T(8,128)(2,1)} %bitcast.3, f32[5,8,128]{2,1,0:T(8,128)S(1)} %collective-permute-done.4.third_ref, f32[5,8,128]{2,1,0:T(8,128)S(1)} %collective-permute-done.5.fourth_ref), custom_call_target="tpu_custom_call" | custom-call | tf_op jit(solution)/shard_map/fetch_again/pallas_call | solution.py:498
  57.1 0.0 collective-permute-done.6.first_ref
  57.1 0.0 collective-permute-done.7.second_ref
  57.2 0.1 second.1
  57.3 14.1 %all_to_all.21.refs_0_ = bf16[32,16,128]{2,1,0:T(8,128)(2,1)S(1)} all-to-all(bf16[32,16,128]{2,1,0:T(8,128)(2,1)S(1)} %get-tuple-element.43), channel_id=1, replica_groups=mesh['space'=8,'work'=32] {'work'}, dimensions={0} | all-to-all | bytes 262144 | tf_op jit(solution)/shard_map/all_to_all | solution.py:448
  71.4 2.4 %owner.1 = bf16[32,16,128]{2,1,0:T(8,128)(2,1)S(1)} custom-call(bf16[32,16,128]{2,1,0:T(8,128)(2,1)S(1)} %all_to_all.21.refs_0_, bf16[32,4,128,128]{3,2,1,0:T(8,128)(2,1)S(1)} %get-tuple-element.44.refs_1_), custom_call_target="tpu_custom_call" | custom-call | tf_op jit(solution)/shard_map/owner/pallas_call | solution.py:435
  73.7 13.9 %all_to_all.22.returned_ref = bf16[32,16,128]{2,1,0:T(8,128)(2,1)S(1)} all-to-all(bf16[32,16,128]{2,1,0:T(8,128)(2,1)S(1)} %owner.1), channel_id=1, replica_groups=mesh['space'=8,'work'=32] {'work'}, dimensions={0} | all-to-all | bytes 262144 | tf_op jit(solution)/shard_map/all_to_all | solution.py:448
  87.6 0.7 last.1
  (1 shorter events, 0.0 us)
Async XLA Ops:
  1.0 5.2 %collective-permute-start = (f32[5,8,128]{2,1,0:T(8,128)S(1)}, f32[5,8,128]{2,1,0:T(8,128)S(1)}, u32[]{:S(2)}, u32[]{:S(2)}) collective-permute-start(f32[5,8,128]{2,1,0:T(8,128)S(1)} %get-tuple-element.27.near_ref), channel_id=1, source_target_pairs={{0,32},{32,0},{64,96},{96,64},{128,160},{160,128},{192,224},{224,1... | collective-permute-start | bytes 61448 | tf_op jit(solution)/shard_map/ppermute | solution.py:420
  1.1 5.1 %collective-permute-start.1 = (f32[5,8,128]{2,1,0:T(8,128)S(1)}, f32[5,8,128]{2,1,0:T(8,128)S(1)}, u32[]{:S(2)}, u32[]{:S(2)}) collective-permute-start(f32[5,8,128]{2,1,0:T(8,128)S(1)} %get-tuple-element.28.far_ref), channel_id=1, source_target_pairs={{0,224},{32,64},{64,32},{96,128},{128,96},{160,192},{192,160},{224... | collective-permute-start | bytes 61448 | tf_op jit(solution)/shard_map/ppermute | solution.py:420
  6.2 4.9 %collective-permute-start.2 = (f32[7,8,128]{2,1,0:T(8,128)S(1)}, f32[7,8,128]{2,1,0:T(8,128)S(1)}, u32[]{:S(2)}, u32[]{:S(2)}) collective-permute-start(f32[7,8,128]{2,1,0:T(8,128)S(1)} %get-tuple-element.30), channel_id=1, source_target_pairs={{0,1},{1,0},{2,3},{3,2},{4,5},{5,4},{6,7},{7,6},{8,9},{9,8},{10,11... | collective-permute-start | bytes 86024 | tf_op jit(solution)/shard_map/ppermute | solution.py:420
  7.5 4.4 %collective-permute-start.3 = (f32[7,8,128]{2,1,0:T(8,128)S(1)}, f32[7,8,128]{2,1,0:T(8,128)S(1)}, u32[]{:S(2)}, u32[]{:S(2)}) collective-permute-start(f32[7,8,128]{2,1,0:T(8,128)S(1)} %get-tuple-element.31), channel_id=1, source_target_pairs={{0,31},{1,2},{2,1},{3,4},{4,3},{5,6},{6,5},{7,8},{8,7},{9,10},{10,... | collective-permute-start | bytes 86024 | tf_op jit(solution)/shard_map/ppermute | solution.py:420
  37.0 15.5 %all-to-all-start.1 = ((bf16[32,32,128]{2,1,0:T(8,128)(2,1)}), bf16[32,32,128]{2,1,0:T(8,128)(2,1)S(1)}, u32[]{:S(2)}, u32[]{:S(2)}) async-start(bf16[32,32,128]{2,1,0:T(8,128)(2,1)} %owner_fold.1), calls=%async_computation.1 | async-start | bytes 524288 | tf_op jit(solution)/shard_map/all_to_all | solution.py:448
  41.4 13.5 %collective-permute-start.4 = (f32[5,8,128]{2,1,0:T(8,128)S(1)}, f32[5,8,128]{2,1,0:T(8,128)S(1)}, u32[]{:S(2)}, u32[]{:S(2)}) collective-permute-start(f32[5,8,128]{2,1,0:T(8,128)S(1)} %get-tuple-element.34), channel_id=1, source_target_pairs={{0,1},{1,0},{2,3},{3,2},{4,5},{5,4},{6,7},{7,6},{8,9},{9,8},{10,11... | collective-permute-start | bytes 61448 | tf_op jit(solution)/shard_map/ppermute | solution.py:420
  41.8 13.1 %collective-permute-start.5 = (f32[5,8,128]{2,1,0:T(8,128)S(1)}, f32[5,8,128]{2,1,0:T(8,128)S(1)}, u32[]{:S(2)}, u32[]{:S(2)}) collective-permute-start(f32[5,8,128]{2,1,0:T(8,128)S(1)} %get-tuple-element.35), channel_id=1, source_target_pairs={{0,31},{1,2},{2,1},{3,4},{4,3},{5,6},{6,5},{7,8},{8,7},{9,10},{10,... | collective-permute-start | bytes 61448 | tf_op jit(solution)/shard_map/ppermute | solution.py:420
  52.6 4.6 %collective-permute-start.6 = (f32[3,8,128]{2,1,0:T(8,128)S(1)}, f32[3,8,128]{2,1,0:T(8,128)S(1)}, u32[]{:S(2)}, u32[]{:S(2)}) collective-permute-start(f32[3,8,128]{2,1,0:T(8,128)S(1)} %get-tuple-element.41), channel_id=1, source_target_pairs={{0,32},{32,0},{64,96},{96,64},{128,160},{160,128},{192,224},{224,1... | collective-permute-start | bytes 36872 | tf_op jit(solution)/shard_map/ppermute | solution.py:420
  52.7 4.5 %collective-permute-start.7 = (f32[3,8,128]{2,1,0:T(8,128)S(1)}, f32[3,8,128]{2,1,0:T(8,128)S(1)}, u32[]{:S(2)}, u32[]{:S(2)}) collective-permute-start(f32[3,8,128]{2,1,0:T(8,128)S(1)} %get-tuple-element.42), channel_id=1, source_target_pairs={{0,224},{32,64},{64,32},{96,128},{128,96},{160,192},{192,160},{224... | collective-permute-start | bytes 36872 | tf_op jit(solution)/shard_map/ppermute | solution.py:420

commit v4 on v3

--- a/solution.py
+++ b/solution.py
@@ -91,8 +91,8 @@
     return (a < lax.axis_size("space") - 1, a > 0, b < lax.axis_size("work") - 1, b > 0)
 
 
-def is_even(axis):
-    return lax.axis_index(axis) % 2 == 0
+def near_is_upper(axis):
+    return lax.axis_index(axis) % 2 == 1
 
 
 def arrange_kernel(
@@ -121,11 +121,11 @@
                     row = 4 * x + s
                     ref[n, row : row + 1, :] = field_ref[s, INDEX[c], x]
                 ref[n, 4 * x + 3 : 4 * x + 4, :] = keep[x]
-    even = is_even("space")
+    upper = near_is_upper("space")
     for n in range(5):
         plus, minus = (plus_ref[n], minus_ref[n])
-        near_ref[n] = jnp.where(even, minus, plus)
-        far_ref[n] = jnp.where(even, plus, minus)
+        near_ref[n] = jnp.where(upper, minus, plus)
+        far_ref[n] = jnp.where(upper, plus, minus)
     fixed_ref[0] = per_species(relaxation_ref)
     fixed_ref[1] = per_species(uptake_ref)
     fixed_ref[2] = jnp.where(first_half, keep[0], keep[1])
@@ -158,11 +158,11 @@
 def fetch_again_kernel(response_hbm, third_ref, fourth_ref, response_ref, sides_ref, done):
     copies = start_fetch(response_hbm, response_ref, done)
     _, _, has_above, has_below = edges()
-    even_row = is_even("work")
+    upper_row = near_is_upper("work")
     for n in range(5):
         third, fourth = (third_ref[n], fourth_ref[n])
-        sides_ref[n] = jnp.where(has_above, jnp.where(even_row, third, fourth), 0.0)
-        sides_ref[5 + n] = jnp.where(has_below, jnp.where(even_row, fourth, third), 0.0)
+        sides_ref[n] = jnp.where(has_above, jnp.where(upper_row, third, fourth), 0.0)
+        sides_ref[5 + n] = jnp.where(has_below, jnp.where(upper_row, fourth, third), 0.0)
     for copy in copies:
         copy.wait()
 
@@ -187,20 +187,20 @@
 
 def across_kernel(sides_ref, near_ref, far_ref, first_ref, second_ref, one_ref, two_ref):
     has_right, has_left, _, _ = edges()
-    even = is_even("space")
-    even_row = is_even("work")
+    upper = near_is_upper("space")
+    upper_row = near_is_upper("work")
     pieces = {}
     for sign in (1, -1):
         p, m = (PLACE[(1, sign, 0)], PLACE[(-1, sign, 0)])
         pieces[sign] = [sides_ref[PLACE[(0, sign, cz)] - 3] for cz in (0, 1, -1)] + [
-            jnp.where(even, far_ref[p], near_ref[p]),
-            jnp.where(has_right, jnp.where(even, first_ref[p], second_ref[p]), 0.0),
-            jnp.where(even, near_ref[m], far_ref[m]),
-            jnp.where(has_left, jnp.where(even, second_ref[m], first_ref[m]), 0.0),
+            jnp.where(upper, far_ref[p], near_ref[p]),
+            jnp.where(has_right, jnp.where(upper, first_ref[p], second_ref[p]), 0.0),
+            jnp.where(upper, near_ref[m], far_ref[m]),
+            jnp.where(has_left, jnp.where(upper, second_ref[m], first_ref[m]), 0.0),
         ]
     for n in range(7):
-        one_ref[n] = jnp.where(even_row, pieces[-1][n], pieces[1][n])
-        two_ref[n] = jnp.where(even_row, pieces[1][n], pieces[-1][n])
+        one_ref[n] = jnp.where(upper_row, pieces[-1][n], pieces[1][n])
+        two_ref[n] = jnp.where(upper_row, pieces[1][n], pieces[-1][n])
 
 
 def write_payload(payload_ref, density, slots_ref):
@@ -216,17 +216,17 @@
     stay_ref, third_ref, fourth_ref, gain_ref, payload_ref,
 ):
     has_right, has_left, has_above, has_below = edges()
-    even = is_even("space")
-    even_row = is_even("work")
+    upper = near_is_upper("space")
+    upper_row = near_is_upper("work")
     first_half = rows_of() < 4
     rate = fixed_ref[0]
     keep = fixed_ref[2]
-    plus = [jnp.where(even, far_ref[n], near_ref[n]) for n in range(3)]
-    minus = [jnp.where(even, near_ref[n], far_ref[n]) for n in range(3)]
-    right = [jnp.where(has_right, jnp.where(even, first_ref[n], second_ref[n]), 0.0) for n in range(3)]
-    left = [jnp.where(has_left, jnp.where(even, second_ref[n], first_ref[n]), 0.0) for n in range(3)]
-    above = [jnp.where(has_above, jnp.where(even_row, one_ref[n], two_ref[n]), 0.0) for n in range(7)]
-    below = [jnp.where(has_below, jnp.where(even_row, two_ref[n], one_ref[n]), 0.0) for n in range(7)]
+    plus = [jnp.where(upper, far_ref[n], near_ref[n]) for n in range(3)]
+    minus = [jnp.where(upper, near_ref[n], far_ref[n]) for n in range(3)]
+    right = [jnp.where(has_right, jnp.where(upper, first_ref[n], second_ref[n]), 0.0) for n in range(3)]
+    left = [jnp.where(has_left, jnp.where(upper, second_ref[n], first_ref[n]), 0.0) for n in range(3)]
+    above = [jnp.where(has_above, jnp.where(upper_row, one_ref[n], two_ref[n]), 0.0) for n in range(7)]
+    below = [jnp.where(has_below, jnp.where(upper_row, two_ref[n], one_ref[n]), 0.0) for n in range(7)]
     pulled = {}
     for n, cz in enumerate((0, 1, -1)):
         pulled[(0, 0, cz)] = along(middle_ref[PLACE[(0, 0, cz)]], cz)
@@ -253,8 +253,8 @@
     for sign, side in ((1, above), (-1, below)):
         sends[sign] = [here * pulled[(0, sign, cz)] for cz in (0, 1, -1)] + [to_right * side[4], to_left * side[6]]
     for n in range(5):
-        third_ref[n] = jnp.where(even_row, sends[-1][n], sends[1][n])
-        fourth_ref[n] = jnp.where(even_row, sends[1][n], sends[-1][n])
+        third_ref[n] = jnp.where(upper_row, sends[-1][n], sends[1][n])
+        fourth_ref[n] = jnp.where(upper_row, sends[1][n], sends[-1][n])
     gain_ref[0] = jnp.where(first_half, below[0][3:4], below[0][7:8]) * rate
     gain_ref[1] = keep * rate
     gain_ref[2] = jnp.where(first_half, above[0][3:4], above[0][7:8]) * rate
@@ -332,7 +332,7 @@
     sources = (total[16:24], total[0:8] + total[8:16], total[24:32])
     b = lax.axis_index("work")
     last = lax.axis_size("work") - 1
-    even = is_even("space")
+    upper = near_is_upper("space")
     for n, source in enumerate(sources):
         source = factor * source
         if n == 1:
@@ -345,8 +345,8 @@
         parts_ref[3 + n] = source
         to_lower = jnp.where(first_half, equilibrium, half(source))
         to_upper = jnp.where(first_half, half(equilibrium), source)
-        near_ref[n] = jnp.where(even, to_upper, to_lower)
-        far_ref[n] = jnp.where(even, to_lower, to_upper)
+        near_ref[n] = jnp.where(upper, to_upper, to_lower)
+        far_ref[n] = jnp.where(upper, to_lower, to_upper)
 
 
 def second_kernel(
@@ -354,15 +354,15 @@
     pulled_ref, density_ref, payload_ref,
 ):
     has_right, has_left, _, _ = edges()
-    even = is_even("space")
+    upper = near_is_upper("space")
     first_half = rows_of() < 4
     above = [sides_ref[n] for n in range(5)]
     below = [sides_ref[5 + n] for n in range(5)]
     pulled = {}
     for n, cy in enumerate((-1, 0, 1)):
         equilibrium, source = (parts_ref[n], parts_ref[3 + n])
-        right = jnp.where(has_right, jnp.where(even, first_ref[n], second_ref[n]), 0.0)
-        left = jnp.where(has_left, jnp.where(even, second_ref[n], first_ref[n]), 0.0)
+        right = jnp.where(has_right, jnp.where(upper, first_ref[n], second_ref[n]), 0.0)
+        left = jnp.where(has_left, jnp.where(upper, second_ref[n], first_ref[n]), 0.0)
         moved = {
             0: (equilibrium, source),
             1: (jnp.where(first_half, half(equilibrium), half(right)), jnp.where(first_half, half(source), right)),
@@ -429,7 +429,7 @@
         return pltpu.with_memory_space_constraint(value, pltpu.HBM)
 
     def both_ways(near, far, axis):
-        return swapped(near, axis, False), swapped(far, axis, True)
+        return swapped(near, axis, True), swapped(far, axis, False)
 
     def owner(incoming, fetched, fold):
         return call(

time: 89 us -> 87.2 us (0.980)
  blocking collectives: 49.8 us -> 44.2 us
  starting transfers between devices: 16.6 us -> 22.1 us
  waiting for transfers between devices: 8.99 us -> 7.37 us
    all_to_all x3, blocking collectives: 49.8 us -> 44.2 us  [exchange(): lax.all_to_all(value, 'work', split_axis=0, concat_axis=0, tiled=True)]
    ppermute x8, starting transfers between devices: 12.2 us -> 17.6 us  [swapped(): lax.ppermute(value, axis, [(i, (i + step[i]) % count) for i in range(coun...]
    all_to_all x1, waiting for transfers between devices: 8.12 us -> 5.46 us  [exchange(): lax.all_to_all(value, 'work', split_axis=0, concat_axis=0, tiled=True)]
    ppermute x8, waiting for transfers between devices: 0.86 us -> 1.91 us  [swapped(): lax.ppermute(value, axis, [(i, (i + step[i]) % count) for i in range(coun...]
  transfers between devices with their start and end apart: 9 -> 9, of which waited for: 2 -> 3; matrix products, arithmetic and copies ran while one was open for 0% -> 0% of each run, Pallas kernels for 6% -> 6%
where the time goes in v4:
time: 87.2 us; the launch traced here: 86.5 us
  blocking collectives  44.2 us (51%)
  starting transfers between devices  22.1 us (25%)
  Pallas kernels  12.8 us (15%)
  waiting for transfers between devices  7.37 us (8%)
    all_to_all x3, blocking collectives, exchange(): lax.all_to_all(value, 'work', split_axis=0, concat_axis=0, tiled=True)  44.2 us
    ppermute x8, starting transfers between devices, swapped(): lax.ppermute(value, axis, [(i, (i + step[i]) % count) for i in range(coun...  17.6 us
    all_to_all x1, waiting for transfers between devices, exchange(): lax.all_to_all(value, 'work', split_axis=0, concat_axis=0, tiled=True)  5.46 us
    pallas_call x2, Pallas kernels, owner(): call(lambda *refs: owner_kernel(*refs, fold=fold), jax.ShapeDtypeStruct((...  5.42 us
    all_to_all x1, starting transfers between devices, exchange(): lax.all_to_all(value, 'work', split_axis=0, concat_axis=0, tiled=True)  4.49 us
    pallas_call x1, Pallas kernels, body(): call(fetch_again_kernel, (pltpu.VMEM(matrices.shape, BF16), tile(10)), [H...  2.21 us
    pallas_call x1, Pallas kernels, body(): call(fetch_kernel, (pltpu.VMEM(matrices.shape, BF16), tile(6)), [HBM, VM]...  2.21 us
    ppermute x8, waiting for transfers between devices, swapped(): lax.ppermute(value, axis, [(i, (i + step[i]) % count) for i in range(coun...  1.91 us
  transfers between devices with their start and end apart: 9, of which 3 were waited for; matrix products, arithmetic and copies ran while one was open for 0% of the time, Pallas kernels for 6%

profile of v4, /device:TPU:32, one launch (start us, length us, event | category | flops | bytes accessed | tf_op | source)
XLA Modules:
  0.0 86.5 jit_solution(11215564611559369372)
XLA Ops:
  0.0 1.0 %arrange.1 = (f32[9,8,128]{2,1,0:T(8,128)S(1)}, f32[5,8,128]{2,1,0:T(8,128)S(1)}, f32[5,8,128]{2,1,0:T(8,128)S(1)}, f32[6,8,128]{2,1,0:T(8,128)S(1)}) custom-call(f32[3,19,2,1,128]{4,3,2,1,0:T(1,128)} %field_hbm.1, bf16[3,1,2,128]{3,2,1,0:T(2,128)(2,1)} %bitcast.4, s32[2,1,128]{2,1,0:T(1,128)} %mask_hbm.1, f32[3]{0:T(128)} %relaxation_hbm.1, f32[3]{0:T(128)} %uptake_hbm.1), custom_call_target="tpu_custom_call" | custom-call | tf_op jit(solution)/shard_map/arrange/pallas_call | solution.py:451
  1.0 2.3 %collective-permute-start = (f32[5,8,128]{2,1,0:T(8,128)S(1)}, f32[5,8,128]{2,1,0:T(8,128)S(1)}, u32[]{:S(2)}, u32[]{:S(2)}) collective-permute-start(f32[5,8,128]{2,1,0:T(8,128)S(1)} %get-tuple-element.27.near_ref), channel_id=1, source_target_pairs={{0,224},{32,64},{64,32},{96,128},{128,96},{160,192},{192,160},{224... | collective-permute-start | bytes 61448 | tf_op jit(solution)/shard_map/ppermute | solution.py:420
  3.2 0.0 collective-permute-start.1
  3.2 2.2 %fetch.1 = (bf16[32,4,128,128]{3,2,1,0:T(8,128)(2,1)S(1)}, f32[6,8,128]{2,1,0:T(8,128)S(1)}) custom-call(bf16[32,4,128,128]{3,2,1,0:T(8,128)(2,1)} %bitcast.2, f32[9,8,128]{2,1,0:T(8,128)S(1)} %get-tuple-element.26.middle_ref), custom_call_target="tpu_custom_call" | custom-call | tf_op jit(solution)/shard_map/fetch/pallas_call | solution.py:479
  5.5 0.0 collective-permute-done.first_ref
  5.5 0.0 collective-permute-done.1.second_ref
  5.5 2.0 %collective-permute-start.2 = (f32[7,8,128]{2,1,0:T(8,128)S(1)}, f32[7,8,128]{2,1,0:T(8,128)S(1)}, u32[]{:S(2)}, u32[]{:S(2)}) collective-permute-start(f32[7,8,128]{2,1,0:T(8,128)S(1)} %get-tuple-element.30), channel_id=1, source_target_pairs={{0,31},{1,2},{2,1},{3,4},{4,3},{5,6},{6,5},{7,8},{8,7},{9,10},{10,... | collective-permute-start | bytes 86024 | tf_op jit(solution)/shard_map/ppermute | solution.py:420
  7.5 6.5 %collective-permute-start.3 = (f32[7,8,128]{2,1,0:T(8,128)S(1)}, f32[7,8,128]{2,1,0:T(8,128)S(1)}, u32[]{:S(2)}, u32[]{:S(2)}) collective-permute-start(f32[7,8,128]{2,1,0:T(8,128)S(1)} %get-tuple-element.31), channel_id=1, source_target_pairs={{0,1},{1,0},{2,3},{3,2},{4,5},{5,4},{6,7},{7,6},{8,9},{9,8},{10,11... | collective-permute-start | bytes 86024 | tf_op jit(solution)/shard_map/ppermute | solution.py:420
  14.0 1.0 %slots.1.slots_ref = f32[32,16,128]{2,1,0:T(8,128)S(1)} custom-call(s32[1,1,32,4,128]{4,3,2,1,0:T(4,128)} %cells_hbm.1, s32[1,1,32]{2,1,0:T(1,128)} %load_hbm.1), custom_call_target="tpu_custom_call" | custom-call | tf_op jit(solution)/shard_map/slots/pallas_call | solution.py:468
  15.0 0.0 collective-permute-done.2.one_ref
  15.0 0.8 collective-permute-done.3.two_ref
  15.9 0.1 first.1
  16.0 16.2 %all_to_all.20.refs_0_.incoming_ref = bf16[32,16,128]{2,1,0:T(8,128)(2,1)S(1)} all-to-all(bf16[32,16,128]{2,1,0:T(8,128)(2,1)S(1)} %get-tuple-element.37), channel_id=1, replica_groups=mesh['space'=8,'work'=32] {'work'}, dimensions={0} | all-to-all | bytes 262144 | tf_op jit(solution)/shard_map/all_to_all | solution.py:448
  32.2 3.1 %owner_fold.1 = bf16[32,32,128]{2,1,0:T(8,128)(2,1)} custom-call(bf16[32,16,128]{2,1,0:T(8,128)(2,1)S(1)} %all_to_all.20.refs_0_.incoming_ref, bf16[32,4,128,128]{3,2,1,0:T(8,128)(2,1)S(1)} %get-tuple-element.38.refs_1_), custom_call_target="tpu_custom_call" | custom-call | tf_op jit(solution)/shard_map/owner_fold/pallas_call | solution.py:435
  35.3 4.5 %all-to-all-start.1 = ((bf16[32,32,128]{2,1,0:T(8,128)(2,1)}), bf16[32,32,128]{2,1,0:T(8,128)(2,1)S(1)}, u32[]{:S(2)}, u32[]{:S(2)}) async-start(bf16[32,32,128]{2,1,0:T(8,128)(2,1)} %owner_fold.1), calls=%async_computation.1 | async-start | bytes 524288 | tf_op jit(solution)/shard_map/all_to_all | solution.py:448
  39.8 1.6 %collective-permute-start.4 = (f32[5,8,128]{2,1,0:T(8,128)S(1)}, f32[5,8,128]{2,1,0:T(8,128)S(1)}, u32[]{:S(2)}, u32[]{:S(2)}) collective-permute-start(f32[5,8,128]{2,1,0:T(8,128)S(1)} %get-tuple-element.34), channel_id=1, source_target_pairs={{0,31},{1,2},{2,1},{3,4},{4,3},{5,6},{6,5},{7,8},{8,7},{9,10},{10,... | collective-permute-start | bytes 61448 | tf_op jit(solution)/shard_map/ppermute | solution.py:420
  41.4 4.1 %collective-permute-start.5 = (f32[5,8,128]{2,1,0:T(8,128)S(1)}, f32[5,8,128]{2,1,0:T(8,128)S(1)}, u32[]{:S(2)}, u32[]{:S(2)}) collective-permute-start(f32[5,8,128]{2,1,0:T(8,128)S(1)} %get-tuple-element.35), channel_id=1, source_target_pairs={{0,1},{1,0},{2,3},{3,2},{4,5},{5,4},{6,7},{7,6},{8,9},{9,8},{10,11... | collective-permute-start | bytes 61448 | tf_op jit(solution)/shard_map/ppermute | solution.py:420
  45.4 5.5 %all-to-all-done.1.returned_ref = bf16[32,32,128]{2,1,0:T(8,128)(2,1)S(1)} async-done(((bf16[32,32,128]{2,1,0:T(8,128)(2,1)}), bf16[32,32,128]{2,1,0:T(8,128)(2,1)S(1)}, u32[]{:S(2)}, u32[]{:S(2)}) %all-to-all-start.1) | async-done | bytes 262176 | tf_op jit(solution)/shard_map/all_to_all | solution.py:448
  50.9 0.1 gather.1
  51.0 0.1 collective-permute-start.6
  51.1 1.0 %collective-permute-start.7 = (f32[3,8,128]{2,1,0:T(8,128)S(1)}, f32[3,8,128]{2,1,0:T(8,128)S(1)}, u32[]{:S(2)}, u32[]{:S(2)}) collective-permute-start(f32[3,8,128]{2,1,0:T(8,128)S(1)} %get-tuple-element.42), channel_id=1, source_target_pairs={{0,32},{32,0},{64,96},{96,64},{128,160},{160,128},{192,224},{224,1... | collective-permute-start | bytes 36872 | tf_op jit(solution)/shard_map/ppermute | solution.py:420
  52.1 0.0 collective-permute-done.4.third_ref
  52.1 0.0 collective-permute-done.5.fourth_ref
  52.1 2.2 %fetch_again.1 = (bf16[32,4,128,128]{3,2,1,0:T(8,128)(2,1)S(1)}, f32[10,8,128]{2,1,0:T(8,128)S(1)}) custom-call(bf16[32,4,128,128]{3,2,1,0:T(8,128)(2,1)} %bitcast.3, f32[5,8,128]{2,1,0:T(8,128)S(1)} %collective-permute-done.4.third_ref, f32[5,8,128]{2,1,0:T(8,128)S(1)} %collective-permute-done.5.fourth_ref), custom_call_target="tpu_custom_call" | custom-call | tf_op jit(solution)/shard_map/fetch_again/pallas_call | solution.py:498
  54.3 1.1 %collective-permute-done.6.first_ref = f32[3,8,128]{2,1,0:T(8,128)S(1)} collective-permute-done((f32[3,8,128]{2,1,0:T(8,128)S(1)}, f32[3,8,128]{2,1,0:T(8,128)S(1)}, u32[]{:S(2)}, u32[]{:S(2)}) %collective-permute-start.6) | collective-permute-done | bytes 12320 | tf_op jit(solution)/shard_map/ppermute | solution.py:420
  55.4 0.0 collective-permute-done.7.second_ref
  55.4 0.1 second.1
  55.5 14.1 %all_to_all.21.refs_0_ = bf16[32,16,128]{2,1,0:T(8,128)(2,1)S(1)} all-to-all(bf16[32,16,128]{2,1,0:T(8,128)(2,1)S(1)} %get-tuple-element.43), channel_id=1, replica_groups=mesh['space'=8,'work'=32] {'work'}, dimensions={0} | all-to-all | bytes 262144 | tf_op jit(solution)/shard_map/all_to_all | solution.py:448
  69.6 2.4 %owner.1 = bf16[32,16,128]{2,1,0:T(8,128)(2,1)S(1)} custom-call(bf16[32,16,128]{2,1,0:T(8,128)(2,1)S(1)} %all_to_all.21.refs_0_, bf16[32,4,128,128]{3,2,1,0:T(8,128)(2,1)S(1)} %get-tuple-element.44.refs_1_), custom_call_target="tpu_custom_call" | custom-call | tf_op jit(solution)/shard_map/owner/pallas_call | solution.py:435
  71.9 13.9 %all_to_all.22.returned_ref = bf16[32,16,128]{2,1,0:T(8,128)(2,1)S(1)} all-to-all(bf16[32,16,128]{2,1,0:T(8,128)(2,1)S(1)} %owner.1), channel_id=1, replica_groups=mesh['space'=8,'work'=32] {'work'}, dimensions={0} | all-to-all | bytes 262144 | tf_op jit(solution)/shard_map/all_to_all | solution.py:448
  85.8 0.7 last.1
  (1 shorter events, 0.0 us)
Async XLA Ops:
  1.0 4.5 %collective-permute-start = (f32[5,8,128]{2,1,0:T(8,128)S(1)}, f32[5,8,128]{2,1,0:T(8,128)S(1)}, u32[]{:S(2)}, u32[]{:S(2)}) collective-permute-start(f32[5,8,128]{2,1,0:T(8,128)S(1)} %get-tuple-element.27.near_ref), channel_id=1, source_target_pairs={{0,224},{32,64},{64,32},{96,128},{128,96},{160,192},{192,160},{224... | collective-permute-start | bytes 61448 | tf_op jit(solution)/shard_map/ppermute | solution.py:420
  3.2 2.2 %collective-permute-start.1 = (f32[5,8,128]{2,1,0:T(8,128)S(1)}, f32[5,8,128]{2,1,0:T(8,128)S(1)}, u32[]{:S(2)}, u32[]{:S(2)}) collective-permute-start(f32[5,8,128]{2,1,0:T(8,128)S(1)} %get-tuple-element.28.far_ref), channel_id=1, source_target_pairs={{0,32},{32,0},{64,96},{96,64},{128,160},{160,128},{192,224},{224,1... | collective-permute-start | bytes 61448 | tf_op jit(solution)/shard_map/ppermute | solution.py:420
  5.5 9.5 %collective-permute-start.2 = (f32[7,8,128]{2,1,0:T(8,128)S(1)}, f32[7,8,128]{2,1,0:T(8,128)S(1)}, u32[]{:S(2)}, u32[]{:S(2)}) collective-permute-start(f32[7,8,128]{2,1,0:T(8,128)S(1)} %get-tuple-element.30), channel_id=1, source_target_pairs={{0,31},{1,2},{2,1},{3,4},{4,3},{5,6},{6,5},{7,8},{8,7},{9,10},{10,... | collective-permute-start | bytes 86024 | tf_op jit(solution)/shard_map/ppermute | solution.py:420
  7.5 8.3 %collective-permute-start.3 = (f32[7,8,128]{2,1,0:T(8,128)S(1)}, f32[7,8,128]{2,1,0:T(8,128)S(1)}, u32[]{:S(2)}, u32[]{:S(2)}) collective-permute-start(f32[7,8,128]{2,1,0:T(8,128)S(1)} %get-tuple-element.31), channel_id=1, source_target_pairs={{0,1},{1,0},{2,3},{3,2},{4,5},{5,4},{6,7},{7,6},{8,9},{9,8},{10,11... | collective-permute-start | bytes 86024 | tf_op jit(solution)/shard_map/ppermute | solution.py:420
  35.3 15.6 %all-to-all-start.1 = ((bf16[32,32,128]{2,1,0:T(8,128)(2,1)}), bf16[32,32,128]{2,1,0:T(8,128)(2,1)S(1)}, u32[]{:S(2)}, u32[]{:S(2)}) async-start(bf16[32,32,128]{2,1,0:T(8,128)(2,1)} %owner_fold.1), calls=%async_computation.1 | async-start | bytes 524288 | tf_op jit(solution)/shard_map/all_to_all | solution.py:448
  39.8 12.3 %collective-permute-start.4 = (f32[5,8,128]{2,1,0:T(8,128)S(1)}, f32[5,8,128]{2,1,0:T(8,128)S(1)}, u32[]{:S(2)}, u32[]{:S(2)}) collective-permute-start(f32[5,8,128]{2,1,0:T(8,128)S(1)} %get-tuple-element.34), channel_id=1, source_target_pairs={{0,31},{1,2},{2,1},{3,4},{4,3},{5,6},{6,5},{7,8},{8,7},{9,10},{10,... | collective-permute-start | bytes 61448 | tf_op jit(solution)/shard_map/ppermute | solution.py:420
  41.4 10.7 %collective-permute-start.5 = (f32[5,8,128]{2,1,0:T(8,128)S(1)}, f32[5,8,128]{2,1,0:T(8,128)S(1)}, u32[]{:S(2)}, u32[]{:S(2)}) collective-permute-start(f32[5,8,128]{2,1,0:T(8,128)S(1)} %get-tuple-element.35), channel_id=1, source_target_pairs={{0,1},{1,0},{2,3},{3,2},{4,5},{5,4},{6,7},{7,6},{8,9},{9,8},{10,11... | collective-permute-start | bytes 61448 | tf_op jit(solution)/shard_map/ppermute | solution.py:420
  51.0 4.4 %collective-permute-start.6 = (f32[3,8,128]{2,1,0:T(8,128)S(1)}, f32[3,8,128]{2,1,0:T(8,128)S(1)}, u32[]{:S(2)}, u32[]{:S(2)}) collective-permute-start(f32[3,8,128]{2,1,0:T(8,128)S(1)} %get-tuple-element.41), channel_id=1, source_target_pairs={{0,224},{32,64},{64,32},{96,128},{128,96},{160,192},{192,160},{224... | collective-permute-start | bytes 36872 | tf_op jit(solution)/shard_map/ppermute | solution.py:420
  51.1 4.3 %collective-permute-start.7 = (f32[3,8,128]{2,1,0:T(8,128)S(1)}, f32[3,8,128]{2,1,0:T(8,128)S(1)}, u32[]{:S(2)}, u32[]{:S(2)}) collective-permute-start(f32[3,8,128]{2,1,0:T(8,128)S(1)} %get-tuple-element.42), channel_id=1, source_target_pairs={{0,32},{32,0},{64,96},{96,64},{128,160},{160,128},{192,224},{224,1... | collective-permute-start | bytes 36872 | tf_op jit(solution)/shard_map/ppermute | solution.py:420

commit v5 on v4

--- a/solution.py
+++ b/solution.py
@@ -40,6 +40,10 @@
 F32 = jnp.float32
 BF16 = jnp.bfloat16
 CHUNKS = 4
+GROUP = 4
+SECTION_BITS = 6
+SECTION = 1 << SECTION_BITS
+SECTIONS = LANES // SECTION
 
 VM = pl.BlockSpec(memory_space=pltpu.VMEM)
 SM = pl.BlockSpec(memory_space=pltpu.SMEM)
@@ -261,16 +265,20 @@
     gain_ref[3] = density
 
 
-def owner_kernel(incoming_ref, matrices_ref, out_ref, picked_ref, reply_ref, sums_ref, *, fold):
+def owner_kernel(incoming_ref, density_ref, matrices_ref, out_ref, picked_ref, reply_ref, sums_ref, *, fold):
     count = incoming_ref.shape[0]
     column = jnp.where(rows_of() < 4, 0, 1)
-    cell_rows = lax.broadcasted_iota(jnp.int32, (LANES, LANES), 0)
+    cell_rows = lax.broadcasted_iota(jnp.int32, (SECTION, LANES), 0)
     contract = (((1,), (1,)), ((), ()))
     zero = jnp.zeros((8, LANES), F32)
     slot_rows = (3, 7, 11, 15)
-    for b in range(count):
+    def pick(b):
         tiles = incoming_ref[b].astype(F32)
-        top = tiles[0:8]
+        if fold:
+            top = tiles[0:8]
+        else:
+            pair = density_ref[16 * (b // 2) : 16 * (b // 2) + 16, :].astype(F32)
+            top = pair[0:8] if b % 2 == 0 else pair[8:16]
         picked = []
         for row in slot_rows:
             cell = jnp.broadcast_to(tiles[row : row + 1].astype(jnp.int32), (8, LANES))
@@ -293,29 +301,45 @@
         rights = []
         for k, row in enumerate(slot_rows):
             cell = tiles[row : row + 1].astype(jnp.int32)
-            mine = jnp.broadcast_to(cell >> 7, (8, LANES)) == column
-            reply = jnp.where(mine, reply_ref[b, 8 * k : 8 * k + 8, :], 0.0)
-            high = reply.astype(BF16).astype(F32)
-            lefts.append(jnp.concatenate([high, reply - high], axis=0).astype(BF16))
-            rights.append(jnp.where(cell_rows == (cell & (LANES - 1)), 1.0, 0.0).astype(BF16))
+            section = jnp.broadcast_to(cell >> SECTION_BITS, (8, LANES))
+            reply = reply_ref[b, 8 * k : 8 * k + 8, :]
+            parts = [jnp.where(section == column * SECTIONS + m, reply, 0.0) for m in range(SECTIONS)]
+            highs = [part.astype(BF16).astype(F32) for part in parts]
+            lows = [part - high for part, high in zip(parts, highs)]
+            lefts.append(jnp.concatenate(highs + lows, axis=0).astype(BF16))
+            rights.append(jnp.where(cell_rows == (cell & (SECTION - 1)), 1.0, 0.0).astype(BF16))
         both = lax.dot_general(
             jnp.concatenate(lefts, axis=1), jnp.concatenate(rights, axis=1), contract, preferred_element_type=F32
         )
-        total = both[0:8] + both[8:16]
-        high = total.astype(BF16).astype(F32)
-        out_ref[b, 0:16, :] = jnp.concatenate([high, total - high], axis=0).astype(BF16)
-        if fold:
-            sums_ref[b] = total
-
-    for b in range(count):
-        respond(b)
-    for b in range(count):
-        spread(b)
+        sums = [
+            both[8 * m : 8 * m + 8] + both[8 * (SECTIONS + m) : 8 * (SECTIONS + m) + 8] for m in range(SECTIONS)
+        ]
+        total = jnp.concatenate(sums, axis=1)
+        sums_ref[b] = total
+        if not fold:
+            high = total.astype(BF16).astype(F32)
+            out_ref[b, 0:16, :] = jnp.concatenate([high, total - high], axis=0).astype(BF16)
+
+    stages = (pick, respond, spread)
+    groups = count // GROUP
+    for turn in range(groups + len(stages) - 1):
+        for lag, stage in enumerate(stages):
+            if 0 <= turn - lag < groups:
+                for b in range((turn - lag) * GROUP, (turn - lag + 1) * GROUP):
+                    stage(b)
     if fold:
-        for b in range(count):
-            before = sums_ref[b - 1] if b > 0 else zero
-            after = sums_ref[b + 1] if b < count - 1 else zero
-            out_ref[b, 16:32, :] = jnp.concatenate([before, after], axis=0).astype(BF16)
+        rows = rows_of()
+        for pair in range(count // 2):
+            packed = []
+            for b in (2 * pair, 2 * pair + 1):
+                total = sums_ref[b]
+                high = total.astype(BF16).astype(F32)
+                before = sums_ref[b - 1] if b > 0 else zero
+                after = sums_ref[b + 1] if b < count - 1 else zero
+                for value, third, seventh in ((high, 0, 1), (total - high, 2, 4), (before, 5, 6)):
+                    value = jnp.where(rows == 3, after[third : third + 1], value)
+                    packed.append(jnp.where(rows == 7, after[seventh : seventh + 1], value))
+            out_ref[48 * pair : 48 * pair + 48, :] = jnp.concatenate(packed, axis=0).astype(BF16)
 
 
 def total_of(returned_ref, rows):
@@ -328,8 +352,13 @@
 def gather_kernel(returned_ref, incoming_ref, gain_ref, fixed_ref, parts_ref, near_ref, far_ref):
     first_half = rows_of() < 4
     factor = fixed_ref[1]
-    total = total_of(returned_ref, 32)
-    sources = (total[16:24], total[0:8] + total[8:16], total[24:32])
+    total = returned_ref[0:48, :].astype(F32)
+    for pair in range(1, returned_ref.shape[0] // 48):
+        total = total + returned_ref[48 * pair : 48 * pair + 48, :].astype(F32)
+    total = total[0:24] + total[24:48]
+    ends = [total[row : row + 1] for row in (3, 7, 11, 15, 19, 23)]
+    after = jnp.concatenate(ends[0:3] + ends[0:1] + ends[3:6] + ends[0:1], axis=0)
+    sources = (total[16:24], total[0:8] + total[8:16], after)
     b = lax.axis_index("work")
     last = lax.axis_size("work") - 1
     upper = near_is_upper("space")
@@ -350,7 +379,7 @@
 
 
 def second_kernel(
-    stay_ref, sides_ref, parts_ref, first_ref, second_ref, fixed_ref, slots_ref,
+    stay_ref, sides_ref, parts_ref, first_ref, second_ref, fixed_ref,
     pulled_ref, density_ref, payload_ref,
 ):
     has_right, has_left, _, _ = edges()
@@ -380,7 +409,9 @@
             pulled[c] = along(base + shifted + WEIGHTS[INDEX[c]] * added, c[2])
     pulled = {c: pulled[c] for c in DIRECTIONS}
     density = moment(pulled, [fixed_ref[3 + c] for c in range(3)])
-    write_payload(payload_ref, density, slots_ref)
+    twice = jnp.concatenate([density, density], axis=0).astype(BF16)
+    for pair in range(payload_ref.shape[0] // 16):
+        payload_ref[16 * pair : 16 * pair + 16, :] = twice
     for i, c in enumerate(DIRECTIONS):
         pulled_ref[i] = pulled[c]
     density_ref[0] = density
@@ -431,18 +462,18 @@
     def both_ways(near, far, axis):
         return swapped(near, axis, True), swapped(far, axis, False)
 
-    def owner(incoming, fetched, fold):
+    def owner(incoming, densities, fetched, fold):
         return call(
             lambda *refs: owner_kernel(*refs, fold=fold),
-            jax.ShapeDtypeStruct((owners, 32 if fold else 16, LANES), BF16),
-            [VM, VM],
+            jax.ShapeDtypeStruct((owners * 24, LANES) if fold else (owners, 16, LANES), BF16),
+            [VM, VM, VM],
             "owner_fold" if fold else "owner",
             scratch_shapes=[
                 pltpu.VMEM((owners, 32, 2 * LANES), BF16),
                 pltpu.VMEM((owners, 32, LANES), F32),
                 pltpu.VMEM((owners, 8, LANES), F32),
             ],
-        )(incoming, fetched)
+        )(incoming, densities, fetched)
 
     def exchange(value):
         return lax.all_to_all(value, "work", split_axis=0, concat_axis=0, tiled=True)
@@ -490,7 +521,8 @@
     )(middle, near, far, first, second, one, two, fixed, slots)
     incoming = exchange(payload)
     third, fourth = both_ways(third, fourth, "work")
-    returned = exchange(owner(incoming, fetched, True))
+    returned = owner(incoming, payload, fetched, True).reshape(owners, 24, LANES)
+    returned = exchange(returned).reshape(-1, LANES)
     parts, near, far = call(gather_kernel, (tile(6), tile(3), tile(3)), [VM] * 4, "gather")(
         returned, incoming, gain, fixed
     )
@@ -503,9 +535,10 @@
         scratch_shapes=[pltpu.SemaphoreType.DMA((CHUNKS,))],
     )(outside(matrices), third, fourth)
     pulled, density, payload = call(
-        second_kernel, (tile(19), tile(1), payload_shape), [VM] * 7, "second"
-    )(stay, sides, parts, first, second, fixed, slots)
-    returned = exchange(owner(exchange(payload), fetched, False))
+        second_kernel, (tile(19), tile(1), jax.ShapeDtypeStruct((owners * 8, LANES), BF16)), [VM] * 6, "second"
+    )(stay, sides, parts, first, second, fixed)
+    densities = exchange(payload.reshape(owners, 8, LANES)).reshape(-1, LANES)
+    returned = exchange(owner(incoming, densities, fetched, False))
     return call(last_kernel, jax.ShapeDtypeStruct(adjoint.shape, F32), [VM] * 4, "last")(
         returned, pulled, density, fixed
     )

time: 87.2 us -> 84.6 us (0.970)
  blocking collectives: 44.2 us -> 43.3 us
    all_to_all x3, blocking collectives: 44.2 us -> 43.3 us  [exchange(): lax.all_to_all(value, 'work', split_axis=0, concat_axis=0, tiled=True)]
where the time goes in v5:
time: 84.6 us; the launch traced here: 84.3 us
  blocking collectives  43.3 us (51%)
  starting transfers between devices  22 us (26%)
  Pallas kernels  12 us (14%)
  waiting for transfers between devices  6.98 us (8%)
    all_to_all x3, blocking collectives, exchange(): lax.all_to_all(value, 'work', split_axis=0, concat_axis=0, tiled=True)  43.3 us
    ppermute x8, starting transfers between devices, swapped(): lax.ppermute(value, axis, [(i, (i + step[i]) % count) for i in range(coun...  17.5 us
    all_to_all x1, waiting for transfers between devices, exchange(): lax.all_to_all(value, 'work', split_axis=0, concat_axis=0, tiled=True)  4.97 us
    pallas_call x2, Pallas kernels, owner(): call(lambda *refs: owner_kernel(*refs, fold=fold), jax.ShapeDtypeStruct((...  4.65 us
    all_to_all x1, starting transfers between devices, exchange(): lax.all_to_all(value, 'work', split_axis=0, concat_axis=0, tiled=True)  4.49 us
    pallas_call x1, Pallas kernels, body(): call(fetch_again_kernel, (pltpu.VMEM(matrices.shape, BF16), tile(10)), [H...  2.21 us
    pallas_call x1, Pallas kernels, body(): call(fetch_kernel, (pltpu.VMEM(matrices.shape, BF16), tile(6)), [HBM, VM]...  2.21 us
    ppermute x8, waiting for transfers between devices, swapped(): lax.ppermute(value, axis, [(i, (i + step[i]) % count) for i in range(coun...  2.01 us
  transfers between devices with their start and end apart: 9, of which 3 were waited for; matrix products, arithmetic and copies ran while one was open for 0% of the time, Pallas kernels for 6%

profile of v5, /device:TPU:32, one launch (start us, length us, event | category | flops | bytes accessed | tf_op | source)
XLA Modules:
  0.0 84.3 jit_solution(10769904388585980530)
XLA Ops:
  0.0 1.0 %arrange.1 = (f32[9,8,128]{2,1,0:T(8,128)S(1)}, f32[5,8,128]{2,1,0:T(8,128)S(1)}, f32[5,8,128]{2,1,0:T(8,128)S(1)}, f32[6,8,128]{2,1,0:T(8,128)S(1)}) custom-call(f32[3,19,2,1,128]{4,3,2,1,0:T(1,128)} %field_hbm.1, bf16[3,1,2,128]{3,2,1,0:T(2,128)(2,1)} %bitcast.11, s32[2,1,128]{2,1,0:T(1,128)} %mask_hbm.1, f32[3]{0:T(128)} %relaxation_hbm.1, f32[3]{0:T(128)} %uptake_hbm.1), custom_call_target="tpu_custom_call" | custom-call | tf_op jit(solution)/shard_map/arrange/pallas_call | solution.py:482
  1.0 2.3 %collective-permute-start = (f32[5,8,128]{2,1,0:T(8,128)S(1)}, f32[5,8,128]{2,1,0:T(8,128)S(1)}, u32[]{:S(2)}, u32[]{:S(2)}) collective-permute-start(f32[5,8,128]{2,1,0:T(8,128)S(1)} %get-tuple-element.27.near_ref), channel_id=1, source_target_pairs={{0,224},{32,64},{64,32},{96,128},{128,96},{160,192},{192,160},{224... | collective-permute-start | bytes 61448 | tf_op jit(solution)/shard_map/ppermute | solution.py:451
  3.2 0.0 collective-permute-start.1
  3.2 2.2 %fetch.1 = (bf16[32,4,128,128]{3,2,1,0:T(8,128)(2,1)S(1)}, f32[6,8,128]{2,1,0:T(8,128)S(1)}) custom-call(bf16[32,4,128,128]{3,2,1,0:T(8,128)(2,1)} %bitcast.9, f32[9,8,128]{2,1,0:T(8,128)S(1)} %get-tuple-element.26.middle_ref), custom_call_target="tpu_custom_call" | custom-call | tf_op jit(solution)/shard_map/fetch/pallas_call | solution.py:510
  5.5 0.0 collective-permute-done.first_ref
  5.5 0.0 collective-permute-done.1.second_ref
  5.5 2.0 %collective-permute-start.2 = (f32[7,8,128]{2,1,0:T(8,128)S(1)}, f32[7,8,128]{2,1,0:T(8,128)S(1)}, u32[]{:S(2)}, u32[]{:S(2)}) collective-permute-start(f32[7,8,128]{2,1,0:T(8,128)S(1)} %get-tuple-element.30), channel_id=1, source_target_pairs={{0,31},{1,2},{2,1},{3,4},{4,3},{5,6},{6,5},{7,8},{8,7},{9,10},{10,... | collective-permute-start | bytes 86024 | tf_op jit(solution)/shard_map/ppermute | solution.py:451
  7.5 6.5 %collective-permute-start.3 = (f32[7,8,128]{2,1,0:T(8,128)S(1)}, f32[7,8,128]{2,1,0:T(8,128)S(1)}, u32[]{:S(2)}, u32[]{:S(2)}) collective-permute-start(f32[7,8,128]{2,1,0:T(8,128)S(1)} %get-tuple-element.31), channel_id=1, source_target_pairs={{0,1},{1,0},{2,3},{3,2},{4,5},{5,4},{6,7},{7,6},{8,9},{9,8},{10,11... | collective-permute-start | bytes 86024 | tf_op jit(solution)/shard_map/ppermute | solution.py:451
  14.0 1.0 %slots.1.slots_ref = f32[32,16,128]{2,1,0:T(8,128)S(1)} custom-call(s32[1,1,32,4,128]{4,3,2,1,0:T(4,128)} %cells_hbm.1, s32[1,1,32]{2,1,0:T(1,128)} %load_hbm.1), custom_call_target="tpu_custom_call" | custom-call | tf_op jit(solution)/shard_map/slots/pallas_call | solution.py:499
  15.0 0.0 collective-permute-done.2.one_ref
  15.0 0.8 %collective-permute-done.3.two_ref = f32[7,8,128]{2,1,0:T(8,128)S(1)} collective-permute-done((f32[7,8,128]{2,1,0:T(8,128)S(1)}, f32[7,8,128]{2,1,0:T(8,128)S(1)}, u32[]{:S(2)}, u32[]{:S(2)}) %collective-permute-start.3) | collective-permute-done | bytes 28704 | tf_op jit(solution)/shard_map/ppermute | solution.py:451
  15.9 0.1 first.1
  16.0 16.2 %all_to_all.20.refs_0_.incoming_ref = bf16[32,16,128]{2,1,0:T(8,128)(2,1)S(1)} all-to-all(bf16[32,16,128]{2,1,0:T(8,128)(2,1)S(1)} %get-tuple-element.33.refs_1_), channel_id=1, replica_groups=mesh['space'=8,'work'=32] {'work'}, dimensions={0} | all-to-all | bytes 262144 | tf_op jit(solution)/shard_map/all_to_all | solution.py:479
  32.2 2.7 %owner_fold.1 = bf16[768,128]{1,0:T(8,128)(2,1)} custom-call(bf16[32,16,128]{2,1,0:T(8,128)(2,1)S(1)} %all_to_all.20.refs_0_.incoming_ref, bf16[32,16,128]{2,1,0:T(8,128)(2,1)S(1)} %get-tuple-element.33.refs_1_, bf16[32,4,128,128]{3,2,1,0:T(8,128)(2,1)S(1)} %get-tuple-element.38.refs_2_), custom_call_target="tpu_custom_call" | custom-call | tf_op jit(solution)/shard_map/owner_fold/pallas_call | solution.py:466
  34.9 4.5 %all-to-all-start.1 = ((bf16[32,24,128]{2,1,0:T(8,128)(2,1)}), bf16[32,24,128]{2,1,0:T(8,128)(2,1)S(1)}, u32[]{:S(2)}, u32[]{:S(2)}) async-start(bf16[32,24,128]{2,1,0:T(8,128)(2,1)} %bitcast.2), calls=%async_computation.1 | async-start | bytes 393216 | tf_op jit(solution)/shard_map/all_to_all | solution.py:479
  39.4 1.6 %collective-permute-start.4 = (f32[5,8,128]{2,1,0:T(8,128)S(1)}, f32[5,8,128]{2,1,0:T(8,128)S(1)}, u32[]{:S(2)}, u32[]{:S(2)}) collective-permute-start(f32[5,8,128]{2,1,0:T(8,128)S(1)} %get-tuple-element.35), channel_id=1, source_target_pairs={{0,31},{1,2},{2,1},{3,4},{4,3},{5,6},{6,5},{7,8},{8,7},{9,10},{10,... | collective-permute-start | bytes 61448 | tf_op jit(solution)/shard_map/ppermute | solution.py:451
  41.0 4.1 %collective-permute-start.5 = (f32[5,8,128]{2,1,0:T(8,128)S(1)}, f32[5,8,128]{2,1,0:T(8,128)S(1)}, u32[]{:S(2)}, u32[]{:S(2)}) collective-permute-start(f32[5,8,128]{2,1,0:T(8,128)S(1)} %get-tuple-element.36), channel_id=1, source_target_pairs={{0,1},{1,0},{2,3},{3,2},{4,5},{5,4},{6,7},{7,6},{8,9},{9,8},{10,11... | collective-permute-start | bytes 61448 | tf_op jit(solution)/shard_map/ppermute | solution.py:451
  45.1 5.0 %all-to-all-done.1 = bf16[32,24,128]{2,1,0:T(8,128)(2,1)S(1)} async-done(((bf16[32,24,128]{2,1,0:T(8,128)(2,1)}), bf16[32,24,128]{2,1,0:T(8,128)(2,1)S(1)}, u32[]{:S(2)}, u32[]{:S(2)}) %all-to-all-start.1) | async-done | bytes 196640 | tf_op jit(solution)/shard_map/all_to_all | solution.py:479
  50.1 0.1 collective-permute-start.6
  50.2 0.9 %collective-permute-start.7 = (f32[3,8,128]{2,1,0:T(8,128)S(1)}, f32[3,8,128]{2,1,0:T(8,128)S(1)}, u32[]{:S(2)}, u32[]{:S(2)}) collective-permute-start(f32[3,8,128]{2,1,0:T(8,128)S(1)} %get-tuple-element.42), channel_id=1, source_target_pairs={{0,32},{32,0},{64,96},{96,64},{128,160},{160,128},{192,224},{224,1... | collective-permute-start | bytes 36872 | tf_op jit(solution)/shard_map/ppermute | solution.py:451
  51.1 0.0 collective-permute-done.4.third_ref
  51.1 0.0 collective-permute-done.5.fourth_ref
  51.1 2.2 %fetch_again.1 = (bf16[32,4,128,128]{3,2,1,0:T(8,128)(2,1)S(1)}, f32[10,8,128]{2,1,0:T(8,128)S(1)}) custom-call(bf16[32,4,128,128]{3,2,1,0:T(8,128)(2,1)} %bitcast.10, f32[5,8,128]{2,1,0:T(8,128)S(1)} %collective-permute-done.4.third_ref, f32[5,8,128]{2,1,0:T(8,128)S(1)} %collective-permute-done.5.fourth_ref), custom_call_target="tpu_custom_call" | custom-call | tf_op jit(solution)/shard_map/fetch_again/pallas_call | solution.py:530
  53.4 1.1 %collective-permute-done.6.first_ref = f32[3,8,128]{2,1,0:T(8,128)S(1)} collective-permute-done((f32[3,8,128]{2,1,0:T(8,128)S(1)}, f32[3,8,128]{2,1,0:T(8,128)S(1)}, u32[]{:S(2)}, u32[]{:S(2)}) %collective-permute-start.6) | collective-permute-done | bytes 12320 | tf_op jit(solution)/shard_map/ppermute | solution.py:451
  54.5 0.0 collective-permute-done.7.second_ref
  54.5 0.1 second.1
  54.6 13.3 %all_to_all.21 = bf16[32,8,128]{2,1,0:T(8,128)(2,1)S(1)} all-to-all(bf16[32,8,128]{2,1,0:T(8,128)(2,1)S(1)} %bitcast.8), channel_id=1, replica_groups=mesh['space'=8,'work'=32] {'work'}, dimensions={0} | all-to-all | bytes 131072 | tf_op jit(solution)/shard_map/all_to_all | solution.py:479
  67.9 1.9 %owner.1 = bf16[32,16,128]{2,1,0:T(8,128)(2,1)S(1)} custom-call(bf16[32,16,128]{2,1,0:T(8,128)(2,1)S(1)} %all_to_all.20.refs_0_.incoming_ref, bf16[256,128]{1,0:T(8,128)(2,1)S(1)} %bitcast.7, bf16[32,4,128,128]{3,2,1,0:T(8,128)(2,1)S(1)} %get-tuple-element.44.refs_2_), custom_call_target="tpu_custom_call" | custom-call | tf_op jit(solution)/shard_map/owner/pallas_call | solution.py:466
  69.8 13.7 %all_to_all.22.returned_ref = bf16[32,16,128]{2,1,0:T(8,128)(2,1)S(1)} all-to-all(bf16[32,16,128]{2,1,0:T(8,128)(2,1)S(1)} %owner.1), channel_id=1, replica_groups=mesh['space'=8,'work'=32] {'work'}, dimensions={0} | all-to-all | bytes 262144 | tf_op jit(solution)/shard_map/all_to_all | solution.py:479
  83.6 0.7 last.1
  (2 shorter events, 0.1 us)
Async XLA Ops:
  1.0 4.5 %collective-permute-start = (f32[5,8,128]{2,1,0:T(8,128)S(1)}, f32[5,8,128]{2,1,0:T(8,128)S(1)}, u32[]{:S(2)}, u32[]{:S(2)}) collective-permute-start(f32[5,8,128]{2,1,0:T(8,128)S(1)} %get-tuple-element.27.near_ref), channel_id=1, source_target_pairs={{0,224},{32,64},{64,32},{96,128},{128,96},{160,192},{192,160},{224... | collective-permute-start | bytes 61448 | tf_op jit(solution)/shard_map/ppermute | solution.py:451
  3.2 2.2 %collective-permute-start.1 = (f32[5,8,128]{2,1,0:T(8,128)S(1)}, f32[5,8,128]{2,1,0:T(8,128)S(1)}, u32[]{:S(2)}, u32[]{:S(2)}) collective-permute-start(f32[5,8,128]{2,1,0:T(8,128)S(1)} %get-tuple-element.28.far_ref), channel_id=1, source_target_pairs={{0,32},{32,0},{64,96},{96,64},{128,160},{160,128},{192,224},{224,1... | collective-permute-start | bytes 61448 | tf_op jit(solution)/shard_map/ppermute | solution.py:451
  5.5 9.5 %collective-permute-start.2 = (f32[7,8,128]{2,1,0:T(8,128)S(1)}, f32[7,8,128]{2,1,0:T(8,128)S(1)}, u32[]{:S(2)}, u32[]{:S(2)}) collective-permute-start(f32[7,8,128]{2,1,0:T(8,128)S(1)} %get-tuple-element.30), channel_id=1, source_target_pairs={{0,31},{1,2},{2,1},{3,4},{4,3},{5,6},{6,5},{7,8},{8,7},{9,10},{10,... | collective-permute-start | bytes 86024 | tf_op jit(solution)/shard_map/ppermute | solution.py:451
  7.5 8.3 %collective-permute-start.3 = (f32[7,8,128]{2,1,0:T(8,128)S(1)}, f32[7,8,128]{2,1,0:T(8,128)S(1)}, u32[]{:S(2)}, u32[]{:S(2)}) collective-permute-start(f32[7,8,128]{2,1,0:T(8,128)S(1)} %get-tuple-element.31), channel_id=1, source_target_pairs={{0,1},{1,0},{2,3},{3,2},{4,5},{5,4},{6,7},{7,6},{8,9},{9,8},{10,11... | collective-permute-start | bytes 86024 | tf_op jit(solution)/shard_map/ppermute | solution.py:451
  34.9 15.1 %all-to-all-start.1 = ((bf16[32,24,128]{2,1,0:T(8,128)(2,1)}), bf16[32,24,128]{2,1,0:T(8,128)(2,1)S(1)}, u32[]{:S(2)}, u32[]{:S(2)}) async-start(bf16[32,24,128]{2,1,0:T(8,128)(2,1)} %bitcast.2), calls=%async_computation.1 | async-start | bytes 393216 | tf_op jit(solution)/shard_map/all_to_all | solution.py:479
  39.4 11.7 %collective-permute-start.4 = (f32[5,8,128]{2,1,0:T(8,128)S(1)}, f32[5,8,128]{2,1,0:T(8,128)S(1)}, u32[]{:S(2)}, u32[]{:S(2)}) collective-permute-start(f32[5,8,128]{2,1,0:T(8,128)S(1)} %get-tuple-element.35), channel_id=1, source_target_pairs={{0,31},{1,2},{2,1},{3,4},{4,3},{5,6},{6,5},{7,8},{8,7},{9,10},{10,... | collective-permute-start | bytes 61448 | tf_op jit(solution)/shard_map/ppermute | solution.py:451
  41.0 10.1 %collective-permute-start.5 = (f32[5,8,128]{2,1,0:T(8,128)S(1)}, f32[5,8,128]{2,1,0:T(8,128)S(1)}, u32[]{:S(2)}, u32[]{:S(2)}) collective-permute-start(f32[5,8,128]{2,1,0:T(8,128)S(1)} %get-tuple-element.36), channel_id=1, source_target_pairs={{0,1},{1,0},{2,3},{3,2},{4,5},{5,4},{6,7},{7,6},{8,9},{9,8},{10,11... | collective-permute-start | bytes 61448 | tf_op jit(solution)/shard_map/ppermute | solution.py:451
  50.1 4.4 %collective-permute-start.6 = (f32[3,8,128]{2,1,0:T(8,128)S(1)}, f32[3,8,128]{2,1,0:T(8,128)S(1)}, u32[]{:S(2)}, u32[]{:S(2)}) collective-permute-start(f32[3,8,128]{2,1,0:T(8,128)S(1)} %get-tuple-element.41), channel_id=1, source_target_pairs={{0,224},{32,64},{64,32},{96,128},{128,96},{160,192},{192,160},{224... | collective-permute-start | bytes 36872 | tf_op jit(solution)/shard_map/ppermute | solution.py:451
  50.2 4.3 %collective-permute-start.7 = (f32[3,8,128]{2,1,0:T(8,128)S(1)}, f32[3,8,128]{2,1,0:T(8,128)S(1)}, u32[]{:S(2)}, u32[]{:S(2)}) collective-permute-start(f32[3,8,128]{2,1,0:T(8,128)S(1)} %get-tuple-element.42), channel_id=1, source_target_pairs={{0,32},{32,0},{64,96},{96,64},{128,160},{160,128},{192,224},{224,1... | collective-permute-start | bytes 36872 | tf_op jit(solution)/shard_map/ppermute | solution.py:451

commit v6 on v5

--- a/solution.py
+++ b/solution.py
@@ -446,9 +446,18 @@
 
 
 def swapped(value, axis, odd):
-    count = lax.axis_size(axis)
-    step = [(1 if (i % 2 == 0) != odd else -1) for i in range(count)]
-    return lax.ppermute(value, axis, [(i, (i + step[i]) % count) for i in range(count)])
+    columns, owners = (lax.axis_size("space"), lax.axis_size("work"))
+    pairs = []
+    for a in range(columns):
+        for b in range(owners):
+            at, count = (b, owners) if axis == "work" else (a, columns)
+            to = at + (1 if (at % 2 == 0) != odd else -1)
+            if 0 <= to < count:
+                other = to * owners + b if axis == "space" else a * owners + to
+            else:
+                other = a * owners + (b ^ 1) if axis == "space" else (a ^ 1) * owners + b
+            pairs.append((a * owners + b, other))
+    return lax.ppermute(value, ("space", "work"), pairs)
 
 
 def body(adjoint, velocity, relaxation, uptake, fluid_mask, block_cells, owner_load, response):

time: 84.6 us -> 83.5 us (0.987)
  starting transfers between devices: 22 us -> 11.7 us
  waiting for transfers between devices: 6.98 us -> 11.9 us
  blocking collectives: 43.3 us -> 46.9 us
    ppermute x8, starting transfers between devices: 17.5 us -> 7.27 us  [swapped(): return lax.ppermute(value, ('space', 'work'), pairs)]
    all_to_all x1, waiting for transfers between devices: 4.97 us -> 9.04 us  [exchange(): lax.all_to_all(value, 'work', split_axis=0, concat_axis=0, tiled=True)]
    all_to_all x3, blocking collectives: 43.3 us -> 46.9 us  [exchange(): lax.all_to_all(value, 'work', split_axis=0, concat_axis=0, tiled=True)]
    ppermute x8, waiting for transfers between devices: 2.01 us -> 2.89 us  [swapped(): return lax.ppermute(value, ('space', 'work'), pairs)]
  transfers between devices with their start and end apart: 9 -> 9, of which waited for: 3 -> 3; matrix products, arithmetic and copies ran while one was open for 0% -> 0% of each run, Pallas kernels for 6% -> 7%
where the time goes in v6:
time: 83.5 us; the launch traced here: 82.6 us
  blocking collectives  46.9 us (56%)
  Pallas kernels  12 us (14%)
  waiting for transfers between devices  11.9 us (14%)
  starting transfers between devices  11.7 us (14%)
    all_to_all x3, blocking collectives, exchange(): lax.all_to_all(value, 'work', split_axis=0, concat_axis=0, tiled=True)  46.9 us
    all_to_all x1, waiting for transfers between devices, exchange(): lax.all_to_all(value, 'work', split_axis=0, concat_axis=0, tiled=True)  9.04 us
    ppermute x8, starting transfers between devices, swapped(): return lax.ppermute(value, ('space', 'work'), pairs)  7.27 us
    pallas_call x2, Pallas kernels, owner(): call(lambda *refs: owner_kernel(*refs, fold=fold), jax.ShapeDtypeStruct((...  4.65 us
    all_to_all x1, starting transfers between devices, exchange(): lax.all_to_all(value, 'work', split_axis=0, concat_axis=0, tiled=True)  4.43 us
    ppermute x8, waiting for transfers between devices, swapped(): return lax.ppermute(value, ('space', 'work'), pairs)  2.89 us
    pallas_call x1, Pallas kernels, body(): call(fetch_again_kernel, (pltpu.VMEM(matrices.shape, BF16), tile(10)), [H...  2.21 us
    pallas_call x1, Pallas kernels, body(): call(fetch_kernel, (pltpu.VMEM(matrices.shape, BF16), tile(6)), [HBM, VM]...  2.21 us
  transfers between devices with their start and end apart: 9, of which 3 were waited for; matrix products, arithmetic and copies ran while one was open for 0% of the time, Pallas kernels for 7%

profile of v6, /device:TPU:32, one launch (start us, length us, event | category | flops | bytes accessed | tf_op | source)
XLA Modules:
  0.0 82.6 jit_solution(3622783896969891818)
XLA Ops:
  0.0 1.0 %arrange.1 = (f32[9,8,128]{2,1,0:T(8,128)S(1)}, f32[5,8,128]{2,1,0:T(8,128)S(1)}, f32[5,8,128]{2,1,0:T(8,128)S(1)}, f32[6,8,128]{2,1,0:T(8,128)S(1)}) custom-call(f32[3,19,2,1,128]{4,3,2,1,0:T(1,128)} %field_hbm.1, bf16[3,1,2,128]{3,2,1,0:T(2,128)(2,1)} %bitcast.11, s32[2,1,128]{2,1,0:T(1,128)} %mask_hbm.1, f32[3]{0:T(128)} %relaxation_hbm.1, f32[3]{0:T(128)} %uptake_hbm.1), custom_call_target="tpu_custom_call" | custom-call | tf_op jit(solution)/shard_map/arrange/pallas_call | solution.py:491
  1.0 1.9 %collective-permute-start = (f32[5,8,128]{2,1,0:T(8,128)S(1)}, f32[5,8,128]{2,1,0:T(8,128)S(1)}, u32[]{:S(2)}, u32[]{:S(2)}) collective-permute-start(f32[5,8,128]{2,1,0:T(8,128)S(1)} %get-tuple-element.27.near_ref), channel_id=1, source_target_pairs={{0,1},{1,0},{2,3},{3,2},{4,5},{5,4},{6,7},{7,6},{8,9},{9,8},{10,11... | collective-permute-start | bytes 61448 | tf_op jit(solution)/shard_map/ppermute | solution.py:460
  2.9 0.0 collective-permute-start.1
  2.9 2.2 %fetch.1 = (bf16[32,4,128,128]{3,2,1,0:T(8,128)(2,1)S(1)}, f32[6,8,128]{2,1,0:T(8,128)S(1)}) custom-call(bf16[32,4,128,128]{3,2,1,0:T(8,128)(2,1)} %bitcast.9, f32[9,8,128]{2,1,0:T(8,128)S(1)} %get-tuple-element.26.middle_ref), custom_call_target="tpu_custom_call" | custom-call | tf_op jit(solution)/shard_map/fetch/pallas_call | solution.py:519
  5.1 0.0 collective-permute-done.first_ref
  5.1 0.0 collective-permute-done.1.second_ref
  5.2 2.1 %collective-permute-start.2 = (f32[7,8,128]{2,1,0:T(8,128)S(1)}, f32[7,8,128]{2,1,0:T(8,128)S(1)}, u32[]{:S(2)}, u32[]{:S(2)}) collective-permute-start(f32[7,8,128]{2,1,0:T(8,128)S(1)} %get-tuple-element.30), channel_id=1, source_target_pairs={{0,32},{1,2},{2,1},{3,4},{4,3},{5,6},{6,5},{7,8},{8,7},{9,10},{10,... | collective-permute-start | bytes 86024 | tf_op jit(solution)/shard_map/ppermute | solution.py:460
  7.2 0.0 collective-permute-start.3
  7.2 1.0 %slots.1.slots_ref = f32[32,16,128]{2,1,0:T(8,128)S(1)} custom-call(s32[1,1,32,4,128]{4,3,2,1,0:T(4,128)} %cells_hbm.1, s32[1,1,32]{2,1,0:T(1,128)} %load_hbm.1), custom_call_target="tpu_custom_call" | custom-call | tf_op jit(solution)/shard_map/slots/pallas_call | solution.py:508
  8.2 1.0 %collective-permute-done.2.one_ref = f32[7,8,128]{2,1,0:T(8,128)S(1)} collective-permute-done((f32[7,8,128]{2,1,0:T(8,128)S(1)}, f32[7,8,128]{2,1,0:T(8,128)S(1)}, u32[]{:S(2)}, u32[]{:S(2)}) %collective-permute-start.2) | collective-permute-done | bytes 28704 | tf_op jit(solution)/shard_map/ppermute | solution.py:460
  9.2 1.9 %collective-permute-done.3.two_ref = f32[7,8,128]{2,1,0:T(8,128)S(1)} collective-permute-done((f32[7,8,128]{2,1,0:T(8,128)S(1)}, f32[7,8,128]{2,1,0:T(8,128)S(1)}, u32[]{:S(2)}, u32[]{:S(2)}) %collective-permute-start.3) | collective-permute-done | bytes 28704 | tf_op jit(solution)/shard_map/ppermute | solution.py:460
  11.1 0.1 first.1
  11.2 19.8 %all_to_all.20.refs_0_.incoming_ref = bf16[32,16,128]{2,1,0:T(8,128)(2,1)S(1)} all-to-all(bf16[32,16,128]{2,1,0:T(8,128)(2,1)S(1)} %get-tuple-element.33.refs_1_), channel_id=1, replica_groups=mesh['space'=8,'work'=32] {'work'}, dimensions={0} | all-to-all | bytes 262144 | tf_op jit(solution)/shard_map/all_to_all | solution.py:488
  31.1 2.7 %owner_fold.1 = bf16[768,128]{1,0:T(8,128)(2,1)} custom-call(bf16[32,16,128]{2,1,0:T(8,128)(2,1)S(1)} %all_to_all.20.refs_0_.incoming_ref, bf16[32,16,128]{2,1,0:T(8,128)(2,1)S(1)} %get-tuple-element.33.refs_1_, bf16[32,4,128,128]{3,2,1,0:T(8,128)(2,1)S(1)} %get-tuple-element.38.refs_2_), custom_call_target="tpu_custom_call" | custom-call | tf_op jit(solution)/shard_map/owner_fold/pallas_call | solution.py:475
  33.8 4.4 %all-to-all-start.1 = ((bf16[32,24,128]{2,1,0:T(8,128)(2,1)}), bf16[32,24,128]{2,1,0:T(8,128)(2,1)S(1)}, u32[]{:S(2)}, u32[]{:S(2)}) async-start(bf16[32,24,128]{2,1,0:T(8,128)(2,1)} %bitcast.2), calls=%async_computation.1 | async-start | bytes 393216 | tf_op jit(solution)/shard_map/all_to_all | solution.py:488
  38.2 1.6 %collective-permute-start.4 = (f32[5,8,128]{2,1,0:T(8,128)S(1)}, f32[5,8,128]{2,1,0:T(8,128)S(1)}, u32[]{:S(2)}, u32[]{:S(2)}) collective-permute-start(f32[5,8,128]{2,1,0:T(8,128)S(1)} %get-tuple-element.35), channel_id=1, source_target_pairs={{0,32},{1,2},{2,1},{3,4},{4,3},{5,6},{6,5},{7,8},{8,7},{9,10},{10,... | collective-permute-start | bytes 61448 | tf_op jit(solution)/shard_map/ppermute | solution.py:460
  39.8 0.0 collective-permute-start.5
  39.8 9.0 %all-to-all-done.1 = bf16[32,24,128]{2,1,0:T(8,128)(2,1)S(1)} async-done(((bf16[32,24,128]{2,1,0:T(8,128)(2,1)}), bf16[32,24,128]{2,1,0:T(8,128)(2,1)S(1)}, u32[]{:S(2)}, u32[]{:S(2)}) %all-to-all-start.1) | async-done | bytes 196640 | tf_op jit(solution)/shard_map/all_to_all | solution.py:488
  48.8 0.4 collective-permute-start.6
  49.3 1.3 %collective-permute-start.7 = (f32[3,8,128]{2,1,0:T(8,128)S(1)}, f32[3,8,128]{2,1,0:T(8,128)S(1)}, u32[]{:S(2)}, u32[]{:S(2)}) collective-permute-start(f32[3,8,128]{2,1,0:T(8,128)S(1)} %get-tuple-element.42), channel_id=1, source_target_pairs={{0,32},{1,33},{2,34},{3,35},{4,36},{5,37},{6,38},{7,39},{8,40},{9,... | collective-permute-start | bytes 36872 | tf_op jit(solution)/shard_map/ppermute | solution.py:460
  50.5 0.0 collective-permute-done.4.third_ref
  50.5 0.0 collective-permute-done.5.fourth_ref
  50.5 2.2 %fetch_again.1 = (bf16[32,4,128,128]{3,2,1,0:T(8,128)(2,1)S(1)}, f32[10,8,128]{2,1,0:T(8,128)S(1)}) custom-call(bf16[32,4,128,128]{3,2,1,0:T(8,128)(2,1)} %bitcast.10, f32[5,8,128]{2,1,0:T(8,128)S(1)} %collective-permute-done.4.third_ref, f32[5,8,128]{2,1,0:T(8,128)S(1)} %collective-permute-done.5.fourth_ref), custom_call_target="tpu_custom_call" | custom-call | tf_op jit(solution)/shard_map/fetch_again/pallas_call | solution.py:539
  52.8 0.0 collective-permute-done.6.first_ref
  52.8 0.0 collective-permute-done.7.second_ref
  52.8 0.1 second.1
  52.9 13.3 %all_to_all.21 = bf16[32,8,128]{2,1,0:T(8,128)(2,1)S(1)} all-to-all(bf16[32,8,128]{2,1,0:T(8,128)(2,1)S(1)} %bitcast.8), channel_id=1, replica_groups=mesh['space'=8,'work'=32] {'work'}, dimensions={0} | all-to-all | bytes 131072 | tf_op jit(solution)/shard_map/all_to_all | solution.py:488
  66.2 1.9 %owner.1 = bf16[32,16,128]{2,1,0:T(8,128)(2,1)S(1)} custom-call(bf16[32,16,128]{2,1,0:T(8,128)(2,1)S(1)} %all_to_all.20.refs_0_.incoming_ref, bf16[256,128]{1,0:T(8,128)(2,1)S(1)} %bitcast.7, bf16[32,4,128,128]{3,2,1,0:T(8,128)(2,1)S(1)} %get-tuple-element.44.refs_2_), custom_call_target="tpu_custom_call" | custom-call | tf_op jit(solution)/shard_map/owner/pallas_call | solution.py:475
  68.2 13.8 %all_to_all.22.returned_ref = bf16[32,16,128]{2,1,0:T(8,128)(2,1)S(1)} all-to-all(bf16[32,16,128]{2,1,0:T(8,128)(2,1)S(1)} %owner.1), channel_id=1, replica_groups=mesh['space'=8,'work'=32] {'work'}, dimensions={0} | all-to-all | bytes 262144 | tf_op jit(solution)/shard_map/all_to_all | solution.py:488
  81.9 0.7 last.1
  (2 shorter events, 0.1 us)
Async XLA Ops:
  1.0 4.2 %collective-permute-start = (f32[5,8,128]{2,1,0:T(8,128)S(1)}, f32[5,8,128]{2,1,0:T(8,128)S(1)}, u32[]{:S(2)}, u32[]{:S(2)}) collective-permute-start(f32[5,8,128]{2,1,0:T(8,128)S(1)} %get-tuple-element.27.near_ref), channel_id=1, source_target_pairs={{0,1},{1,0},{2,3},{3,2},{4,5},{5,4},{6,7},{7,6},{8,9},{9,8},{10,11... | collective-permute-start | bytes 61448 | tf_op jit(solution)/shard_map/ppermute | solution.py:460
  2.9 2.2 %collective-permute-start.1 = (f32[5,8,128]{2,1,0:T(8,128)S(1)}, f32[5,8,128]{2,1,0:T(8,128)S(1)}, u32[]{:S(2)}, u32[]{:S(2)}) collective-permute-start(f32[5,8,128]{2,1,0:T(8,128)S(1)} %get-tuple-element.28.far_ref), channel_id=1, source_target_pairs={{0,32},{1,33},{2,34},{3,35},{4,36},{5,37},{6,38},{7,39},{8,40},{9,... | collective-permute-start | bytes 61448 | tf_op jit(solution)/shard_map/ppermute | solution.py:460
  5.2 4.1 %collective-permute-start.2 = (f32[7,8,128]{2,1,0:T(8,128)S(1)}, f32[7,8,128]{2,1,0:T(8,128)S(1)}, u32[]{:S(2)}, u32[]{:S(2)}) collective-permute-start(f32[7,8,128]{2,1,0:T(8,128)S(1)} %get-tuple-element.30), channel_id=1, source_target_pairs={{0,32},{1,2},{2,1},{3,4},{4,3},{5,6},{6,5},{7,8},{8,7},{9,10},{10,... | collective-permute-start | bytes 86024 | tf_op jit(solution)/shard_map/ppermute | solution.py:460
  7.2 3.9 %collective-permute-start.3 = (f32[7,8,128]{2,1,0:T(8,128)S(1)}, f32[7,8,128]{2,1,0:T(8,128)S(1)}, u32[]{:S(2)}, u32[]{:S(2)}) collective-permute-start(f32[7,8,128]{2,1,0:T(8,128)S(1)} %get-tuple-element.31), channel_id=1, source_target_pairs={{0,1},{1,0},{2,3},{3,2},{4,5},{5,4},{6,7},{7,6},{8,9},{9,8},{10,11... | collective-permute-start | bytes 86024 | tf_op jit(solution)/shard_map/ppermute | solution.py:460
  33.8 15.0 %all-to-all-start.1 = ((bf16[32,24,128]{2,1,0:T(8,128)(2,1)}), bf16[32,24,128]{2,1,0:T(8,128)(2,1)S(1)}, u32[]{:S(2)}, u32[]{:S(2)}) async-start(bf16[32,24,128]{2,1,0:T(8,128)(2,1)} %bitcast.2), calls=%async_computation.1 | async-start | bytes 393216 | tf_op jit(solution)/shard_map/all_to_all | solution.py:488
  38.2 12.3 %collective-permute-start.4 = (f32[5,8,128]{2,1,0:T(8,128)S(1)}, f32[5,8,128]{2,1,0:T(8,128)S(1)}, u32[]{:S(2)}, u32[]{:S(2)}) collective-permute-start(f32[5,8,128]{2,1,0:T(8,128)S(1)} %get-tuple-element.35), channel_id=1, source_target_pairs={{0,32},{1,2},{2,1},{3,4},{4,3},{5,6},{6,5},{7,8},{8,7},{9,10},{10,... | collective-permute-start | bytes 61448 | tf_op jit(solution)/shard_map/ppermute | solution.py:460
  39.8 10.8 %collective-permute-start.5 = (f32[5,8,128]{2,1,0:T(8,128)S(1)}, f32[5,8,128]{2,1,0:T(8,128)S(1)}, u32[]{:S(2)}, u32[]{:S(2)}) collective-permute-start(f32[5,8,128]{2,1,0:T(8,128)S(1)} %get-tuple-element.36), channel_id=1, source_target_pairs={{0,1},{1,0},{2,3},{3,2},{4,5},{5,4},{6,7},{7,6},{8,9},{9,8},{10,11... | collective-permute-start | bytes 61448 | tf_op jit(solution)/shard_map/ppermute | solution.py:460
  48.8 3.9 %collective-permute-start.6 = (f32[3,8,128]{2,1,0:T(8,128)S(1)}, f32[3,8,128]{2,1,0:T(8,128)S(1)}, u32[]{:S(2)}, u32[]{:S(2)}) collective-permute-start(f32[3,8,128]{2,1,0:T(8,128)S(1)} %get-tuple-element.41), channel_id=1, source_target_pairs={{0,1},{1,0},{2,3},{3,2},{4,5},{5,4},{6,7},{7,6},{8,9},{9,8},{10,11... | collective-permute-start | bytes 36872 | tf_op jit(solution)/shard_map/ppermute | solution.py:460
  49.3 3.5 %collective-permute-start.7 = (f32[3,8,128]{2,1,0:T(8,128)S(1)}, f32[3,8,128]{2,1,0:T(8,128)S(1)}, u32[]{:S(2)}, u32[]{:S(2)}) collective-permute-start(f32[3,8,128]{2,1,0:T(8,128)S(1)} %get-tuple-element.42), channel_id=1, source_target_pairs={{0,32},{1,33},{2,34},{3,35},{4,36},{5,37},{6,38},{7,39},{8,40},{9,... | collective-permute-start | bytes 36872 | tf_op jit(solution)/shard_map/ppermute | solution.py:460

commit v7 on v6

--- a/solution.py
+++ b/solution.py
@@ -96,7 +96,7 @@
 
 
 def near_is_upper(axis):
-    return lax.axis_index(axis) % 2 == 1
+    return lax.axis_index(axis) % 2 == (1 if axis == "work" else 0)
 
 
 def arrange_kernel(
@@ -152,9 +152,9 @@
     return copies
 
 
-def fetch_kernel(response_hbm, middle_ref, response_ref, sides_ref, done):
+def fetch_kernel(response_hbm, middle_ref, response_ref, own_ref, done):
     copies = start_fetch(response_hbm, response_ref, done)
-    sides_ref[...] = middle_ref[3:9]
+    own_ref[...] = middle_ref[0:3]
     for copy in copies:
         copy.wait()
 
@@ -171,11 +171,12 @@
         copy.wait()
 
 
-def slots_kernel(cells_hbm, load_hbm, slots_ref, cells_ref, load_ref, done):
+def slots_kernel(cells_hbm, load_hbm, middle_ref, slots_ref, sides_ref, cells_ref, load_ref, done):
     pairs = ((cells_hbm, cells_ref), (load_hbm, load_ref))
     copies = [pltpu.make_async_copy(source, target, done.at[n]) for n, (source, target) in enumerate(pairs)]
     for copy in copies:
         copy.start()
+    sides_ref[...] = middle_ref[3:9]
     for copy in copies:
         copy.wait()
     rows = rows_of()
@@ -469,7 +470,7 @@
         return pltpu.with_memory_space_constraint(value, pltpu.HBM)
 
     def both_ways(near, far, axis):
-        return swapped(near, axis, True), swapped(far, axis, False)
+        return swapped(near, axis, axis == "work"), swapped(far, axis, axis != "work")
 
     def owner(incoming, densities, fetched, fold):
         return call(
@@ -505,20 +506,20 @@
         ],
     )(*map(outside, (adjoint, speeds, fluid_mask, relaxation, uptake)))
     first, second = both_ways(near, far, "space")
-    slots = call(
+    slots, sides = call(
         slots_kernel,
-        tile(owners, rows=16),
-        [HBM] * 2,
+        (tile(owners, rows=16), tile(6)),
+        [HBM, HBM, VM],
         "slots",
         scratch_shapes=[
             pltpu.VMEM(block_cells.shape, jnp.int32),
             pltpu.SMEM(owner_load.shape, jnp.int32),
             pltpu.SemaphoreType.DMA((2,)),
         ],
-    )(*map(outside, (block_cells, owner_load)))
-    fetched, sides = call(
+    )(outside(block_cells), outside(owner_load), middle)
+    fetched, own = call(
         fetch_kernel,
-        (pltpu.VMEM(matrices.shape, BF16), tile(6)),
+        (pltpu.VMEM(matrices.shape, BF16), tile(3)),
         [HBM, VM],
         "fetch",
         scratch_shapes=[pltpu.SemaphoreType.DMA((CHUNKS,))],
@@ -527,7 +528,7 @@
     one, two = both_ways(one, two, "work")
     stay, third, fourth, gain, payload = call(
         first_kernel, (tile(9), tile(5), tile(5), tile(4), payload_shape), [VM] * 9, "first"
-    )(middle, near, far, first, second, one, two, fixed, slots)
+    )(own, near, far, first, second, one, two, fixed, slots)
     incoming = exchange(payload)
     third, fourth = both_ways(third, fourth, "work")
     returned = owner(incoming, payload, fetched, True).reshape(owners, 24, LANES)

time: 83.5 us -> 82.9 us (level)
  starting transfers between devices: 11.7 us -> 10.7 us
    ppermute x8, starting transfers between devices: 7.27 us -> 6.2 us  [swapped(): return lax.ppermute(value, ('space', 'work'), pairs)]
  transfers between devices with their start and end apart: 9 -> 9, of which waited for: 3 -> 4; matrix products, arithmetic and copies ran while one was open for 0% -> 0% of each run, Pallas kernels for 7% -> 7%
where the time goes in v7:
time: 82.9 us; the launch traced here: 82.6 us
  blocking collectives  47.2 us (57%)
  waiting for transfers between devices  12.7 us (15%)
  Pallas kernels  11.9 us (14%)
  starting transfers between devices  10.7 us (13%)
    all_to_all x3, blocking collectives, exchange(): lax.all_to_all(value, 'work', split_axis=0, concat_axis=0, tiled=True)  47.2 us
    all_to_all x1, waiting for transfers between devices, exchange(): lax.all_to_all(value, 'work', split_axis=0, concat_axis=0, tiled=True)  9.06 us
    ppermute x8, starting transfers between devices, swapped(): return lax.ppermute(value, ('space', 'work'), pairs)  6.2 us
    pallas_call x2, Pallas kernels, owner(): call(lambda *refs: owner_kernel(*refs, fold=fold), jax.ShapeDtypeStruct((...  4.64 us
    all_to_all x1, starting transfers between devices, exchange(): lax.all_to_all(value, 'work', split_axis=0, concat_axis=0, tiled=True)  4.48 us
    ppermute x8, waiting for transfers between devices, swapped(): return lax.ppermute(value, ('space', 'work'), pairs)  3.62 us
    pallas_call x1, Pallas kernels, body(): call(fetch_again_kernel, (pltpu.VMEM(matrices.shape, BF16), tile(10)), [H...  2.21 us
    pallas_call x1, Pallas kernels, body(): call(fetch_kernel, (pltpu.VMEM(matrices.shape, BF16), tile(3)), [HBM, VM]...  2.21 us
  transfers between devices with their start and end apart: 9, of which 4 were waited for; matrix products, arithmetic and copies ran while one was open for 0% of the time, Pallas kernels for 7%

profile of v7, /device:TPU:32, one launch (start us, length us, event | category | flops | bytes accessed | tf_op | source)
XLA Modules:
  0.0 82.6 jit_solution(263893541262603196)
XLA Ops:
  0.0 1.0 %arrange.1 = (f32[9,8,128]{2,1,0:T(8,128)S(1)}, f32[5,8,128]{2,1,0:T(8,128)S(1)}, f32[5,8,128]{2,1,0:T(8,128)S(1)}, f32[6,8,128]{2,1,0:T(8,128)S(1)}) custom-call(f32[3,19,2,1,128]{4,3,2,1,0:T(1,128)} %field_hbm.1, bf16[3,1,2,128]{3,2,1,0:T(2,128)(2,1)} %bitcast.11, s32[2,1,128]{2,1,0:T(1,128)} %mask_hbm.1, f32[3]{0:T(128)} %relaxation_hbm.1, f32[3]{0:T(128)} %uptake_hbm.1), custom_call_target="tpu_custom_call" | custom-call | tf_op jit(solution)/shard_map/arrange/pallas_call | solution.py:492
  1.0 0.1 collective-permute-start
  1.1 1.9 %collective-permute-start.1 = (f32[5,8,128]{2,1,0:T(8,128)S(1)}, f32[5,8,128]{2,1,0:T(8,128)S(1)}, u32[]{:S(2)}, u32[]{:S(2)}) collective-permute-start(f32[5,8,128]{2,1,0:T(8,128)S(1)} %get-tuple-element.31.far_ref), channel_id=1, source_target_pairs={{0,1},{1,0},{2,3},{3,2},{4,5},{5,4},{6,7},{7,6},{8,9},{9,8},{10,11... | collective-permute-start | bytes 61448 | tf_op jit(solution)/shard_map/ppermute | solution.py:461
  3.0 1.0 %slots.1 = (f32[32,16,128]{2,1,0:T(8,128)S(1)}, f32[6,8,128]{2,1,0:T(8,128)S(1)}) custom-call(s32[1,1,32,4,128]{4,3,2,1,0:T(4,128)} %cells_hbm.1, s32[1,1,32]{2,1,0:T(1,128)} %load_hbm.1, f32[9,8,128]{2,1,0:T(8,128)S(1)} %get-tuple-element.28.middle_ref), custom_call_target="tpu_custom_call" | custom-call | tf_op jit(solution)/shard_map/slots/pallas_call | solution.py:509
  4.0 0.0 collective-permute-done.first_ref
  4.0 0.9 %collective-permute-done.1.second_ref = f32[5,8,128]{2,1,0:T(8,128)S(1)} collective-permute-done((f32[5,8,128]{2,1,0:T(8,128)S(1)}, f32[5,8,128]{2,1,0:T(8,128)S(1)}, u32[]{:S(2)}, u32[]{:S(2)}) %collective-permute-start.1) | collective-permute-done | bytes 20512 | tf_op jit(solution)/shard_map/ppermute | solution.py:461
  4.9 2.0 %collective-permute-start.2 = (f32[7,8,128]{2,1,0:T(8,128)S(1)}, f32[7,8,128]{2,1,0:T(8,128)S(1)}, u32[]{:S(2)}, u32[]{:S(2)}) collective-permute-start(f32[7,8,128]{2,1,0:T(8,128)S(1)} %get-tuple-element.33), channel_id=1, source_target_pairs={{0,32},{1,2},{2,1},{3,4},{4,3},{5,6},{6,5},{7,8},{8,7},{9,10},{10,... | collective-permute-start | bytes 86024 | tf_op jit(solution)/shard_map/ppermute | solution.py:461
  7.0 0.1 collective-permute-start.3
  7.0 2.2 %fetch.1 = (bf16[32,4,128,128]{3,2,1,0:T(8,128)(2,1)S(1)}, f32[3,8,128]{2,1,0:T(8,128)S(1)}) custom-call(bf16[32,4,128,128]{3,2,1,0:T(8,128)(2,1)} %bitcast.9, f32[9,8,128]{2,1,0:T(8,128)S(1)} %get-tuple-element.28.middle_ref), custom_call_target="tpu_custom_call" | custom-call | tf_op jit(solution)/shard_map/fetch/pallas_call | solution.py:520
  9.2 0.0 collective-permute-done.2.one_ref
  9.3 1.6 %collective-permute-done.3.two_ref = f32[7,8,128]{2,1,0:T(8,128)S(1)} collective-permute-done((f32[7,8,128]{2,1,0:T(8,128)S(1)}, f32[7,8,128]{2,1,0:T(8,128)S(1)}, u32[]{:S(2)}, u32[]{:S(2)}) %collective-permute-start.3) | collective-permute-done | bytes 28704 | tf_op jit(solution)/shard_map/ppermute | solution.py:461
  10.8 0.1 first.1
  10.9 20.1 %all_to_all.20.refs_0_.incoming_ref = bf16[32,16,128]{2,1,0:T(8,128)(2,1)S(1)} all-to-all(bf16[32,16,128]{2,1,0:T(8,128)(2,1)S(1)} %get-tuple-element.37.refs_1_), channel_id=1, replica_groups=mesh['space'=8,'work'=32] {'work'}, dimensions={0} | all-to-all | bytes 262144 | tf_op jit(solution)/shard_map/all_to_all | solution.py:489
  31.1 2.7 %owner_fold.1 = bf16[768,128]{1,0:T(8,128)(2,1)} custom-call(bf16[32,16,128]{2,1,0:T(8,128)(2,1)S(1)} %all_to_all.20.refs_0_.incoming_ref, bf16[32,16,128]{2,1,0:T(8,128)(2,1)S(1)} %get-tuple-element.37.refs_1_, bf16[32,4,128,128]{3,2,1,0:T(8,128)(2,1)S(1)} %get-tuple-element.42.refs_2_), custom_call_target="tpu_custom_call" | custom-call | tf_op jit(solution)/shard_map/owner_fold/pallas_call | solution.py:476
  33.8 4.5 %all-to-all-start.1 = ((bf16[32,24,128]{2,1,0:T(8,128)(2,1)}), bf16[32,24,128]{2,1,0:T(8,128)(2,1)S(1)}, u32[]{:S(2)}, u32[]{:S(2)}) async-start(bf16[32,24,128]{2,1,0:T(8,128)(2,1)} %bitcast.2), calls=%async_computation.1 | async-start | bytes 393216 | tf_op jit(solution)/shard_map/all_to_all | solution.py:489
  38.2 1.6 %collective-permute-start.4 = (f32[5,8,128]{2,1,0:T(8,128)S(1)}, f32[5,8,128]{2,1,0:T(8,128)S(1)}, u32[]{:S(2)}, u32[]{:S(2)}) collective-permute-start(f32[5,8,128]{2,1,0:T(8,128)S(1)} %get-tuple-element.39), channel_id=1, source_target_pairs={{0,32},{1,2},{2,1},{3,4},{4,3},{5,6},{6,5},{7,8},{8,7},{9,10},{10,... | collective-permute-start | bytes 61448 | tf_op jit(solution)/shard_map/ppermute | solution.py:461
  39.8 0.0 collective-permute-start.5
  39.8 9.1 %all-to-all-done.1 = bf16[32,24,128]{2,1,0:T(8,128)(2,1)S(1)} async-done(((bf16[32,24,128]{2,1,0:T(8,128)(2,1)}), bf16[32,24,128]{2,1,0:T(8,128)(2,1)S(1)}, u32[]{:S(2)}, u32[]{:S(2)}) %all-to-all-start.1) | async-done | bytes 196640 | tf_op jit(solution)/shard_map/all_to_all | solution.py:489
  48.9 0.1 collective-permute-start.6
  49.0 0.4 collective-permute-start.7
  49.5 0.0 collective-permute-done.4.third_ref
  49.5 0.0 collective-permute-done.5.fourth_ref
  49.5 2.2 %fetch_again.1 = (bf16[32,4,128,128]{3,2,1,0:T(8,128)(2,1)S(1)}, f32[10,8,128]{2,1,0:T(8,128)S(1)}) custom-call(bf16[32,4,128,128]{3,2,1,0:T(8,128)(2,1)} %bitcast.10, f32[5,8,128]{2,1,0:T(8,128)S(1)} %collective-permute-done.4.third_ref, f32[5,8,128]{2,1,0:T(8,128)S(1)} %collective-permute-done.5.fourth_ref), custom_call_target="tpu_custom_call" | custom-call | tf_op jit(solution)/shard_map/fetch_again/pallas_call | solution.py:540
  51.7 0.0 collective-permute-done.6.first_ref
  51.7 1.1 %collective-permute-done.7.second_ref = f32[3,8,128]{2,1,0:T(8,128)S(1)} collective-permute-done((f32[3,8,128]{2,1,0:T(8,128)S(1)}, f32[3,8,128]{2,1,0:T(8,128)S(1)}, u32[]{:S(2)}, u32[]{:S(2)}) %collective-permute-start.7) | collective-permute-done | bytes 12320 | tf_op jit(solution)/shard_map/ppermute | solution.py:461
  52.8 0.1 second.1
  52.9 13.3 %all_to_all.21 = bf16[32,8,128]{2,1,0:T(8,128)(2,1)S(1)} all-to-all(bf16[32,8,128]{2,1,0:T(8,128)(2,1)S(1)} %bitcast.8), channel_id=1, replica_groups=mesh['space'=8,'work'=32] {'work'}, dimensions={0} | all-to-all | bytes 131072 | tf_op jit(solution)/shard_map/all_to_all | solution.py:489
  66.2 1.9 %owner.1 = bf16[32,16,128]{2,1,0:T(8,128)(2,1)S(1)} custom-call(bf16[32,16,128]{2,1,0:T(8,128)(2,1)S(1)} %all_to_all.20.refs_0_.incoming_ref, bf16[256,128]{1,0:T(8,128)(2,1)S(1)} %bitcast.7, bf16[32,4,128,128]{3,2,1,0:T(8,128)(2,1)S(1)} %get-tuple-element.48.refs_2_), custom_call_target="tpu_custom_call" | custom-call | tf_op jit(solution)/shard_map/owner/pallas_call | solution.py:476
  68.2 13.7 %all_to_all.22.returned_ref = bf16[32,16,128]{2,1,0:T(8,128)(2,1)S(1)} all-to-all(bf16[32,16,128]{2,1,0:T(8,128)(2,1)S(1)} %owner.1), channel_id=1, replica_groups=mesh['space'=8,'work'=32] {'work'}, dimensions={0} | all-to-all | bytes 262144 | tf_op jit(solution)/shard_map/all_to_all | solution.py:489
  81.9 0.7 last.1
  (2 shorter events, 0.1 us)
Async XLA Ops:
  1.0 3.0 %collective-permute-start = (f32[5,8,128]{2,1,0:T(8,128)S(1)}, f32[5,8,128]{2,1,0:T(8,128)S(1)}, u32[]{:S(2)}, u32[]{:S(2)}) collective-permute-start(f32[5,8,128]{2,1,0:T(8,128)S(1)} %get-tuple-element.30.near_ref), channel_id=1, source_target_pairs={{0,32},{1,33},{2,34},{3,35},{4,36},{5,37},{6,38},{7,39},{8,40},{9,... | collective-permute-start | bytes 61448 | tf_op jit(solution)/shard_map/ppermute | solution.py:461
  1.1 3.9 %collective-permute-start.1 = (f32[5,8,128]{2,1,0:T(8,128)S(1)}, f32[5,8,128]{2,1,0:T(8,128)S(1)}, u32[]{:S(2)}, u32[]{:S(2)}) collective-permute-start(f32[5,8,128]{2,1,0:T(8,128)S(1)} %get-tuple-element.31.far_ref), channel_id=1, source_target_pairs={{0,1},{1,0},{2,3},{3,2},{4,5},{5,4},{6,7},{7,6},{8,9},{9,8},{10,11... | collective-permute-start | bytes 61448 | tf_op jit(solution)/shard_map/ppermute | solution.py:461
  4.9 4.3 %collective-permute-start.2 = (f32[7,8,128]{2,1,0:T(8,128)S(1)}, f32[7,8,128]{2,1,0:T(8,128)S(1)}, u32[]{:S(2)}, u32[]{:S(2)}) collective-permute-start(f32[7,8,128]{2,1,0:T(8,128)S(1)} %get-tuple-element.33), channel_id=1, source_target_pairs={{0,32},{1,2},{2,1},{3,4},{4,3},{5,6},{6,5},{7,8},{8,7},{9,10},{10,... | collective-permute-start | bytes 86024 | tf_op jit(solution)/shard_map/ppermute | solution.py:461
  7.0 3.9 %collective-permute-start.3 = (f32[7,8,128]{2,1,0:T(8,128)S(1)}, f32[7,8,128]{2,1,0:T(8,128)S(1)}, u32[]{:S(2)}, u32[]{:S(2)}) collective-permute-start(f32[7,8,128]{2,1,0:T(8,128)S(1)} %get-tuple-element.34), channel_id=1, source_target_pairs={{0,1},{1,0},{2,3},{3,2},{4,5},{5,4},{6,7},{7,6},{8,9},{9,8},{10,11... | collective-permute-start | bytes 86024 | tf_op jit(solution)/shard_map/ppermute | solution.py:461
  33.8 15.1 %all-to-all-start.1 = ((bf16[32,24,128]{2,1,0:T(8,128)(2,1)}), bf16[32,24,128]{2,1,0:T(8,128)(2,1)S(1)}, u32[]{:S(2)}, u32[]{:S(2)}) async-start(bf16[32,24,128]{2,1,0:T(8,128)(2,1)} %bitcast.2), calls=%async_computation.1 | async-start | bytes 393216 | tf_op jit(solution)/shard_map/all_to_all | solution.py:489
  38.2 11.2 %collective-permute-start.4 = (f32[5,8,128]{2,1,0:T(8,128)S(1)}, f32[5,8,128]{2,1,0:T(8,128)S(1)}, u32[]{:S(2)}, u32[]{:S(2)}) collective-permute-start(f32[5,8,128]{2,1,0:T(8,128)S(1)} %get-tuple-element.39), channel_id=1, source_target_pairs={{0,32},{1,2},{2,1},{3,4},{4,3},{5,6},{6,5},{7,8},{8,7},{9,10},{10,... | collective-permute-start | bytes 61448 | tf_op jit(solution)/shard_map/ppermute | solution.py:461
  39.8 9.7 %collective-permute-start.5 = (f32[5,8,128]{2,1,0:T(8,128)S(1)}, f32[5,8,128]{2,1,0:T(8,128)S(1)}, u32[]{:S(2)}, u32[]{:S(2)}) collective-permute-start(f32[5,8,128]{2,1,0:T(8,128)S(1)} %get-tuple-element.40), channel_id=1, source_target_pairs={{0,1},{1,0},{2,3},{3,2},{4,5},{5,4},{6,7},{7,6},{8,9},{9,8},{10,11... | collective-permute-start | bytes 61448 | tf_op jit(solution)/shard_map/ppermute | solution.py:461
  48.9 2.8 %collective-permute-start.6 = (f32[3,8,128]{2,1,0:T(8,128)S(1)}, f32[3,8,128]{2,1,0:T(8,128)S(1)}, u32[]{:S(2)}, u32[]{:S(2)}) collective-permute-start(f32[3,8,128]{2,1,0:T(8,128)S(1)} %get-tuple-element.45), channel_id=1, source_target_pairs={{0,32},{1,33},{2,34},{3,35},{4,36},{5,37},{6,38},{7,39},{8,40},{9,... | collective-permute-start | bytes 36872 | tf_op jit(solution)/shard_map/ppermute | solution.py:461
  49.0 3.8 %collective-permute-start.7 = (f32[3,8,128]{2,1,0:T(8,128)S(1)}, f32[3,8,128]{2,1,0:T(8,128)S(1)}, u32[]{:S(2)}, u32[]{:S(2)}) collective-permute-start(f32[3,8,128]{2,1,0:T(8,128)S(1)} %get-tuple-element.46), channel_id=1, source_target_pairs={{0,1},{1,0},{2,3},{3,2},{4,5},{5,4},{6,7},{7,6},{8,9},{9,8},{10,11... | collective-permute-start | bytes 36872 | tf_op jit(solution)/shard_map/ppermute | solution.py:461

commit v8 on v7

--- a/solution.py
+++ b/solution.py
@@ -194,16 +194,18 @@
     has_right, has_left, _, _ = edges()
     upper = near_is_upper("space")
     upper_row = near_is_upper("work")
+    first_half = rows_of() < 4
     pieces = {}
     for sign in (1, -1):
         p, m = (PLACE[(1, sign, 0)], PLACE[(-1, sign, 0)])
         pieces[sign] = [sides_ref[PLACE[(0, sign, cz)] - 3] for cz in (0, 1, -1)] + [
-            jnp.where(upper, far_ref[p], near_ref[p]),
+            jnp.where(
+                first_half, jnp.where(upper, near_ref[m], far_ref[m]), jnp.where(upper, far_ref[p], near_ref[p])
+            ),
             jnp.where(has_right, jnp.where(upper, first_ref[p], second_ref[p]), 0.0),
-            jnp.where(upper, near_ref[m], far_ref[m]),
             jnp.where(has_left, jnp.where(upper, second_ref[m], first_ref[m]), 0.0),
         ]
-    for n in range(7):
+    for n in range(6):
         one_ref[n] = jnp.where(upper_row, pieces[-1][n], pieces[1][n])
         two_ref[n] = jnp.where(upper_row, pieces[1][n], pieces[-1][n])
 
@@ -230,8 +232,8 @@
     minus = [jnp.where(upper, near_ref[n], far_ref[n]) for n in range(3)]
     right = [jnp.where(has_right, jnp.where(upper, first_ref[n], second_ref[n]), 0.0) for n in range(3)]
     left = [jnp.where(has_left, jnp.where(upper, second_ref[n], first_ref[n]), 0.0) for n in range(3)]
-    above = [jnp.where(has_above, jnp.where(upper_row, one_ref[n], two_ref[n]), 0.0) for n in range(7)]
-    below = [jnp.where(has_below, jnp.where(upper_row, two_ref[n], one_ref[n]), 0.0) for n in range(7)]
+    above = [jnp.where(has_above, jnp.where(upper_row, one_ref[n], two_ref[n]), 0.0) for n in range(6)]
+    below = [jnp.where(has_below, jnp.where(upper_row, two_ref[n], one_ref[n]), 0.0) for n in range(6)]
     pulled = {}
     for n, cz in enumerate((0, 1, -1)):
         pulled[(0, 0, cz)] = along(middle_ref[PLACE[(0, 0, cz)]], cz)
@@ -241,7 +243,7 @@
         for n, cz in enumerate((0, 1, -1)):
             pulled[(0, sign, cz)] = along(side[n], cz)
         pulled[(1, sign, 0)] = jnp.where(first_half, half(side[3]), half(side[4]))
-        pulled[(-1, sign, 0)] = jnp.where(first_half, half(side[6]), half(side[5]))
+        pulled[(-1, sign, 0)] = jnp.where(first_half, half(side[5]), half(side[3]))
     pulled = {c: pulled[c] for c in DIRECTIONS}
     density = moment(pulled, [fixed_ref[3 + c] for c in range(3)])
     write_payload(payload_ref, density, slots_ref)
@@ -256,7 +258,7 @@
         stay_ref[6 + n] = to_left * along(left[n], cz)
     sends = {}
     for sign, side in ((1, above), (-1, below)):
-        sends[sign] = [here * pulled[(0, sign, cz)] for cz in (0, 1, -1)] + [to_right * side[4], to_left * side[6]]
+        sends[sign] = [here * pulled[(0, sign, cz)] for cz in (0, 1, -1)] + [to_right * side[4], to_left * side[5]]
     for n in range(5):
         third_ref[n] = jnp.where(upper_row, sends[-1][n], sends[1][n])
         fourth_ref[n] = jnp.where(upper_row, sends[1][n], sends[-1][n])
@@ -524,7 +526,7 @@
         "fetch",
         scratch_shapes=[pltpu.SemaphoreType.DMA((CHUNKS,))],
     )(outside(matrices), middle)
-    one, two = call(across_kernel, (tile(7), tile(7)), [VM] * 5, "across")(sides, near, far, first, second)
+    one, two = call(across_kernel, (tile(6), tile(6)), [VM] * 5, "across")(sides, near, far, first, second)
     one, two = both_ways(one, two, "work")
     stay, third, fourth, gain, payload = call(
         first_kernel, (tile(9), tile(5), tile(5), tile(4), payload_shape), [VM] * 9, "first"

time: 82.9 us -> 82.9 us (level)
  no operation moved by 1% of the time
where the time goes in v8:
time: 82.9 us; the launch traced here: 82.5 us
  blocking collectives  47.2 us (57%)
  waiting for transfers between devices  12.6 us (15%)
  Pallas kernels  11.9 us (14%)
  starting transfers between devices  10.7 us (13%)
    all_to_all x3, blocking collectives, exchange(): lax.all_to_all(value, 'work', split_axis=0, concat_axis=0, tiled=True)  47.2 us
    all_to_all x1, waiting for transfers between devices, exchange(): lax.all_to_all(value, 'work', split_axis=0, concat_axis=0, tiled=True)  9.06 us
    ppermute x8, starting transfers between devices, swapped(): return lax.ppermute(value, ('space', 'work'), pairs)  6.19 us
    pallas_call x2, Pallas kernels, owner(): call(lambda *refs: owner_kernel(*refs, fold=fold), jax.ShapeDtypeStruct((...  4.64 us
    all_to_all x1, starting transfers between devices, exchange(): lax.all_to_all(value, 'work', split_axis=0, concat_axis=0, tiled=True)  4.48 us
    ppermute x8, waiting for transfers between devices, swapped(): return lax.ppermute(value, ('space', 'work'), pairs)  3.58 us
    pallas_call x1, Pallas kernels, body(): call(fetch_again_kernel, (pltpu.VMEM(matrices.shape, BF16), tile(10)), [H...  2.21 us
    pallas_call x1, Pallas kernels, body(): call(fetch_kernel, (pltpu.VMEM(matrices.shape, BF16), tile(3)), [HBM, VM]...  2.21 us
  transfers between devices with their start and end apart: 9, of which 4 were waited for; matrix products, arithmetic and copies ran while one was open for 0% of the time, Pallas kernels for 7%

profile of v8, /device:TPU:32, one launch (start us, length us, event | category | flops | bytes accessed | tf_op | source)
XLA Modules:
  0.0 82.5 jit_solution(4667179696911598537)
XLA Ops:
  0.0 1.0 %arrange.1 = (f32[9,8,128]{2,1,0:T(8,128)S(1)}, f32[5,8,128]{2,1,0:T(8,128)S(1)}, f32[5,8,128]{2,1,0:T(8,128)S(1)}, f32[6,8,128]{2,1,0:T(8,128)S(1)}) custom-call(f32[3,19,2,1,128]{4,3,2,1,0:T(1,128)} %field_hbm.1, bf16[3,1,2,128]{3,2,1,0:T(2,128)(2,1)} %bitcast.11, s32[2,1,128]{2,1,0:T(1,128)} %mask_hbm.1, f32[3]{0:T(128)} %relaxation_hbm.1, f32[3]{0:T(128)} %uptake_hbm.1), custom_call_target="tpu_custom_call" | custom-call | tf_op jit(solution)/shard_map/arrange/pallas_call | solution.py:494
  1.0 0.1 collective-permute-start
  1.1 1.9 %collective-permute-start.1 = (f32[5,8,128]{2,1,0:T(8,128)S(1)}, f32[5,8,128]{2,1,0:T(8,128)S(1)}, u32[]{:S(2)}, u32[]{:S(2)}) collective-permute-start(f32[5,8,128]{2,1,0:T(8,128)S(1)} %get-tuple-element.31.far_ref), channel_id=1, source_target_pairs={{0,1},{1,0},{2,3},{3,2},{4,5},{5,4},{6,7},{7,6},{8,9},{9,8},{10,11... | collective-permute-start | bytes 61448 | tf_op jit(solution)/shard_map/ppermute | solution.py:463
  3.0 1.0 %slots.1 = (f32[32,16,128]{2,1,0:T(8,128)S(1)}, f32[6,8,128]{2,1,0:T(8,128)S(1)}) custom-call(s32[1,1,32,4,128]{4,3,2,1,0:T(4,128)} %cells_hbm.1, s32[1,1,32]{2,1,0:T(1,128)} %load_hbm.1, f32[9,8,128]{2,1,0:T(8,128)S(1)} %get-tuple-element.28.middle_ref), custom_call_target="tpu_custom_call" | custom-call | tf_op jit(solution)/shard_map/slots/pallas_call | solution.py:511
  4.0 0.0 collective-permute-done.first_ref
  4.0 0.9 %collective-permute-done.1.second_ref = f32[5,8,128]{2,1,0:T(8,128)S(1)} collective-permute-done((f32[5,8,128]{2,1,0:T(8,128)S(1)}, f32[5,8,128]{2,1,0:T(8,128)S(1)}, u32[]{:S(2)}, u32[]{:S(2)}) %collective-permute-start.1) | collective-permute-done | bytes 20512 | tf_op jit(solution)/shard_map/ppermute | solution.py:463
  4.9 2.0 %collective-permute-start.2 = (f32[6,8,128]{2,1,0:T(8,128)S(1)}, f32[6,8,128]{2,1,0:T(8,128)S(1)}, u32[]{:S(2)}, u32[]{:S(2)}) collective-permute-start(f32[6,8,128]{2,1,0:T(8,128)S(1)} %get-tuple-element.33), channel_id=1, source_target_pairs={{0,32},{1,2},{2,1},{3,4},{4,3},{5,6},{6,5},{7,8},{8,7},{9,10},{10,... | collective-permute-start | bytes 73736 | tf_op jit(solution)/shard_map/ppermute | solution.py:463
  7.0 0.1 collective-permute-start.3
  7.0 2.2 %fetch.1 = (bf16[32,4,128,128]{3,2,1,0:T(8,128)(2,1)S(1)}, f32[3,8,128]{2,1,0:T(8,128)S(1)}) custom-call(bf16[32,4,128,128]{3,2,1,0:T(8,128)(2,1)} %bitcast.9, f32[9,8,128]{2,1,0:T(8,128)S(1)} %get-tuple-element.28.middle_ref), custom_call_target="tpu_custom_call" | custom-call | tf_op jit(solution)/shard_map/fetch/pallas_call | solution.py:522
  9.2 0.0 collective-permute-done.2.one_ref
  9.3 1.5 %collective-permute-done.3.two_ref = f32[6,8,128]{2,1,0:T(8,128)S(1)} collective-permute-done((f32[6,8,128]{2,1,0:T(8,128)S(1)}, f32[6,8,128]{2,1,0:T(8,128)S(1)}, u32[]{:S(2)}, u32[]{:S(2)}) %collective-permute-start.3) | collective-permute-done | bytes 24608 | tf_op jit(solution)/shard_map/ppermute | solution.py:463
  10.8 0.1 first.1
  10.9 20.1 %all_to_all.20.refs_0_.incoming_ref = bf16[32,16,128]{2,1,0:T(8,128)(2,1)S(1)} all-to-all(bf16[32,16,128]{2,1,0:T(8,128)(2,1)S(1)} %get-tuple-element.37.refs_1_), channel_id=1, replica_groups=mesh['space'=8,'work'=32] {'work'}, dimensions={0} | all-to-all | bytes 262144 | tf_op jit(solution)/shard_map/all_to_all | solution.py:491
  31.0 2.7 %owner_fold.1 = bf16[768,128]{1,0:T(8,128)(2,1)} custom-call(bf16[32,16,128]{2,1,0:T(8,128)(2,1)S(1)} %all_to_all.20.refs_0_.incoming_ref, bf16[32,16,128]{2,1,0:T(8,128)(2,1)S(1)} %get-tuple-element.37.refs_1_, bf16[32,4,128,128]{3,2,1,0:T(8,128)(2,1)S(1)} %get-tuple-element.42.refs_2_), custom_call_target="tpu_custom_call" | custom-call | tf_op jit(solution)/shard_map/owner_fold/pallas_call | solution.py:478
  33.7 4.5 %all-to-all-start.1 = ((bf16[32,24,128]{2,1,0:T(8,128)(2,1)}), bf16[32,24,128]{2,1,0:T(8,128)(2,1)S(1)}, u32[]{:S(2)}, u32[]{:S(2)}) async-start(bf16[32,24,128]{2,1,0:T(8,128)(2,1)} %bitcast.2), calls=%async_computation.1 | async-start | bytes 393216 | tf_op jit(solution)/shard_map/all_to_all | solution.py:491
  38.2 1.6 %collective-permute-start.4 = (f32[5,8,128]{2,1,0:T(8,128)S(1)}, f32[5,8,128]{2,1,0:T(8,128)S(1)}, u32[]{:S(2)}, u32[]{:S(2)}) collective-permute-start(f32[5,8,128]{2,1,0:T(8,128)S(1)} %get-tuple-element.39), channel_id=1, source_target_pairs={{0,32},{1,2},{2,1},{3,4},{4,3},{5,6},{6,5},{7,8},{8,7},{9,10},{10,... | collective-permute-start | bytes 61448 | tf_op jit(solution)/shard_map/ppermute | solution.py:463
  39.8 0.0 collective-permute-start.5
  39.8 9.1 %all-to-all-done.1 = bf16[32,24,128]{2,1,0:T(8,128)(2,1)S(1)} async-done(((bf16[32,24,128]{2,1,0:T(8,128)(2,1)}), bf16[32,24,128]{2,1,0:T(8,128)(2,1)S(1)}, u32[]{:S(2)}, u32[]{:S(2)}) %all-to-all-start.1) | async-done | bytes 196640 | tf_op jit(solution)/shard_map/all_to_all | solution.py:491
  48.9 0.1 collective-permute-start.6
  49.0 0.4 collective-permute-start.7
  49.4 0.0 collective-permute-done.4.third_ref
  49.4 0.0 collective-permute-done.5.fourth_ref
  49.4 2.2 %fetch_again.1 = (bf16[32,4,128,128]{3,2,1,0:T(8,128)(2,1)S(1)}, f32[10,8,128]{2,1,0:T(8,128)S(1)}) custom-call(bf16[32,4,128,128]{3,2,1,0:T(8,128)(2,1)} %bitcast.10, f32[5,8,128]{2,1,0:T(8,128)S(1)} %collective-permute-done.4.third_ref, f32[5,8,128]{2,1,0:T(8,128)S(1)} %collective-permute-done.5.fourth_ref), custom_call_target="tpu_custom_call" | custom-call | tf_op jit(solution)/shard_map/fetch_again/pallas_call | solution.py:542
  51.6 0.0 collective-permute-done.6.first_ref
  51.6 1.1 %collective-permute-done.7.second_ref = f32[3,8,128]{2,1,0:T(8,128)S(1)} collective-permute-done((f32[3,8,128]{2,1,0:T(8,128)S(1)}, f32[3,8,128]{2,1,0:T(8,128)S(1)}, u32[]{:S(2)}, u32[]{:S(2)}) %collective-permute-start.7) | collective-permute-done | bytes 12320 | tf_op jit(solution)/shard_map/ppermute | solution.py:463
  52.8 0.1 second.1
  52.9 13.3 %all_to_all.21 = bf16[32,8,128]{2,1,0:T(8,128)(2,1)S(1)} all-to-all(bf16[32,8,128]{2,1,0:T(8,128)(2,1)S(1)} %bitcast.8), channel_id=1, replica_groups=mesh['space'=8,'work'=32] {'work'}, dimensions={0} | all-to-all | bytes 131072 | tf_op jit(solution)/shard_map/all_to_all | solution.py:491
  66.2 1.9 %owner.1 = bf16[32,16,128]{2,1,0:T(8,128)(2,1)S(1)} custom-call(bf16[32,16,128]{2,1,0:T(8,128)(2,1)S(1)} %all_to_all.20.refs_0_.incoming_ref, bf16[256,128]{1,0:T(8,128)(2,1)S(1)} %bitcast.7, bf16[32,4,128,128]{3,2,1,0:T(8,128)(2,1)S(1)} %get-tuple-element.48.refs_2_), custom_call_target="tpu_custom_call" | custom-call | tf_op jit(solution)/shard_map/owner/pallas_call | solution.py:478
  68.1 13.7 %all_to_all.22.returned_ref = bf16[32,16,128]{2,1,0:T(8,128)(2,1)S(1)} all-to-all(bf16[32,16,128]{2,1,0:T(8,128)(2,1)S(1)} %owner.1), channel_id=1, replica_groups=mesh['space'=8,'work'=32] {'work'}, dimensions={0} | all-to-all | bytes 262144 | tf_op jit(solution)/shard_map/all_to_all | solution.py:491
  81.8 0.7 last.1
  (2 shorter events, 0.1 us)
Async XLA Ops:
  1.0 3.0 %collective-permute-start = (f32[5,8,128]{2,1,0:T(8,128)S(1)}, f32[5,8,128]{2,1,0:T(8,128)S(1)}, u32[]{:S(2)}, u32[]{:S(2)}) collective-permute-start(f32[5,8,128]{2,1,0:T(8,128)S(1)} %get-tuple-element.30.near_ref), channel_id=1, source_target_pairs={{0,32},{1,33},{2,34},{3,35},{4,36},{5,37},{6,38},{7,39},{8,40},{9,... | collective-permute-start | bytes 61448 | tf_op jit(solution)/shard_map/ppermute | solution.py:463
  1.1 3.9 %collective-permute-start.1 = (f32[5,8,128]{2,1,0:T(8,128)S(1)}, f32[5,8,128]{2,1,0:T(8,128)S(1)}, u32[]{:S(2)}, u32[]{:S(2)}) collective-permute-start(f32[5,8,128]{2,1,0:T(8,128)S(1)} %get-tuple-element.31.far_ref), channel_id=1, source_target_pairs={{0,1},{1,0},{2,3},{3,2},{4,5},{5,4},{6,7},{7,6},{8,9},{9,8},{10,11... | collective-permute-start | bytes 61448 | tf_op jit(solution)/shard_map/ppermute | solution.py:463
  4.9 4.3 %collective-permute-start.2 = (f32[6,8,128]{2,1,0:T(8,128)S(1)}, f32[6,8,128]{2,1,0:T(8,128)S(1)}, u32[]{:S(2)}, u32[]{:S(2)}) collective-permute-start(f32[6,8,128]{2,1,0:T(8,128)S(1)} %get-tuple-element.33), channel_id=1, source_target_pairs={{0,32},{1,2},{2,1},{3,4},{4,3},{5,6},{6,5},{7,8},{8,7},{9,10},{10,... | collective-permute-start | bytes 73736 | tf_op jit(solution)/shard_map/ppermute | solution.py:463
  7.0 3.8 %collective-permute-start.3 = (f32[6,8,128]{2,1,0:T(8,128)S(1)}, f32[6,8,128]{2,1,0:T(8,128)S(1)}, u32[]{:S(2)}, u32[]{:S(2)}) collective-permute-start(f32[6,8,128]{2,1,0:T(8,128)S(1)} %get-tuple-element.34), channel_id=1, source_target_pairs={{0,1},{1,0},{2,3},{3,2},{4,5},{5,4},{6,7},{7,6},{8,9},{9,8},{10,11... | collective-permute-start | bytes 73736 | tf_op jit(solution)/shard_map/ppermute | solution.py:463
  33.7 15.1 %all-to-all-start.1 = ((bf16[32,24,128]{2,1,0:T(8,128)(2,1)}), bf16[32,24,128]{2,1,0:T(8,128)(2,1)S(1)}, u32[]{:S(2)}, u32[]{:S(2)}) async-start(bf16[32,24,128]{2,1,0:T(8,128)(2,1)} %bitcast.2), calls=%async_computation.1 | async-start | bytes 393216 | tf_op jit(solution)/shard_map/all_to_all | solution.py:491
  38.2 11.2 %collective-permute-start.4 = (f32[5,8,128]{2,1,0:T(8,128)S(1)}, f32[5,8,128]{2,1,0:T(8,128)S(1)}, u32[]{:S(2)}, u32[]{:S(2)}) collective-permute-start(f32[5,8,128]{2,1,0:T(8,128)S(1)} %get-tuple-element.39), channel_id=1, source_target_pairs={{0,32},{1,2},{2,1},{3,4},{4,3},{5,6},{6,5},{7,8},{8,7},{9,10},{10,... | collective-permute-start | bytes 61448 | tf_op jit(solution)/shard_map/ppermute | solution.py:463
  39.8 9.7 %collective-permute-start.5 = (f32[5,8,128]{2,1,0:T(8,128)S(1)}, f32[5,8,128]{2,1,0:T(8,128)S(1)}, u32[]{:S(2)}, u32[]{:S(2)}) collective-permute-start(f32[5,8,128]{2,1,0:T(8,128)S(1)} %get-tuple-element.40), channel_id=1, source_target_pairs={{0,1},{1,0},{2,3},{3,2},{4,5},{5,4},{6,7},{7,6},{8,9},{9,8},{10,11... | collective-permute-start | bytes 61448 | tf_op jit(solution)/shard_map/ppermute | solution.py:463
  48.9 2.8 %collective-permute-start.6 = (f32[3,8,128]{2,1,0:T(8,128)S(1)}, f32[3,8,128]{2,1,0:T(8,128)S(1)}, u32[]{:S(2)}, u32[]{:S(2)}) collective-permute-start(f32[3,8,128]{2,1,0:T(8,128)S(1)} %get-tuple-element.45), channel_id=1, source_target_pairs={{0,32},{1,33},{2,34},{3,35},{4,36},{5,37},{6,38},{7,39},{8,40},{9,... | collective-permute-start | bytes 36872 | tf_op jit(solution)/shard_map/ppermute | solution.py:463
  49.0 3.8 %collective-permute-start.7 = (f32[3,8,128]{2,1,0:T(8,128)S(1)}, f32[3,8,128]{2,1,0:T(8,128)S(1)}, u32[]{:S(2)}, u32[]{:S(2)}) collective-permute-start(f32[3,8,128]{2,1,0:T(8,128)S(1)} %get-tuple-element.46), channel_id=1, source_target_pairs={{0,1},{1,0},{2,3},{3,2},{4,5},{5,4},{6,7},{7,6},{8,9},{9,8},{10,11... | collective-permute-start | bytes 36872 | tf_op jit(solution)/shard_map/ppermute | solution.py:463
